TPU v7x, 32 devices: a whole 2x2x4 slice. The times are simulated.
32 devices in a mesh: seq: 4 (over y, x), shard: 8 (over z, core).
Axes of the slice: x: 2, y: 2, z: 4, core: 2. Of those that a mesh axis runs over, the one named last changes fastest.
Arguments:
- block_input: bfloat16 [16, 1024, 768], P('shard', 'seq'), may hold values from -6 to 6
- gain_attn: float32 [768], replicated, may hold values from 0.25 to 1.75
- gain_ffn: float32 [768], replicated, may hold values from 0.25 to 1.75
- w_qkv: bfloat16 [768, 2304], P('shard'), may hold values from -0.09375 to 0.09375
- w_out: bfloat16 [768, 768], P('shard'), may hold values from -4 to 4
- w_router: bfloat16 [768, 16], P('shard'), may hold values from -0.109375 to 0.109375
- rel_bias: float32 [32, 12], replicated, may hold values from -4 to 4
- w_in: bfloat16 [16, 768, 3072], P('shard'), may hold values from -0.21875 to 0.21875
- w_exp_out: bfloat16 [16, 3072, 768], P('shard'), may hold values from -6 to 6
- expert_id: int32 [16, 1024], P('shard', 'seq'), may hold values from 0 to 15, as said below
- capacity_slot: int32 [16, 1024], P('shard', 'seq'), may hold values from 0 to 64, as said below
- buckets: int32 [2047], replicated, may hold values from 0 to 31
- output_grad: bfloat16 [16, 1024, 768], P('shard', 'seq'), may hold values from -6 to 6
Outputs:
- block_output: bfloat16 [16, 1024, 768], P('shard', 'seq')
- input_grad: float32 [16, 1024, 768], P('shard', 'seq')
- grad_gain_attn: float32 [768], replicated
- grad_gain_ffn: float32 [768], replicated
- grad_w_qkv: float32 [768, 2304], P('shard')
- grad_w_out: float32 [768, 768], P('shard')
- grad_w_router: float32 [768, 16], P('shard')
- grad_rel_bias: float32 [32, 12], replicated
- grad_w_in: float32 [16, 768, 3072], P('shard', None, 'seq')
- grad_w_exp_out: float32 [16, 3072, 768], P('shard', 'seq')
Inputs may be any that keep to these rules, and one draw needn't show every extreme that they name: `expert_id`: among the 512 tokens of one device (one shard index, one seq index), each expert is named by at most 64 kept tokens, with distinct slots. Slot 64 marks a dropped token; an expert with a dropped token has all 64 slots of that device taken. Some experts have all 64 slots taken on every device. `capacity_slot`: the slot of a token in its expert's buffer for its device's tokens; 64 means dropped.
All inputs are finite; a program needn't handle non-finite values.
Results may differ from a plain program's by a relative error of at most 0.019.
Values may be sent and summed in bfloat16 or wider, within the bound.
No kernel may reach another device: no remote copies, remote signals or barrier semaphores. Data moves between devices by JAX's collectives and lax.ppermute only.
A program may use at most 192 MiB of HBM per device.

v0:
```python
import math

import jax
import jax.numpy as jnp
from jax import lax
from jax.sharding import PartitionSpec as P

norm_eps = 1e-06
exact_matmul_mode = lax.Precision.HIGHEST


def rms_forward(values, gain_vec):
    inverse = lax.rsqrt(jnp.mean(values * values, axis=-1, keepdims=True) + norm_eps)
    return (values * inverse * gain_vec, inverse)


def rms_backward(values, inverse, gain_vec, upstream):
    scaled = upstream * gain_vec
    gain_grad = jnp.sum(upstream * values * inverse, axis=(0, 1))
    inner_mean = jnp.mean(scaled * values, axis=-1, keepdims=True)
    return (inverse * scaled - values * inverse * inverse * inverse * inner_mean, gain_grad)


def gelu_derivative(values):
    cumulative = 0.5 * (1.0 + lax.erf(values * (1.0 / math.sqrt(2.0))))
    density = jnp.exp(-0.5 * values * values) * (1.0 / math.sqrt(2.0 * math.pi))
    return cumulative + values * density


def bias_rows(offset_bias, row_start, block_rows, length):
    heads_dev = offset_bias.shape[0]
    span_len = length + block_rows - 1
    window = lax.dynamic_slice_in_dim(offset_bias, length - block_rows - row_start, span_len, 1)
    tiled_rows = jnp.tile(window, (1, block_rows + 1))[:, : block_rows * (length + block_rows)]
    return tiled_rows.reshape(heads_dev, block_rows, length + block_rows)[:, ::-1, :length]


def bias_grad_rows(score_sum, block_rows, length):
    heads_dev = score_sum.shape[0]
    flipped = score_sum[:, ::-1, :]
    padded = jnp.concatenate(
        [flipped, jnp.zeros((heads_dev, block_rows, block_rows), jnp.float32)], axis=2
    )
    sheared = padded.reshape(heads_dev, block_rows * (length + block_rows))[
        :, : block_rows * (length + block_rows - 1)
    ]
    sheared = sheared.reshape(heads_dev, block_rows, length + block_rows - 1)
    return jnp.sum(sheared, axis=1)


def body(
    block_input,
    gain_attn,
    gain_ffn,
    w_qkv,
    w_out,
    w_router,
    rel_bias,
    w_in,
    w_exp_out,
    expert_id,
    capacity_slot,
    buckets,
    output_grad,
):
    seq_count, tok_piece, model_width = block_input.shape
    seq_ways = lax.axis_size("seq")
    length = tok_piece * seq_ways
    heads_all = rel_bias.shape[1]
    heads_dev = heads_all // seq_ways
    head_dim = model_width // heads_all
    bucket_count = rel_bias.shape[0]
    experts = w_router.shape[1]
    token_count = seq_count * tok_piece
    capacity = 2 * token_count // experts
    positions = experts * capacity
    block_rows = min(512, length)
    block_count = length // block_rows
    span_len = length + block_rows - 1
    query_key_value_weight, output_projection, routing_weight = (
        lax.all_gather(w_qkv, "shard", axis=0, tiled=True),
        lax.all_gather(w_out, "shard", axis=0, tiled=True),
        lax.all_gather(w_router, "shard", axis=0, tiled=True),
    )
    inputs = block_input.astype(jnp.float32)
    normalized_input, inverse_one = rms_forward(inputs, gain_attn)
    normed_low = normalized_input.astype(jnp.bfloat16)
    qkv_local = jnp.einsum(
        "std,de->ste", normed_low, query_key_value_weight, preferred_element_type=jnp.float32
    )
    qkv_local = qkv_local.astype(jnp.bfloat16).reshape(seq_count, tok_piece, 3, model_width)
    qkv_heads = lax.all_to_all(qkv_local, "seq", split_axis=3, concat_axis=1, tiled=True)
    qkv_heads = qkv_heads.reshape(seq_count, length, 3, heads_dev, head_dim)
    queries = qkv_heads[:, :, 0]
    keys_all = qkv_heads[:, :, 1]
    values_all = qkv_heads[:, :, 2]
    head_start = lax.axis_index("seq") * heads_dev
    bias_dev = lax.dynamic_slice_in_dim(rel_bias, head_start, heads_dev, 1)
    bucket_hot = (buckets[None, :] == jnp.arange(bucket_count, dtype=jnp.int32)[:, None]).astype(
        jnp.float32
    )
    offset_bias = jnp.dot(
        bias_dev.T, bucket_hot, precision=exact_matmul_mode, preferred_element_type=jnp.float32
    )

    def scores_for(row_start):
        block_query = lax.dynamic_slice_in_dim(queries, row_start, block_rows, 1)
        scores = jnp.einsum(
            "sqhd,skhd->shqk", block_query, keys_all, preferred_element_type=jnp.float32
        )
        return (block_query, scores + bias_rows(offset_bias, row_start, block_rows, length)[None])

    def forward_block(block_index):
        row_start = block_index * block_rows
        block_query, scores = scores_for(row_start)
        row_peak = jnp.max(scores, axis=-1, keepdims=True)
        exp_scores = jnp.exp(scores - row_peak)
        row_total = jnp.sum(exp_scores, axis=-1, keepdims=True)
        prob_rows = (exp_scores / row_total).astype(jnp.bfloat16)
        block_out = jnp.einsum(
            "shqk,skhd->sqhd", prob_rows, values_all, preferred_element_type=jnp.float32
        )
        return (block_out.astype(jnp.bfloat16), (row_peak + jnp.log(row_total))[..., 0])

    block_outs, block_logs = lax.map(forward_block, jnp.arange(block_count, dtype=jnp.int32))
    attention_result = jnp.transpose(block_outs, (1, 0, 2, 3, 4)).reshape(
        seq_count, length, heads_dev * head_dim
    )
    log_total = jnp.transpose(block_logs, (1, 2, 0, 3)).reshape(seq_count, heads_dev, length)
    attended_tok = lax.all_to_all(attention_result, "seq", split_axis=1, concat_axis=2, tiled=True)
    residual_branch = jnp.einsum(
        "std,de->ste", attended_tok, output_projection, preferred_element_type=jnp.float32
    )
    middle = inputs + residual_branch
    second_residual, inverse_two = rms_forward(middle, gain_ffn)
    second_low = second_residual.astype(jnp.bfloat16)
    router_logits = jnp.einsum(
        "std,de->ste", second_low, routing_weight, preferred_element_type=jnp.float32
    )
    logit_peak = jnp.max(router_logits, axis=-1, keepdims=True)
    exp_logits = jnp.exp(router_logits - logit_peak)
    router_probs = exp_logits / jnp.sum(exp_logits, axis=-1, keepdims=True)
    chosen = (expert_id[..., None] == jnp.arange(experts, dtype=jnp.int32)).astype(jnp.float32)
    gate_prob = jnp.sum(router_probs * chosen, axis=-1)
    target = jnp.where(capacity_slot < capacity, expert_id * capacity + capacity_slot, -1).reshape(
        token_count
    )
    dispatch_hot = (jnp.arange(positions, dtype=jnp.int32)[:, None] == target[None, :]).astype(
        jnp.bfloat16
    )
    send_rows = jnp.dot(
        dispatch_hot,
        second_low.reshape(token_count, model_width),
        preferred_element_type=jnp.float32,
    )
    send_rows = send_rows.astype(jnp.bfloat16).reshape(experts, capacity, model_width)
    arrived = lax.all_to_all(send_rows, "shard", split_axis=0, concat_axis=1, tiled=True)
    pre_act = jnp.einsum("erd,edf->erf", arrived, w_in, preferred_element_type=jnp.float32)
    hidden = jax.nn.gelu(pre_act, approximate=False).astype(jnp.bfloat16)
    expert_out = jnp.einsum(
        "erf,efd->erd", hidden, w_exp_out, preferred_element_type=jnp.float32
    ).astype(jnp.bfloat16)
    returned = lax.all_to_all(expert_out, "shard", split_axis=1, concat_axis=0, tiled=True)
    token_out = jnp.einsum(
        "pt,pd->td",
        dispatch_hot,
        returned.reshape(positions, model_width),
        preferred_element_type=jnp.float32,
    )
    token_out = token_out.reshape(seq_count, tok_piece, model_width)
    block_output = (middle + gate_prob[..., None] * token_out).astype(jnp.bfloat16)
    upstream = output_grad.astype(jnp.float32)
    gate_grad = jnp.sum(upstream * token_out, axis=-1)
    out_grad = (
        (gate_prob[..., None] * upstream).astype(jnp.bfloat16).reshape(token_count, model_width)
    )
    out_rows = jnp.dot(dispatch_hot, out_grad, preferred_element_type=jnp.float32)
    out_rows = out_rows.astype(jnp.bfloat16).reshape(experts, capacity, model_width)
    out_arrived = lax.all_to_all(out_rows, "shard", split_axis=0, concat_axis=1, tiled=True)
    hidden_grad = jnp.einsum(
        "erd,efd->erf", out_arrived, w_exp_out, preferred_element_type=jnp.float32
    )
    pre_grad = (hidden_grad * gelu_derivative(pre_act)).astype(jnp.bfloat16)
    rows_grad = jnp.einsum(
        "erf,edf->erd", pre_grad, w_in, preferred_element_type=jnp.float32
    ).astype(jnp.bfloat16)
    rows_back = lax.all_to_all(rows_grad, "shard", split_axis=1, concat_axis=0, tiled=True)
    second_grad = jnp.einsum(
        "pt,pd->td",
        dispatch_hot,
        rows_back.reshape(positions, model_width),
        preferred_element_type=jnp.float32,
    )
    second_grad = second_grad.reshape(seq_count, tok_piece, model_width)
    prob_pick = chosen * gate_grad[..., None]
    logit_grad = router_probs * (
        prob_pick - jnp.sum(router_probs * prob_pick, axis=-1, keepdims=True)
    )
    logit_low = logit_grad.astype(jnp.bfloat16)
    grad_router = jnp.einsum(
        "std,ste->de", second_low, logit_low, preferred_element_type=jnp.float32
    )
    second_grad = second_grad + jnp.einsum(
        "ste,de->std", logit_low, routing_weight, preferred_element_type=jnp.float32
    )
    middle_norm_grad, grad_gain_two = rms_backward(middle, inverse_two, gain_ffn, second_grad)
    middle_grad = upstream + middle_norm_grad
    branch_low = middle_grad.astype(jnp.bfloat16)
    grad_out = jnp.einsum(
        "std,ste->de", attended_tok, branch_low, preferred_element_type=jnp.float32
    )
    attended_grad = jnp.einsum(
        "ste,de->std", branch_low, output_projection, preferred_element_type=jnp.float32
    ).astype(jnp.bfloat16)
    attended_grad_heads = lax.all_to_all(
        attended_grad, "seq", split_axis=2, concat_axis=1, tiled=True
    )
    attended_grad_heads = attended_grad_heads.reshape(seq_count, length, heads_dev, head_dim)

    def backward_block(carried, block_index):
        key_grad, value_grad, offset_grad = carried
        row_start = block_index * block_rows
        block_query, scores = scores_for(row_start)
        block_log = lax.dynamic_slice_in_dim(log_total, row_start, block_rows, 2)
        prob_rows = jnp.exp(scores - block_log[..., None])
        probs_low = prob_rows.astype(jnp.bfloat16)
        block_grad = lax.dynamic_slice_in_dim(attended_grad_heads, row_start, block_rows, 1)
        prob_grad = jnp.einsum(
            "sqhd,skhd->shqk", block_grad, values_all, preferred_element_type=jnp.float32
        )
        row_dot = jnp.sum(prob_rows * prob_grad, axis=-1, keepdims=True)
        score_grad = (prob_rows * (prob_grad - row_dot)).astype(jnp.bfloat16)
        query_grad = jnp.einsum(
            "shqk,skhd->sqhd", score_grad, keys_all, preferred_element_type=jnp.float32
        )
        key_grad = key_grad + jnp.einsum(
            "shqk,sqhd->skhd", score_grad, block_query, preferred_element_type=jnp.float32
        )
        value_grad = value_grad + jnp.einsum(
            "shqk,sqhd->skhd", probs_low, block_grad, preferred_element_type=jnp.float32
        )
        score_sum = jnp.sum(score_grad, axis=0, dtype=jnp.float32)
        sheared = bias_grad_rows(score_sum, block_rows, length)
        where_at = length - block_rows - row_start
        current = lax.dynamic_slice_in_dim(offset_grad, where_at, span_len, 1)
        offset_grad = lax.dynamic_update_slice_in_dim(offset_grad, current + sheared, where_at, 1)
        return ((key_grad, value_grad, offset_grad), query_grad.astype(jnp.bfloat16))

    zero_keys = jnp.zeros((seq_count, length, heads_dev, head_dim), jnp.float32)
    zero_offsets = jnp.zeros((heads_dev, 2 * length - 1), jnp.float32)
    finished, query_blocks = lax.scan(
        backward_block,
        (zero_keys, zero_keys, zero_offsets),
        jnp.arange(block_count, dtype=jnp.int32),
    )
    key_grad, value_grad, offset_grad = finished
    query_grad = jnp.transpose(query_blocks, (1, 0, 2, 3, 4)).reshape(
        seq_count, length, heads_dev, head_dim
    )
    qkv_grad = jnp.stack(
        [query_grad, key_grad.astype(jnp.bfloat16), value_grad.astype(jnp.bfloat16)], axis=2
    )
    qkv_grad = qkv_grad.reshape(seq_count, length, 3, heads_dev * head_dim)
    qkv_grad_tok = lax.all_to_all(qkv_grad, "seq", split_axis=1, concat_axis=3, tiled=True).reshape(
        seq_count, tok_piece, 3 * model_width
    )
    grad_qkv = jnp.einsum(
        "std,ste->de", normed_low, qkv_grad_tok, preferred_element_type=jnp.float32
    )
    normed_grad = jnp.einsum(
        "ste,de->std", qkv_grad_tok, query_key_value_weight, preferred_element_type=jnp.float32
    )
    input_norm_grad, grad_gain_one = rms_backward(inputs, inverse_one, gain_attn, normed_grad)
    input_grad = middle_grad + input_norm_grad
    bias_grad_dev = jnp.dot(
        bucket_hot, offset_grad.T, precision=exact_matmul_mode, preferred_element_type=jnp.float32
    )
    bias_grad = lax.dynamic_update_slice_in_dim(
        jnp.zeros((bucket_count, heads_all), jnp.float32), bias_grad_dev, head_start, 1
    )
    bias_grad, grad_gain_one, grad_gain_two = lax.psum(
        (bias_grad, grad_gain_one, grad_gain_two), ("seq", "shard")
    )
    summed_qkv, summed_out, summed_router = (
        lax.psum(grad_qkv.astype(jnp.bfloat16), "seq").astype(jnp.float32),
        lax.psum(grad_out.astype(jnp.bfloat16), "seq").astype(jnp.float32),
        lax.psum(grad_router.astype(jnp.bfloat16), "seq").astype(jnp.float32),
    )
    grad_qkv, grad_out, grad_router = (
        lax.psum_scatter(summed_qkv, "shard", scatter_dimension=0, tiled=True),
        lax.psum_scatter(summed_out, "shard", scatter_dimension=0, tiled=True),
        lax.psum_scatter(summed_router, "shard", scatter_dimension=0, tiled=True),
    )
    grad_exp_out = jnp.einsum(
        "erf,erd->efd", hidden, out_arrived, preferred_element_type=jnp.float32
    )
    grad_in = jnp.einsum("erd,erf->edf", arrived, pre_grad, preferred_element_type=jnp.float32)
    grad_in_part, grad_exp_part = (
        lax.psum_scatter(
            grad_in.astype(jnp.bfloat16), "seq", scatter_dimension=2, tiled=True
        ).astype(jnp.float32),
        lax.psum_scatter(
            grad_exp_out.astype(jnp.bfloat16), "seq", scatter_dimension=1, tiled=True
        ).astype(jnp.float32),
    )
    return (
        block_output,
        input_grad,
        grad_gain_one,
        grad_gain_two,
        grad_qkv,
        grad_out,
        grad_router,
        bias_grad,
        grad_in_part,
        grad_exp_part,
    )


def solution(mesh):
    placed = (
        P("shard", "seq", None),
        P(),
        P(),
        P("shard", None),
        P("shard", None),
        P("shard", None),
        P(),
        P("shard", None, None),
        P("shard", None, None),
        P("shard", "seq"),
        P("shard", "seq"),
        P(),
        P("shard", "seq", None),
    )
    return jax.shard_map(
        body,
        mesh=mesh,
        in_specs=placed,
        out_specs=(
            P("shard", "seq", None),
            P("shard", "seq", None),
            P(),
            P(),
            P("shard", None),
            P("shard", None),
            P("shard", None),
            P(),
            P("shard", None, "seq"),
            P("shard", "seq", None),
        ),
        check_vma=False,
    )
```

profile of v0, /device:TPU:0, one launch (start us, length us, event | category | flops | bytes accessed | tf_op | source)
XLA Modules:
  0.0 1719.4 jit_solution(4209805546289038000)
XLA Ops:
  9.3 44.6 %all-gather.4.cloned.1.call-done = bf16[768,2304]{1,0:T(8,128)(2,1)} async-done(((bf16[96,2304]{1,0:T(8,128)(2,1)}), bf16[768,2304]{1,0:T(8,128)(2,1)}) %all-gather.4.cloned.1.call-update) | async-done | bytes 3538960 | tf_op jit(solution)/shard_map/all_gather | solution.py:81
  71.0 27.3 %all-to-all-done = bf16[2,256,3,768]{1,0,2,3:T(2,128)(2,1)S(1)} async-done(((bf16[2,256,3,768]{1,0,2,3:T(2,128)(2,1)}), bf16[2,256,3,768]{1,0,2,3:T(2,128)(2,1)S(1)}, u32[]{:S(2)}, u32[]{:S(2)}) %all-to-all-start) | async-done | bytes 2359328 | tf_op jit(solution)/shard_map/all_to_all | solution.py:92
  108.7 229.3 %while.33 = (s32[]{:T(128)}, bf16[2,2,512,3,64]{2,4,3,1,0:T(8,128)(2,1)}, f32[2,2,3,512]{3,2,1,0:T(4,128)S(1)}, s32[2]{0:T(128)S(1)}, bf16[2,1024,3,64]{1,3,2,0:...) while((s32[]{:T(128)}, ...), condition=%wide.region_4.5_spmd, body=%wide.region_1.4_spmd.sunk | while | flops 833811456 | bytes 225941856 | solution.py:125
  115.1 15.2 reshape.253
  161.7 48.5 %rev.23 = f32[3,512,1024]{2,1,0:T(8,128)} reverse(f32[3,512,1024]{2,1,0:T(8,128)} %slice.62), dimensions={1} | reverse | bytes 12582912 | tf_op jit(solution)/shard_map/while/body/eval_jaxpr/rev | solution.py:35
  276.0 48.5 %rev.23 = f32[3,512,1024]{2,1,0:T(8,128)} reverse(f32[3,512,1024]{2,1,0:T(8,128)} %slice.62), dimensions={1} | reverse | bytes 12582912 | tf_op jit(solution)/shard_map/while/body/eval_jaxpr/rev | solution.py:35
  365.5 40.6 %all_to_all.129 = bf16[16,64,768]{2,1,0:T(8,128)(2,1)S(1)} all-to-all(bf16[16,64,768]{2,1,0:T(8,128)(2,1)S(1)} %bitcast.226), channel_id=1, replica_groups=mesh['seq'=4,'shard'=8] {'shard'}, dimensions={0} | all-to-all | bytes 3145728 | tf_op jit(solution)/shard_map/all_to_all | solution.py:157
  406.2 16.5 fusion.47
  422.7 29.9 %fusion.30 = bf16[2,512,3072]{2,1,0:T(8,128)(2,1)S(1)} fusion(f32[2,512,3072]{2,1,0:T(8,128)} %get-tuple-element.435, u8[512,3072]{1,0:T(8,128)(4,1)S(1)} %get-tuple-element.370, u8[512,3072]{1,0:T(8,128)(4,1)S(1)} %get-tuple-element.369), kind=kLoop, calls=%fused_computation.47 | loop fusion | flops 220200960 | bytes 22020096 | tf_op jit(solution)/shard_map/convert_element_type | solution.py:159
  469.9 43.8 %all-gather = bf16[8,96,16]{1,2,0:T(8,128)(2,1)S(1)} all-gather(bf16[1,96,16]{1,2,0:T(8,128)(2,1)S(1)} %bitcast.234), channel_id=1, replica_groups=mesh['seq'=4,'shard'=8] {'shard'}, dimensions={0}, use_global_device_ids=true | all-gather | bytes 27648 | tf_op jit(solution)/shard_map/all_gather | solution.py:83
  521.9 41.5 %all_to_all.130 = bf16[16,64,768]{2,1,0:T(8,128)(2,1)S(1)} all-to-all(bf16[16,64,768]{2,1,0:T(8,128)(2,1)S(1)} %bitcast.224), channel_id=1, replica_groups=mesh['seq'=4,'shard'=8] {'shard'}, dimensions={0} | all-to-all | bytes 3145728 | tf_op jit(solution)/shard_map/all_to_all | solution.py:179
  586.7 40.3 %all_to_all.131 = bf16[2,512,768]{2,0,1:T(2,128)(2,1)S(1)} all-to-all(bf16[2,512,768]{2,0,1:T(2,128)(2,1)S(1)} %copy.151), channel_id=1, replica_groups=mesh['seq'=4,'shard'=8] {'shard'}, dimensions={1} | all-to-all | bytes 3145728 | tf_op jit(solution)/shard_map/all_to_all | solution.py:187
  656.6 524.0 %while.34 = (s32[]{:T(128)}, f32[2,1024,3,64]{1,3,2,0:T(8,128)}, f32[2,1024,3,64]{1,3,2,0:T(8,128)}, f32[3,2047]{1,0:T(4,128)S(1)}, bf16[2,2,512,3,64]{2,4,3,1,0...) while((s32[]{:T(128)}, f32[2,1024,3,64]{1,3,2,0:T(8,128)}, ...), condition=%wide.region_16.17_spmd.clone, body=%wide.region_12.16_spmd.clone.sunk | while | flops 2059857408 | bytes 476463648 | solution.py:251
  710.1 48.6 %rev.24 = f32[3,512,1024]{2,1,0:T(8,128)} reverse(f32[3,512,1024]{2,1,0:T(8,128)} %slice.64), dimensions={1} | reverse | bytes 12582912 | tf_op jit(solution)/shard_map/while/body/eval_jaxpr/rev | solution.py:35
  782.3 15.4 convert_reduce_fusion.2
  797.8 48.5 %rev.25 = f32[3,512,1024]{2,1,0:T(8,128)} reverse(f32[3,512,1024]{2,1,0:T(8,128)} %get-tuple-element.575), dimensions={1} | reverse | bytes 12582912 | tf_op jit(solution)/shard_map/while/body/eval_jaxpr/rev | solution.py:40
  855.0 19.8 %copy.192 = f32[1,3,512,1536]{3,1,2,0:T(4,128)S(1)} copy(f32[1,3,512,1536]{3,2,1,0:T(8,128)S(1)} %pad_bitcast_fusion.2) | data formatting | bytes 18874368 | tf_op jit(solution)/shard_map/while
  893.9 15.6 reshape.256
  967.8 48.6 %rev.24 = f32[3,512,1024]{2,1,0:T(8,128)} reverse(f32[3,512,1024]{2,1,0:T(8,128)} %slice.64), dimensions={1} | reverse | bytes 12582912 | tf_op jit(solution)/shard_map/while/body/eval_jaxpr/rev | solution.py:35
  1040.0 15.4 convert_reduce_fusion.2
  1055.4 48.5 %rev.25 = f32[3,512,1024]{2,1,0:T(8,128)} reverse(f32[3,512,1024]{2,1,0:T(8,128)} %get-tuple-element.575), dimensions={1} | reverse | bytes 12582912 | tf_op jit(solution)/shard_map/while/body/eval_jaxpr/rev | solution.py:40
  1112.6 19.8 %copy.192 = f32[1,3,512,1536]{3,1,2,0:T(4,128)S(1)} copy(f32[1,3,512,1536]{3,2,1,0:T(8,128)S(1)} %pad_bitcast_fusion.2) | data formatting | bytes 18874368 | tf_op jit(solution)/shard_map/while
  1151.8 15.6 reshape.256
  1201.9 33.7 %all-to-all-done.7 = bf16[2,1024,3,192]{3,0,2,1:T(2,128)(2,1)} async-done(((bf16[2,1024,3,192]{3,0,2,1:T(2,128)(2,1)}), bf16[2,1024,3,192]{3,0,2,1:T(2,128)(2,1)}, u32[]{:S(2)}, u32[]{:S(2)}) %all-to-all-start.7) | async-done | bytes 2359328 | tf_op jit(solution)/shard_map/all_to_all | solution.py:264
  1252.5 16.2 psum.46
  1290.1 74.4 %all-reduce.5.cloned.1.call-done = (bf16[768,2304]{1,0:T(8,128)(2,1)}, bf16[768,768]{1,0:T(8,128)(2,1)}) async-done(((bf16[768,2304]{1,0:T(8,128)(2,1)}, bf16[768,768]{1,0:T(8,128)(2,1)}), (bf16[768,2304]{1,0:T(8,128)(2,1)}, bf16[768,768]{1,0:T(8,128)(2,1)})) %all-reduce.5.cloned.1.call-update) | async-done | bytes 4718608 | tf_op jit(solution)/shard_map/psum | solution.py:285
  1373.2 24.1 %reduce-scatter.16.cloned.1.call-done = f32[96,16]{1,0:T(8,128)} async-done(((f32[768,16]{1,0:T(8,128)}), f32[96,16]{1,0:T(8,128)}) %reduce-scatter.16.cloned.1.call-update) | async-done | bytes 6160
  1405.1 38.5 %all-reduce.1 = (f32[768]{0:T(1024)}, f32[768]{0:T(1024)}, f32[32,12]{0,1:T(8,128)}) all-reduce(f32[768]{0:T(1024)S(1)} %get-tuple-element.373, f32[768]{0:T(1024)S(1)} %copy-done.43, f32[32,12]{0,1:T(8,128)S(1)} %dynamic_update_slice.29), channel_id=1, replica_groups=mesh['seq'=4,'shard'=8] {'seq','shard'}, use_global_device_ids=true, to_apply=%region_19.20 | all-reduce | flops 1920 | bytes 15360 | tf_op jit(solution)/shard_map/psum | solution.py:281
  1446.8 48.2 %reduce-scatter.12.cloned.1.call-done = bf16[2,768,768]{2,1,0:T(8,128)(2,1)} async-done(((bf16[2,768,3072]{2,1,0:T(8,128)(2,1)}), bf16[2,768,768]{2,1,0:T(8,128)(2,1)}) %reduce-scatter.12.cloned.1.call-update) | async-done | bytes 2359312 | tf_op jit(solution)/shard_map/reduce_scatter | solution.py:299
  1499.2 94.1 %reduce-scatter.14.cloned.1.call-done = bf16[2,768,768]{2,1,0:T(8,128)(2,1)} async-done(((bf16[2,3072,768]{2,1,0:T(8,128)(2,1)}), bf16[2,768,768]{2,1,0:T(8,128)(2,1)}) %reduce-scatter.14.cloned.1.call-update) | async-done | bytes 2359312 | tf_op jit(solution)/shard_map/reduce_scatter | solution.py:302
  1597.6 35.0 %reduce-scatter.10.cloned.1.call-done = f32[96,768]{1,0:T(8,128)} async-done(((f32[768,768]{1,0:T(8,128)}), f32[96,768]{1,0:T(8,128)}) %reduce-scatter.10.cloned.1.call-update) | async-done | bytes 294928 | tf_op jit(solution)/shard_map/reduce_scatter | solution.py:291
  1632.6 79.5 %reduce-scatter.8.cloned.1.call-done = f32[96,2304]{1,0:T(8,128)} async-done(((f32[768,2304]{1,0:T(8,128)}), f32[96,2304]{1,0:T(8,128)}) %reduce-scatter.8.cloned.1.call-update) | async-done | bytes 884752 | tf_op jit(solution)/shard_map/reduce_scatter | solution.py:290
  (335 shorter events, 554.9 us)
Async XLA Ops:
  7.2 63.6 %copy-start = (f32[32,12]{0,1:T(8,128)S(1)}, f32[32,12]{0,1:T(8,128)}, u32[]{:S(2)}) copy-start(f32[32,12]{0,1:T(8,128)} %param.23) | copy-start | bytes 4612
  7.2 46.7 %all-gather.4.cloned.1.call-start = ((), (), s32[]{:S(2)}) async-start(), calls=%async_computation.13 | async-start | bytes 3981312 | tf_op jit(solution)/shard_map/all_gather | solution.py:81
  66.4 32.0 %all-to-all-start = ((bf16[2,256,3,768]{1,0,2,3:T(2,128)(2,1)}), bf16[2,256,3,768]{1,0,2,3:T(2,128)(2,1)S(1)}, u32[]{:S(2)}, u32[]{:S(2)}) async-start(bf16[2,256,3,768]{1,0,2,3:T(2,128)(2,1)} %copy.138), calls=%async_computation | async-start | bytes 4718592 | tf_op jit(solution)/shard_map/all_to_all | solution.py:92
  70.0 291.5 %all-gather.6.cloned.1.call-start = ((), (), s32[]{:S(2)}) async-start(), calls=%async_computation.14 | async-start | bytes 1327104 | tf_op jit(solution)/shard_map/all_gather | solution.py:82
  161.7 48.5 %copy-start.5 = (bf16[2,1024,3,64]{1,3,2,0:T(8,128)(2,1)S(1)}, bf16[2,1024,3,64]{1,3,2,0:T(8,128)(2,1)}, u32[]{:S(2)}) copy-start(bf16[2,1024,3,64]{1,3,2,0:T(8,128)(2,1)} %get-tuple-element.609) | copy-start | bytes 2359300 | tf_op jit(solution)/shard_map/while
  161.7 48.5 %copy-start.9 = (bf16[2,1024,3,64]{1,3,2,0:T(8,128)(2,1)S(1)}, bf16[2,1024,3,64]{1,3,2,0:T(8,128)(2,1)}, u32[]{:S(2)}) copy-start(bf16[2,1024,3,64]{1,3,2,0:T(8,128)(2,1)} %get-tuple-element.608) | copy-start | bytes 2359300 | tf_op jit(solution)/shard_map/while
  276.0 48.5 %copy-start.5 = (bf16[2,1024,3,64]{1,3,2,0:T(8,128)(2,1)S(1)}, bf16[2,1024,3,64]{1,3,2,0:T(8,128)(2,1)}, u32[]{:S(2)}) copy-start(bf16[2,1024,3,64]{1,3,2,0:T(8,128)(2,1)} %get-tuple-element.609) | copy-start | bytes 2359300 | tf_op jit(solution)/shard_map/while
  276.0 48.5 %copy-start.9 = (bf16[2,1024,3,64]{1,3,2,0:T(8,128)(2,1)S(1)}, bf16[2,1024,3,64]{1,3,2,0:T(8,128)(2,1)}, u32[]{:S(2)}) copy-start(bf16[2,1024,3,64]{1,3,2,0:T(8,128)(2,1)} %get-tuple-element.608) | copy-start | bytes 2359300 | tf_op jit(solution)/shard_map/while
  342.5 16.9 all-to-all-start.1
  364.4 150.5 %copy-start.19 = (bf16[2,256,768]{2,1,0:T(8,128)(2,1)}, bf16[2,256,768]{2,1,0:T(8,128)(2,1)S(1)}, u32[]{:S(2)}) copy-start(bf16[2,256,768]{2,1,0:T(8,128)(2,1)S(1)} %multiply_convert_fusion.1) | copy-start | bytes 2359300
  462.8 54.5 %copy-start.22 = (bf16[2,256,768]{2,1,0:T(8,128)(2,1)S(1)}, bf16[2,256,768]{2,1,0:T(8,128)(2,1)}, u32[]{:S(2)}) copy-start(bf16[2,256,768]{2,1,0:T(8,128)(2,1)} %param.29) | copy-start | bytes 2359300
  465.6 49.8 %all-to-all-start.3 = ((bf16[2,512,768]{2,0,1:T(2,128)(2,1)}), bf16[2,512,768]{2,0,1:T(2,128)(2,1)}, u32[]{:S(2)}, u32[]{:S(2)}) async-start(bf16[2,512,768]{2,0,1:T(2,128)(2,1)} %copy.148), calls=%async_computation.3 | async-start | bytes 3145728 | tf_op jit(solution)/shard_map/all_to_all | solution.py:163
  515.2 114.2 %copy-start.32 = (f32[2,256,16]{1,2,0:T(8,128)}, f32[2,256,16]{1,2,0:T(8,128)S(1)}, u32[]{:S(2)}) copy-start(f32[2,256,16]{1,2,0:T(8,128)S(1)} %fusion.89) | copy-start | bytes 98308
  515.4 114.1 %copy-start.37 = (f32[2,256]{1,0:T(2,128)}, f32[2,256]{1,0:T(2,128)S(1)}, u32[]{:S(2)}) copy-start(f32[2,256]{1,0:T(2,128)S(1)} %get-tuple-element.438) | copy-start | bytes 6148
  515.4 48.1 %slice-start.4 = ((s8[9437184]{0:T(1024)(128)(4,1)}), s8[4194304]{0:T(1024)(128)(4,1)S(1)}, s32[]{:S(2)}) async-start(s8[9437184]{0:T(1024)(128)(4,1)} %bitcast.235), calls=%async_computation.25 | async-start | bytes 8388608
  520.6 108.8 %copy-start.39 = (f32[2,256]{1,0:T(2,128)}, f32[2,256]{1,0:T(2,128)S(1)}, u32[]{:S(2)}) copy-start(f32[2,256]{1,0:T(2,128)S(1)} %get-tuple-element.436) | copy-start | bytes 6148
  520.6 108.8 %copy-start.41 = (f32[2,256]{1,0:T(2,128)}, f32[2,256]{1,0:T(2,128)S(1)}, u32[]{:S(2)}) copy-start(f32[2,256]{1,0:T(2,128)S(1)} %get-tuple-element.375) | copy-start | bytes 6148
  639.3 14.2 all-to-all-start.6
  710.1 48.6 %copy-start.6 = (bf16[2,1024,3,64]{1,3,2,0:T(8,128)(2,1)S(1)}, bf16[2,1024,3,64]{1,3,2,0:T(8,128)(2,1)}, u32[]{:S(2)}) copy-start(bf16[2,1024,3,64]{1,3,2,0:T(8,128)(2,1)} %get-tuple-element.663) | copy-start | bytes 2359300 | tf_op jit(solution)/shard_map/while
  710.1 48.6 %copy-start.10 = (bf16[2,1024,3,64]{1,3,2,0:T(8,128)(2,1)S(1)}, bf16[2,1024,3,64]{1,3,2,0:T(8,128)(2,1)}, u32[]{:S(2)}) copy-start(bf16[2,1024,3,64]{1,3,2,0:T(8,128)(2,1)} %get-tuple-element.662) | copy-start | bytes 2359300 | tf_op jit(solution)/shard_map/while
  797.8 54.3 %copy-start.7 = (f32[2,1024,3,64]{1,3,2,0:T(8,128)S(1)}, f32[2,1024,3,64]{1,3,2,0:T(8,128)}, u32[]{:S(2)}) copy-start(f32[2,1024,3,64]{1,3,2,0:T(8,128)} %get-tuple-element.638) | copy-start | bytes 4718596 | tf_op jit(solution)/shard_map/while
  967.7 48.6 %copy-start.6 = (bf16[2,1024,3,64]{1,3,2,0:T(8,128)(2,1)S(1)}, bf16[2,1024,3,64]{1,3,2,0:T(8,128)(2,1)}, u32[]{:S(2)}) copy-start(bf16[2,1024,3,64]{1,3,2,0:T(8,128)(2,1)} %get-tuple-element.663) | copy-start | bytes 2359300 | tf_op jit(solution)/shard_map/while
  967.8 48.6 %copy-start.10 = (bf16[2,1024,3,64]{1,3,2,0:T(8,128)(2,1)S(1)}, bf16[2,1024,3,64]{1,3,2,0:T(8,128)(2,1)}, u32[]{:S(2)}) copy-start(bf16[2,1024,3,64]{1,3,2,0:T(8,128)(2,1)} %get-tuple-element.662) | copy-start | bytes 2359300 | tf_op jit(solution)/shard_map/while
  1055.4 54.2 %copy-start.7 = (f32[2,1024,3,64]{1,3,2,0:T(8,128)S(1)}, f32[2,1024,3,64]{1,3,2,0:T(8,128)}, u32[]{:S(2)}) copy-start(f32[2,1024,3,64]{1,3,2,0:T(8,128)} %get-tuple-element.638) | copy-start | bytes 4718596 | tf_op jit(solution)/shard_map/while
  1195.2 40.3 %all-to-all-start.7 = ((bf16[2,1024,3,192]{3,0,2,1:T(2,128)(2,1)}), bf16[2,1024,3,192]{3,0,2,1:T(2,128)(2,1)}, u32[]{:S(2)}, u32[]{:S(2)}) async-start(bf16[2,1024,3,192]{3,0,2,1:T(2,128)(2,1)} %copy.159), calls=%async_computation.7 | async-start | bytes 6291456 | tf_op jit(solution)/shard_map/all_to_all | solution.py:264
  1200.0 164.5 %all-reduce.5.cloned.1.call-start = ((), (), s32[]{:S(2)}) async-start(), calls=%async_computation.20 | async-start | bytes 9437184 | tf_op jit(solution)/shard_map/psum | solution.py:285
  1252.2 145.0 %reduce-scatter.16.cloned.1.call-start = ((), (), s32[]{:S(2)}) async-start(), calls=%async_computation.19 | async-start | bytes 442368
  1269.7 225.3 %reduce-scatter.12.cloned.1.call-start = ((), (), s32[]{:S(2)}) async-start(), calls=%async_computation.17 | async-start | bytes 11796480 | tf_op jit(solution)/shard_map/reduce_scatter | solution.py:299
  1280.1 313.3 %reduce-scatter.14.cloned.1.call-start = ((), (), s32[]{:S(2)}) async-start(), calls=%async_computation.18 | async-start | bytes 11796480 | tf_op jit(solution)/shard_map/reduce_scatter | solution.py:302
  1290.1 342.5 %reduce-scatter.10.cloned.1.call-start = ((), (), s32[]{:S(2)}) async-start(), calls=%async_computation.16 | async-start | bytes 2654208 | tf_op jit(solution)/shard_map/reduce_scatter | solution.py:291
  1367.3 344.7 %reduce-scatter.8.cloned.1.call-start = ((), (), s32[]{:S(2)}) async-start(), calls=%async_computation.15 | async-start | bytes 7962624 | tf_op jit(solution)/shard_map/reduce_scatter | solution.py:290
  1443.7 268.4 %copy-start.1 = (f32[32,12]{0,1:T(8,128)S(1)}, f32[32,12]{0,1:T(8,128)}, u32[]{:S(2)}) copy-start(f32[32,12]{0,1:T(8,128)} %param.23) | copy-start | bytes 4612
  (63 other events, 712.4 us)
Sparse Core Ops, SparseCore 0:
  9.7 44.2 all-gather.3
  72.5 22.1 all-gather.5
  1252.3 112.1 all-reduce.4
  1366.6 30.5 reduce-scatter.15
  1400.5 94.5 reduce-scatter.11
  1498.3 94.9 reduce-scatter.13
  1596.3 36.2 reduce-scatter.9
  1635.6 76.4 reduce-scatter.7
where the time goes:
time: 1750 us; the launch traced here: 1720 us
  local copies, waits for them, and re-layouts  678 us (39%)
  waiting for transfers between devices  486 us (28%)
  blocking collectives  221 us (13%)
  matrix products  180 us (10%)
  other arithmetic  105 us (6%)
  starting transfers between devices  20.2 us (1%)
    rev x4, local copies, waits for them, and re-layouts, bias_rows(): tiled_rows.reshape(heads_dev, block_rows, length + block_rows)  194 us
    while x86, local copies, waits for them, and re-layouts  158 us
    rev x2, local copies, waits for them, and re-layouts, bias_grad_rows(): flipped = score_sum[:, ::-1, :]  97 us
    reduce_scatter x1, waiting for transfers between devices, body(): lax.psum_scatter(grad_exp_out.astype(jnp.bfloat16), 'seq', scatter_dimens...  94.1 us
    reduce_scatter x1, waiting for transfers between devices, body(): lax.psum_scatter(summed_qkv, 'shard', scatter_dimension=0, tiled=True)  79.5 us
    another operation x8, local copies, waits for them, and re-layouts, bias_rows(): jnp.tile(window, (1, block_rows + 1))  75.4 us
    psum x1, waiting for transfers between devices, body(): lax.psum(grad_qkv.astype(jnp.bfloat16), 'seq').astype(jnp.float32)  74.4 us
    reduce_scatter x1, waiting for transfers between devices, body(): lax.psum_scatter(grad_in.astype(jnp.bfloat16), 'seq', scatter_dimension=2...  48.2 us
  transfers between devices with their start and end apart: 13, of which 11 were waited for; matrix products, arithmetic and copies ran while one was open for 17% of the time, Pallas kernels for 0%

commit v1 on v0

v1 whole, which is shorter than its diff:
```python
import functools
import math

import jax
import jax.numpy as jnp
from jax import lax
from jax.experimental import pallas as pl
from jax.experimental.pallas import tpu as pltpu
from jax.sharding import PartitionSpec as P

f32 = jnp.float32
bf16 = jnp.bfloat16
LANES = 128
MIB = 1024 * 1024
FORWARD_TILE = 1024
norm_eps = 1e-06


def rms_forward(values, gain_vec):
    inverse = lax.rsqrt(jnp.mean(values * values, axis=-1, keepdims=True) + norm_eps)
    return (values * inverse * gain_vec, inverse)


def rms_backward(values, inverse, gain_vec, upstream):
    scaled = upstream * gain_vec
    gain_grad = jnp.sum(upstream * values * inverse, axis=(0, 1))
    inner_mean = jnp.mean(scaled * values, axis=-1, keepdims=True)
    return (inverse * scaled - values * inverse * inverse * inverse * inner_mean, gain_grad)


def nt(a, b):
    return lax.dot_general(a, b, (((1,), (1,)), ((), ())), preferred_element_type=f32)


def tn(a, b):
    return lax.dot_general(a, b, (((0,), (0,)), ((), ())), preferred_element_type=f32)


def attend_kernel(x_ref, w_ref, rel_ref, bucket_ref, qkv_ref, att_ref, prob_ref, toeplitz, *, block_rows):
    heads, length = prob_ref.shape[1], prob_ref.shape[2]
    width = att_ref.shape[-1]
    head_dim = width // heads
    span = 2 * length

    @pl.when(pl.program_id(0) == 0)
    def _():
        bucket_row = bucket_ref[...]
        for head in range(heads):
            row = jnp.zeros((1, span), f32)
            for bucket in range(rel_ref.shape[0]):
                row = jnp.where(bucket_row == bucket, rel_ref[bucket, head], row)
            toeplitz[head] = pltpu.roll(
                jnp.broadcast_to(row, (LANES, span)), span - LANES + 1, 1, stride=1, stride_axis=0
            )

    rows = x_ref[...].reshape(length, x_ref.shape[-1])
    qkv = jnp.dot(rows, w_ref[...], preferred_element_type=f32).astype(bf16)
    qkv_ref[...] = qkv.reshape(qkv_ref.shape)
    pieces = []
    for head in range(heads):
        at = head * head_dim
        q = qkv[:, at : at + head_dim]
        k = qkv[:, width + at : width + at + head_dim]
        v = qkv[:, 2 * width + at : 2 * width + at + head_dim]
        outs = []
        for block in range(length // block_rows):
            start = block * block_rows
            scores = nt(q[start : start + block_rows], k)
            parts = []
            for sub in range(block_rows // LANES):
                off = length - LANES - start - sub * LANES
                parts.append(scores[sub * LANES : (sub + 1) * LANES] + toeplitz[head, :, off : off + length])
            scores = jnp.concatenate(parts, axis=0) if len(parts) > 1 else parts[0]
            peak = jnp.max(scores, axis=-1, keepdims=True)
            expd = jnp.exp(scores - peak)
            total = jnp.sum(expd, axis=-1, keepdims=True)
            prob = (expd * (1.0 / total)).astype(bf16)
            prob_ref[0, head, start : start + block_rows, :] = prob
            outs.append(jnp.dot(prob, v, preferred_element_type=f32).astype(bf16))
        pieces.append(jnp.concatenate(outs, axis=0))
    att_ref[...] = jnp.concatenate(pieces, axis=1).reshape(att_ref.shape)


def attend(x, w, rel, buckets, heads, block_rows=256):
    pieces, seqs, piece, model = x.shape
    length = pieces * piece
    cols = w.shape[1]
    width = cols // 3
    bucket_row = jnp.pad(buckets, (0, 2 * length - buckets.shape[0])).reshape(1, 2 * length)
    return pl.pallas_call(
        functools.partial(attend_kernel, block_rows=block_rows),
        grid=(seqs,),
        in_specs=[
            pl.BlockSpec((pieces, 1, piece, model), lambda s: (0, s, 0, 0)),
            pl.BlockSpec(w.shape, lambda s: (0, 0)),
            pl.BlockSpec(memory_space=pltpu.SMEM),
            pl.BlockSpec(bucket_row.shape, lambda s: (0, 0)),
        ],
        out_specs=[
            pl.BlockSpec((pieces, 1, piece, cols), lambda s: (0, s, 0, 0)),
            pl.BlockSpec((pieces, 1, piece, width), lambda s: (0, s, 0, 0)),
            pl.BlockSpec((1, heads, length, length), lambda s: (s, 0, 0, 0)),
        ],
        out_shape=[
            jax.ShapeDtypeStruct((pieces, seqs, piece, cols), bf16),
            jax.ShapeDtypeStruct((pieces, seqs, piece, width), bf16),
            jax.ShapeDtypeStruct((seqs, heads, length, length), bf16),
        ],
        scratch_shapes=[pltpu.VMEM((heads, LANES, 2 * length), f32)],
        compiler_params=pltpu.CompilerParams(vmem_limit_bytes=52 * MIB),
        name="attend",
    )(x, w, rel, bucket_row)


def attend_back_kernel(qkv_ref, prob_ref, grad_ref, bucket_ref, out_ref, bias_ref, acc, ds_ref, *, block_rows):
    heads, length = prob_ref.shape[1], prob_ref.shape[2]
    width = grad_ref.shape[-1]
    head_dim = width // heads
    span = 2 * length
    step = pl.program_id(0)

    @pl.when(step == 0)
    def _():
        acc[...] = jnp.zeros_like(acc)

    qkv = qkv_ref[...].reshape(length, 3 * width)
    grad = grad_ref[...].reshape(length, width)
    dq, dk, dv = [], [], []
    for head in range(heads):
        at = head * head_dim
        q = qkv[:, at : at + head_dim]
        k = qkv[:, width + at : width + at + head_dim]
        v = qkv[:, 2 * width + at : 2 * width + at + head_dim]
        g = grad[:, at : at + head_dim]
        for block in range(length // block_rows):
            start = block * block_rows
            prob_grad = nt(g[start : start + block_rows], v)
            prob = prob_ref[0, head, start : start + block_rows, :].astype(f32)
            weighted = prob * prob_grad
            inner = jnp.sum(weighted, axis=-1, keepdims=True)
            score_grad = weighted - prob * inner
            ds_ref[start : start + block_rows, :] = score_grad.astype(bf16)
            for sub in range(block_rows // LANES):
                off = length - LANES - start - sub * LANES
                acc[head, :, off : off + length] += score_grad[sub * LANES : (sub + 1) * LANES]
        dq.append(jnp.dot(ds_ref[...], k, preferred_element_type=f32).astype(bf16))
        dk.append(tn(ds_ref[...], q).astype(bf16))
        dv.append(tn(prob_ref[0, head], g).astype(bf16))
    out_ref[...] = jnp.concatenate(dq + dk + dv, axis=1).reshape(out_ref.shape)

    @pl.when(step == pl.num_programs(0) - 1)
    def _():
        buckets = bias_ref.shape[0]
        hot = lax.broadcasted_iota(jnp.int32, (buckets, span), 0) == bucket_ref[...]
        sums = []
        for head in range(heads):
            part = acc[head]
            rows = LANES
            while rows > 8:
                rows //= 2
                part = part[:rows] + pltpu.roll(part[rows:], span - rows, 1)
            offsets = part[0:1]
            for row in range(1, 8):
                offsets = offsets + pltpu.roll(part[row : row + 1], span - row, 1)
            offsets = pltpu.roll(offsets, LANES - 1, 1)
            sums.append(offsets)
        lane = lax.broadcasted_iota(jnp.int32, bias_ref.shape, 1)
        result = jnp.zeros(bias_ref.shape, f32)
        for head in range(heads):
            total = jnp.sum(jnp.where(hot, sums[head], 0.0), axis=1, keepdims=True)
            result = jnp.where(lane == head, total, result)
        bias_ref[...] = result


def attend_back(qkv, prob, grad, buckets, bucket_count, block_rows=256):
    pieces, seqs, piece, cols = qkv.shape
    heads, length = prob.shape[1], prob.shape[2]
    width = cols // 3
    bucket_row = jnp.pad(buckets, (0, 2 * length - buckets.shape[0]), constant_values=-1).reshape(1, 2 * length)
    token_spec = lambda n: pl.BlockSpec((pieces, 1, piece, n), lambda s: (0, s, 0, 0))
    return pl.pallas_call(
        functools.partial(attend_back_kernel, block_rows=block_rows),
        grid=(seqs,),
        in_specs=[
            token_spec(cols),
            pl.BlockSpec((1, heads, length, length), lambda s: (s, 0, 0, 0)),
            token_spec(width),
            pl.BlockSpec(bucket_row.shape, lambda s: (0, 0)),
        ],
        out_specs=[token_spec(cols), pl.BlockSpec((bucket_count, LANES), lambda s: (0, 0))],
        out_shape=[
            jax.ShapeDtypeStruct(qkv.shape, bf16),
            jax.ShapeDtypeStruct((bucket_count, LANES), f32),
        ],
        scratch_shapes=[
            pltpu.VMEM((heads, LANES, 2 * length), f32),
            pltpu.VMEM((length, length), bf16),
        ],
        compiler_params=pltpu.CompilerParams(vmem_limit_bytes=52 * MIB),
        name="attend_back",
    )(qkv, prob, grad, bucket_row)


ROOT_HALF = 1.0 / math.sqrt(2.0)
DENSITY = 1.0 / math.sqrt(2.0 * math.pi)


def gelu_and_slope(v):
    cumulative = 0.5 * (1.0 + lax.erf(v * ROOT_HALF))
    return v * cumulative, cumulative + v * (jnp.exp(-0.5 * v * v) * DENSITY)


def expert_kernel(x_ref, win_ref, wout_ref, y_ref, slope_ref, acc):
    tile = pl.program_id(1)
    rows = acc.shape[0]
    x = x_ref[...].reshape(rows, x_ref.shape[-1])
    pre = jnp.dot(x, win_ref[0], preferred_element_type=f32)
    hidden, slope = gelu_and_slope(pre)
    slope_ref[0] = slope.astype(bf16)
    part = jnp.dot(hidden.astype(bf16), wout_ref[0], preferred_element_type=f32)

    @pl.when(tile == 0)
    def _():
        acc[...] = part

    @pl.when(tile > 0)
    def _():
        acc[...] += part

    @pl.when(tile == pl.num_programs(1) - 1)
    def _():
        y_ref[...] = acc[...].astype(bf16).reshape(y_ref.shape)


def expert_forward(x, w_in, w_out, tile):
    sources, experts, slots, model = x.shape
    hidden = w_in.shape[2]
    rows = sources * slots
    row_spec = pl.BlockSpec((sources, 1, slots, model), lambda e, f: (0, e, 0, 0))
    return pl.pallas_call(
        expert_kernel,
        grid=(experts, hidden // tile),
        in_specs=[
            row_spec,
            pl.BlockSpec((1, model, tile), lambda e, f: (e, 0, f)),
            pl.BlockSpec((1, tile, model), lambda e, f: (e, f, 0)),
        ],
        out_specs=[row_spec, pl.BlockSpec((1, rows, tile), lambda e, f: (e, 0, f))],
        out_shape=[
            jax.ShapeDtypeStruct(x.shape, bf16),
            jax.ShapeDtypeStruct((experts, rows, hidden), bf16),
        ],
        scratch_shapes=[pltpu.VMEM((rows, model), f32)],
        compiler_params=pltpu.CompilerParams(vmem_limit_bytes=52 * MIB),
        name="expert_forward",
    )(x, w_in, w_out)


def expert_back_kernel(g_ref, win_ref, wout_ref, slope_ref, y_ref, acc):
    tile = pl.program_id(1)
    rows = acc.shape[0]
    g = g_ref[...].reshape(rows, g_ref.shape[-1])
    pre_grad = (nt(g, wout_ref[0]) * slope_ref[0].astype(f32)).astype(bf16)
    part = nt(pre_grad, win_ref[0])

    @pl.when(tile == 0)
    def _():
        acc[...] = part

    @pl.when(tile > 0)
    def _():
        acc[...] += part

    @pl.when(tile == pl.num_programs(1) - 1)
    def _():
        y_ref[...] = acc[...].astype(bf16).reshape(y_ref.shape)


def expert_backward(g, w_in, w_out, slope, tile):
    sources, experts, slots, model = g.shape
    hidden = w_in.shape[2]
    rows = sources * slots
    row_spec = pl.BlockSpec((sources, 1, slots, model), lambda e, f: (0, e, 0, 0))
    return pl.pallas_call(
        expert_back_kernel,
        grid=(experts, hidden // tile),
        in_specs=[
            row_spec,
            pl.BlockSpec((1, model, tile), lambda e, f: (e, 0, f)),
            pl.BlockSpec((1, tile, model), lambda e, f: (e, f, 0)),
            pl.BlockSpec((1, rows, tile), lambda e, f: (e, 0, f)),
        ],
        out_specs=row_spec,
        out_shape=jax.ShapeDtypeStruct(g.shape, bf16),
        scratch_shapes=[pltpu.VMEM((rows, model), f32)],
        compiler_params=pltpu.CompilerParams(vmem_limit_bytes=52 * MIB),
        name="expert_backward",
    )(g, w_in, w_out, slope)


def weight_grad_kernel(x_ref, g_ref, win_ref, wout_ref, gin_ref, gout_ref):
    step = pl.program_id(1)
    rows = x_ref.shape[1] * x_ref.shape[3]
    x = x_ref[...].reshape(rows, x_ref.shape[-1])
    g = g_ref[...].reshape(rows, g_ref.shape[-1])
    pre = jnp.dot(x, win_ref[0], preferred_element_type=f32)
    hidden, slope = gelu_and_slope(pre)
    pre_grad = (nt(g, wout_ref[0]) * slope).astype(bf16)
    gin = tn(x, pre_grad)
    gout = tn(hidden.astype(bf16), g)

    @pl.when(step == 0)
    def _():
        gin_ref[0] = gin
        gout_ref[0] = gout

    @pl.when(step > 0)
    def _():
        gin_ref[0] += gin
        gout_ref[0] += gout


def weight_grads(x, g, w_in, w_out, quarter):
    pieces, sources, experts, slots, model = x.shape
    cols = w_in.shape[2] // pieces
    row_spec = pl.BlockSpec((1, sources, 1, slots, model), lambda e, p, q: (p, 0, e, 0, 0))
    grid_spec = pltpu.PrefetchScalarGridSpec(
        num_scalar_prefetch=1,
        grid=(experts, pieces),
        in_specs=[
            row_spec,
            row_spec,
            pl.BlockSpec((1, model, cols), lambda e, p, q: (e, 0, q[0])),
            pl.BlockSpec((1, cols, model), lambda e, p, q: (e, q[0], 0)),
        ],
        out_specs=[
            pl.BlockSpec((1, model, cols), lambda e, p, q: (e, 0, 0)),
            pl.BlockSpec((1, cols, model), lambda e, p, q: (e, 0, 0)),
        ],
    )

    def kern(q_ref, *refs):
        weight_grad_kernel(*refs)

    return pl.pallas_call(
        kern,
        grid_spec=grid_spec,
        out_shape=[
            jax.ShapeDtypeStruct((experts, model, cols), f32),
            jax.ShapeDtypeStruct((experts, cols, model), f32),
        ],
        compiler_params=pltpu.CompilerParams(vmem_limit_bytes=52 * MIB),
        name="weight_grads",
    )(quarter, x, g, w_in, w_out)


def body(
    block_input,
    gain_attn,
    gain_ffn,
    w_qkv,
    w_out,
    w_router,
    rel_bias,
    w_in,
    w_exp_out,
    expert_id,
    capacity_slot,
    buckets,
    output_grad,
):
    seqs, piece, model = block_input.shape
    seq_ways = lax.axis_size("seq")
    shard_ways = lax.axis_size("shard")
    bucket_count, heads_all = rel_bias.shape
    heads = heads_all // seq_ways
    width = model // seq_ways
    experts = w_router.shape[1]
    tokens = seqs * piece
    capacity = 2 * tokens // experts
    positions = experts * capacity
    slot_shape = (shard_ways, experts // shard_ways, capacity, model)
    weight_rows = w_qkv.shape[0]
    seq_index = lax.axis_index("seq")

    own_columns = lax.dynamic_slice_in_dim(
        w_qkv.reshape(weight_rows, 3, model), seq_index * width, width, 2
    ).reshape(weight_rows, 3 * width)
    head_weight = lax.all_gather(own_columns, "shard", axis=0, tiled=True)
    inputs = block_input.astype(f32)
    normalized_input, inverse_one = rms_forward(inputs, gain_attn)
    normed_low = normalized_input.astype(bf16)
    normed_all = lax.all_gather(normed_low, "seq")
    bias_dev = lax.dynamic_slice_in_dim(rel_bias, seq_index * heads, heads, 1)
    qkv_heads, attended, probs = attend(normed_all, head_weight, bias_dev, buckets, heads)
    attended_tok = lax.all_to_all(attended, "seq", 0, 0, tiled=True)
    dense = lax.all_gather(
        jnp.concatenate([w_out, w_router], axis=1), "shard", axis=0, tiled=True
    )
    output_projection = dense[:, :model].reshape(seq_ways, width, model)
    routing_weight = dense[:, model:]
    weight_groups = lax.all_gather(head_weight, "seq")

    residual_branch = jnp.einsum(
        "gstd,gde->ste", attended_tok, output_projection, preferred_element_type=f32
    )
    middle = inputs + residual_branch
    second_residual, inverse_two = rms_forward(middle, gain_ffn)
    second_low = second_residual.astype(bf16)
    router_logits = jnp.einsum("std,de->ste", second_low, routing_weight, preferred_element_type=f32)
    logit_peak = jnp.max(router_logits, axis=-1, keepdims=True)
    exp_logits = jnp.exp(router_logits - logit_peak)
    router_probs = exp_logits / jnp.sum(exp_logits, axis=-1, keepdims=True)
    chosen = (expert_id[..., None] == jnp.arange(experts, dtype=jnp.int32)).astype(f32)
    gate_prob = jnp.sum(router_probs * chosen, axis=-1)
    target = jnp.where(capacity_slot < capacity, expert_id * capacity + capacity_slot, -1).reshape(
        tokens
    )
    dispatch_hot = (jnp.arange(positions, dtype=jnp.int32)[:, None] == target[None, :]).astype(bf16)
    upstream = output_grad.astype(f32)
    out_grad = (gate_prob[..., None] * upstream).astype(bf16).reshape(tokens, model)

    def dispatch(rows):
        sent = jnp.dot(dispatch_hot, rows, preferred_element_type=f32).astype(bf16)
        return lax.all_to_all(sent.reshape(slot_shape), "shard", 0, 0, tiled=True)

    def combine(rows):
        back = lax.all_to_all(rows, "shard", 0, 0, tiled=True).reshape(positions, model)
        merged = jnp.einsum("pt,pd->td", dispatch_hot, back, preferred_element_type=f32)
        return merged.reshape(seqs, piece, model)

    arrived = dispatch(second_low.reshape(tokens, model))
    out_arrived = dispatch(out_grad)
    expert_out, slope = expert_forward(arrived, w_in, w_exp_out, FORWARD_TILE)
    token_out = combine(expert_out)
    rows_grad = expert_backward(out_arrived, w_in, w_exp_out, slope, FORWARD_TILE)
    second_grad = combine(rows_grad)
    arrived_all = lax.all_gather(arrived, "seq")
    out_all = lax.all_gather(out_arrived, "seq")
    grad_in_part, grad_exp_part = weight_grads(
        arrived_all, out_all, w_in, w_exp_out, seq_index.astype(jnp.int32).reshape(1)
    )

    block_output = (middle + gate_prob[..., None] * token_out).astype(bf16)
    gate_grad = jnp.sum(upstream * token_out, axis=-1)
    prob_pick = chosen * gate_grad[..., None]
    logit_grad = router_probs * (
        prob_pick - jnp.sum(router_probs * prob_pick, axis=-1, keepdims=True)
    )
    logit_low = logit_grad.astype(bf16)
    grad_router = jnp.einsum("std,ste->de", second_low, logit_low, preferred_element_type=f32)
    second_grad = second_grad + jnp.einsum(
        "ste,de->std", logit_low, routing_weight, preferred_element_type=f32
    )
    middle_norm_grad, grad_gain_two = rms_backward(middle, inverse_two, gain_ffn, second_grad)
    middle_grad = upstream + middle_norm_grad
    branch_low = middle_grad.astype(bf16)
    attended_grad = jnp.einsum(
        "ste,gde->gstd", branch_low, output_projection, preferred_element_type=f32
    ).astype(bf16)
    attended_grad_heads = lax.all_to_all(attended_grad, "seq", 0, 0, tiled=True)
    grad_out = jnp.einsum(
        "gstd,ste->gde", attended_tok, branch_low, preferred_element_type=f32
    ).reshape(model, model)
    grad_dense = jnp.concatenate([grad_out.astype(bf16), grad_router.astype(bf16)], axis=1)
    grad_dense = lax.psum_scatter(grad_dense, "shard", scatter_dimension=0, tiled=True)
    grad_dense = lax.psum(grad_dense, "seq").astype(f32)
    grad_gain_two = lax.psum(grad_gain_two, ("seq", "shard"))

    qkv_grad, bias_grad_dev = attend_back(
        qkv_heads, probs, attended_grad_heads, buckets, bucket_count
    )
    qkv_grad_tok = lax.all_to_all(qkv_grad, "seq", 0, 0, tiled=True)
    grad_columns = jnp.einsum(
        "pstd,pste->de", normed_all, qkv_grad, preferred_element_type=f32
    ).astype(bf16)
    grad_columns = lax.psum_scatter(grad_columns, "shard", scatter_dimension=0, tiled=True)
    grad_qkv = lax.all_gather(grad_columns, "seq")
    grad_qkv = (
        grad_qkv.reshape(seq_ways, weight_rows, 3, width)
        .transpose(1, 2, 0, 3)
        .reshape(weight_rows, 3 * model)
        .astype(f32)
    )
    normed_grad = jnp.einsum(
        "gste,gde->std", qkv_grad_tok, weight_groups, preferred_element_type=f32
    )
    input_norm_grad, grad_gain_one = rms_backward(inputs, inverse_one, gain_attn, normed_grad)
    input_grad = middle_grad + input_norm_grad
    bias_grad = lax.dynamic_update_slice_in_dim(
        jnp.zeros((bucket_count, heads_all), f32), bias_grad_dev[:, :heads], seq_index * heads, 1
    )
    bias_grad, grad_gain_one = lax.psum((bias_grad, grad_gain_one), ("seq", "shard"))
    return (
        block_output,
        input_grad,
        grad_gain_one,
        grad_gain_two,
        grad_qkv,
        grad_dense[:, :model],
        grad_dense[:, model:],
        bias_grad,
        grad_in_part,
        grad_exp_part,
    )


def solution(mesh):
    placed = (
        P("shard", "seq", None),
        P(),
        P(),
        P("shard", None),
        P("shard", None),
        P("shard", None),
        P(),
        P("shard", None, None),
        P("shard", None, None),
        P("shard", "seq"),
        P("shard", "seq"),
        P(),
        P("shard", "seq", None),
    )
    return jax.shard_map(
        body,
        mesh=mesh,
        in_specs=placed,
        out_specs=(
            P("shard", "seq", None),
            P("shard", "seq", None),
            P(),
            P(),
            P("shard", None),
            P("shard", None),
            P("shard", None),
            P(),
            P("shard", None, "seq"),
            P("shard", "seq", None),
        ),
        check_vma=False,
    )
```

time: 1750 us -> 695 us (0.40)
  local copies, waits for them, and re-layouts: 678 us -> 24.3 us
  waiting for transfers between devices: 486 us -> 295 us
  matrix products: 180 us -> 29.9 us
  Pallas kernels: 0 us -> 112 us
  other arithmetic: 105 us -> 14.3 us
  blocking collectives: 221 us -> 173 us
    rev x6 -> x0, local copies, waits for them, and re-layouts: 291 us -> none  [the longest x4 194 us: bias_rows(): tiled_rows.reshape(heads_dev, block_rows, length + block_rows)]
    reduce_scatter x4 -> x1, waiting for transfers between devices: 257 us -> 17 us  [body(): lax.psum_scatter(grad_columns, 'shard', scatter_dimension=0, tiled=True)]
    while x86 -> x0, local copies, waits for them, and re-layouts: 158 us -> none
    dot_general x33 -> x10, matrix products: 177 us -> 25.9 us  [the longest x1 6.46 us: body(): jnp.einsum('gste,gde->std', qkv_grad_tok, weight_groups, preferred_elemen...]
    all_gather x2 -> x5, waiting for transfers between devices: 44.6 us -> 194 us  [the longest x1 72.2 us: body(): out_all = lax.all_gather(out_arrived, 'seq')]
    pallas_call x0 -> x5, Pallas kernels: none -> 112 us  [the longest x1 29.9 us: weight_grads(): pl.pallas_call(kern, grid_spec=grid_spec, out_shape=[jax.ShapeDtypeStruct...]
    another operation x12 -> x0, local copies, waits for them, and re-layouts: 86.5 us -> none  [the longest x8 75.4 us: bias_rows(): jnp.tile(window, (1, block_rows + 1))]
    psum x1, waiting for transfers between devices: 74.4 us -> 0.01 us  [body(): grad_dense = lax.psum(grad_dense, 'seq').astype(f32)]
  transfers between devices with their start and end apart: 13 -> 12, of which waited for: 11 -> 8; matrix products, arithmetic and copies ran while one was open for 17% -> 6% of each run, Pallas kernels for 0% -> 7%
where the time goes in v1:
time: 695 us; the launch traced here: 681 us
  waiting for transfers between devices  295 us (42%)
  blocking collectives  173 us (25%)
  Pallas kernels  112 us (16%)
  matrix products  29.9 us (4%)
  local copies, waits for them, and re-layouts  24.3 us (3%)
  starting transfers between devices  17.4 us (3%)
  between operations  14.8 us (2%)
  other arithmetic  14.3 us (2%)
    all_to_all x2, blocking collectives, dispatch(): return lax.all_to_all(sent.reshape(slot_shape), 'shard', 0, 0, tiled=True)  83.3 us
    all_to_all x2, waiting for transfers between devices, combine(): lax.all_to_all(rows, 'shard', 0, 0, tiled=True).reshape(positions, model)  72.8 us
    all_gather x1, waiting for transfers between devices, body(): out_all = lax.all_gather(out_arrived, 'seq')  72.2 us
    all_gather x1, waiting for transfers between devices, body(): arrived_all = lax.all_gather(arrived, 'seq')  66 us
    psum x1, blocking collectives, body(): lax.psum((bias_grad, grad_gain_one), ('seq', 'shard'))  39.8 us
    pallas_call x1, Pallas kernels, weight_grads(): pl.pallas_call(kern, grid_spec=grid_spec, out_shape=[jax.ShapeDtypeStruct...  29.9 us
    all_gather x1, waiting for transfers between devices, body(): weight_groups = lax.all_gather(head_weight, 'seq')  29 us
    all_gather x1, waiting for transfers between devices, body(): normed_all = lax.all_gather(normed_low, 'seq')  27.2 us
  transfers between devices with their start and end apart: 12, of which 8 were waited for; matrix products, arithmetic and copies ran while one was open for 6% of the time, Pallas kernels for 7%

profile of v1, /device:TPU:0, one launch (start us, length us, event | category | flops | bytes accessed | tf_op | source)
XLA Modules:
  0.0 680.9 jit_solution(6431180265018932327)
XLA Ops:
  12.8 17.9 %all_gather.38.w_ref = bf16[768,576]{1,0:T(8,128)(2,1)S(1)} all-gather(bf16[96,576]{1,0:T(8,128)(2,1)S(1)} %copy.103), channel_id=1, replica_groups=mesh['seq'=4,'shard'=8] {'shard'}, dimensions={0}, use_global_device_ids=true | all-gather | bytes 995328 | tf_op jit(solution)/shard_map/all_gather | solution.py:389
  30.7 27.2 %all-gather.13.cloned.1.call-done = bf16[8,256,768]{2,1,0:T(8,128)(2,1)} async-done(((bf16[2,256,768]{2,1,0:T(8,128)(2,1)}), bf16[8,256,768]{2,1,0:T(8,128)(2,1)}) %all-gather.13.cloned.1.call-update) | async-done | bytes 3145744 | tf_op jit(solution)/shard_map/all_gather | solution.py:393
  57.9 23.0 %attend.1 = (bf16[4,2,256,576]{3,2,1,0:T(8,128)(2,1)}, bf16[4,2,256,192]{3,2,1,0:T(8,128)(2,1)}, bf16[2,3,1024,1024]{3,2,1,0:T(8,128)(2,1)}) custom-call(bf16[4,2,256,768]{3,2,1,0:T(8,128)(2,1)} %bitcast.100, bf16[768,576]{1,0:T(8,128)(2,1)S(1)} %all_gather.38.w_ref, f32[32,3]{1,0:T(8,128)S(1)} %copy.132.rel_ref, s32[1,2048]{1,0:T(1,128)S(1)} %bitcast.93), custom_call_target="tpu_custom_call" | custom-call | tf_op jit(solution)/shard_map/attend/pallas_call | solution.py:90
  83.1 4.0 all-to-all-start
  89.6 8.5 %all-to-all-done = bf16[4,2,256,192]{2,3,1,0:T(8,128)(2,1)S(1)} async-done(((bf16[4,2,256,192]{2,3,1,0:T(8,128)(2,1)}), bf16[4,2,256,192]{2,3,1,0:T(8,128)(2,1)S(1)}, u32[]{:S(2)}, u32[]{:S(2)}) %all-to-all-start) | async-done | bytes 786464 | tf_op jit(solution)/shard_map/all_to_all | solution.py:396
  101.9 42.3 %all_to_all.35.x_ref = bf16[8,2,64,768]{3,2,1,0:T(8,128)(2,1)} all-to-all(bf16[8,2,64,768]{3,2,1,0:T(8,128)(2,1)S(1)} %bitcast.103), channel_id=1, replica_groups=mesh['seq'=4,'shard'=8] {'shard'}, dimensions={0} | all-to-all | bytes 3145728 | tf_op jit(solution)/shard_map/all_to_all | solution.py:425
  144.3 17.5 %expert_forward.1 = (bf16[8,2,64,768]{3,2,1,0:T(8,128)(2,1)}, bf16[2,512,3072]{2,1,0:T(8,128)(2,1)}) custom-call(bf16[8,2,64,768]{3,2,1,0:T(8,128)(2,1)} %all_to_all.35.x_ref, bf16[2,768,3072]{2,1,0:T(8,128)(2,1)} %refs_2_.1, bf16[2,3072,768]{2,1,0:T(8,128)(2,1)} %refs_3_.1), custom_call_target="tpu_custom_call" | custom-call | tf_op jit(solution)/shard_map/expert_forward/pallas_call | solution.py:240
  161.8 4.3 all-to-all-start.2
  168.6 35.3 %all-to-all-done.2 = bf16[8,2,64,768]{3,2,1,0:T(8,128)(2,1)} async-done(((bf16[8,2,64,768]{3,2,1,0:T(8,128)(2,1)}), bf16[8,2,64,768]{3,2,1,0:T(8,128)(2,1)}, u32[]{:S(2)}, u32[]{:S(2)}) %all-to-all-start.2) | async-done | bytes 1572896 | tf_op jit(solution)/shard_map/all_to_all | solution.py:428
  203.9 3.7 fusion.13
  208.9 41.0 %all_to_all.36.g_ref = bf16[8,2,64,768]{3,2,1,0:T(8,128)(2,1)} all-to-all(bf16[8,2,64,768]{3,2,1,0:T(8,128)(2,1)S(1)} %bitcast.102), channel_id=1, replica_groups=mesh['seq'=4,'shard'=8] {'shard'}, dimensions={0} | all-to-all | bytes 3145728 | tf_op jit(solution)/shard_map/all_to_all | solution.py:425
  249.9 16.6 %expert_backward.1 = bf16[8,2,64,768]{3,2,1,0:T(8,128)(2,1)} custom-call(bf16[8,2,64,768]{3,2,1,0:T(8,128)(2,1)} %all_to_all.36.g_ref, bf16[2,768,3072]{2,1,0:T(8,128)(2,1)} %refs_2_.1, bf16[2,3072,768]{2,1,0:T(8,128)(2,1)} %refs_3_.1, bf16[2,512,3072]{2,1,0:T(8,128)(2,1)} %get-tuple-element.21.slope_ref), custom_call_target="tpu_custom_call" | custom-call | tf_op jit(solution)/shard_map/expert_backward/pallas_call | solution.py:284
  266.5 4.3 all-to-all-start.4
  271.1 37.6 %all-to-all-done.4 = bf16[8,2,64,768]{3,2,1,0:T(8,128)(2,1)} async-done(((bf16[8,2,64,768]{3,2,1,0:T(8,128)(2,1)}), bf16[8,2,64,768]{3,2,1,0:T(8,128)(2,1)}, u32[]{:S(2)}, u32[]{:S(2)}) %all-to-all-start.4) | async-done | bytes 1572896 | tf_op jit(solution)/shard_map/all_to_all | solution.py:428
  308.6 2.6 fusion.37
  311.2 2.8 multiply_reduce_fusion
  313.9 3.7 convert_add_fusion.1
  325.0 14.0 %all_to_all.37 = bf16[4,2,256,192]{2,3,1,0:T(8,128)(2,1)S(1)} all-to-all(bf16[4,2,256,192]{2,3,1,0:T(8,128)(2,1)S(1)} %fusion.18), channel_id=1, replica_groups=mesh['seq'=4,'shard'=8] {'seq'}, dimensions={0} | all-to-all | bytes 1572864 | tf_op jit(solution)/shard_map/all_to_all | solution.py:461
  339.5 25.0 %attend_back.1 = (bf16[4,2,256,576]{3,2,1,0:T(8,128)(2,1)}, f32[32,128]{1,0:T(8,128)S(1)}) custom-call(bf16[4,2,256,576]{3,2,1,0:T(8,128)(2,1)} %get-tuple-element.22.qkv_ref, bf16[2,3,1024,1024]{3,2,1,0:T(8,128)(2,1)} %get-tuple-element.23.prob_ref, bf16[4,2,256,192]{3,2,1,0:T(8,128)(2,1)S(1)} %copy.108.grad_ref, s32[1,2048]{1,0:T(1,128)S(1)} %bitcast.92), custom_call_target="tpu_custom_call" | custom-call | tf_op jit(solution)/shard_map/attend_back/pallas_call | solution.py:181
  364.5 5.5 bitcast_convert_fusion.1
  374.0 4.3 copy.109
  378.3 4.5 all-to-all-start.6
  383.0 17.0 %reduce-scatter.7.cloned.1.call-done = bf16[96,576]{1,0:T(8,128)(2,1)} async-done(((bf16[768,576]{1,0:T(8,128)(2,1)}), bf16[96,576]{1,0:T(8,128)(2,1)}) %reduce-scatter.7.cloned.1.call-update) | async-done | bytes 110608 | tf_op jit(solution)/shard_map/reduce_scatter | solution.py:477
  400.0 18.4 %all-gather.2 = bf16[384,576]{1,0:T(8,128)(2,1)S(1)} all-gather(bf16[96,576]{1,0:T(8,128)(2,1)} %reduce-scatter.7.cloned.1.call-done), channel_id=4, replica_groups=mesh['seq'=4,'shard'=8] {'seq'}, dimensions={0}, use_global_device_ids=true | all-gather | bytes 552960 | tf_op jit(solution)/shard_map/all_gather | solution.py:478
  421.2 3.0 reshape.152
  424.3 29.0 %all-gather.15.cloned.1.call-done = bf16[3072,576]{1,0:T(8,128)(2,1)} async-done(((bf16[768,576]{1,0:T(8,128)(2,1)}), bf16[3072,576]{1,0:T(8,128)(2,1)}) %all-gather.15.cloned.1.call-update) | async-done | bytes 3538960 | tf_op jit(solution)/shard_map/all_gather | solution.py:402
  453.3 6.5 fusion.17
  459.7 39.8 %all-reduce.2 = (f32[768]{0:T(1024)}, f32[768]{0:T(1024)}, f32[32,12]{0,1:T(8,128)}) all-reduce(f32[768]{0:T(1024)S(1)} %get-tuple-element.90, f32[768]{0:T(1024)S(1)} %get-tuple-element.88, f32[32,12]{0,1:T(8,128)S(1)} %dynamic_update_slice.3), channel_id=1, replica_groups=mesh['seq'=4,'shard'=8] {'seq','shard'}, use_global_device_ids=true, to_apply=%region_10.11 | all-reduce | flops 1920 | bytes 15360 | tf_op jit(solution)/shard_map/psum | solution.py:493
  499.5 3.1 fusion.11
  505.7 66.0 %all-gather.17.cloned.1.call-done = bf16[32,2,64,768]{3,2,1,0:T(8,128)(2,1)} async-done(((bf16[8,2,64,768]{3,2,1,0:T(8,128)(2,1)}), bf16[32,2,64,768]{3,2,1,0:T(8,128)(2,1)}) %all-gather.17.cloned.1.call-update) | async-done | bytes 6291472 | tf_op jit(solution)/shard_map/all_gather | solution.py:438
  571.7 72.2 %all-gather.19.cloned.1.call-done = bf16[32,2,64,768]{3,2,1,0:T(8,128)(2,1)} async-done(((bf16[8,2,64,768]{3,2,1,0:T(8,128)(2,1)}), bf16[32,2,64,768]{3,2,1,0:T(8,128)(2,1)}) %all-gather.19.cloned.1.call-update) | async-done | bytes 6291472 | tf_op jit(solution)/shard_map/all_gather | solution.py:439
  643.9 29.9 %weight_grads.1 = (f32[2,768,768]{2,1,0:T(8,128)}, f32[2,768,768]{2,1,0:T(8,128)}) custom-call(s32[1]{0:T(128)} %bitcast.32.q_ref, bf16[4,8,2,64,768]{4,3,2,1,0:T(8,128)(2,1)} %bitcast.96, bf16[4,8,2,64,768]{4,3,2,1,0:T(8,128)(2,1)} %bitcast.97, bf16[2,768,3072]{2,1,0:T(8,128)(2,1)} %refs_2_.1, bf16[2,3072,768]{2,1,0:T(8,128)(2,1)} %refs_3_.1), custom_call_target="tpu_custom_call" | custom-call | tf_op jit(solution)/shard_map/weight_grads/pallas_call | solution.py:345
  (99 shorter events, 35.7 us)
Async XLA Ops:
  7.2 5.5 copy-start
  7.2 3.9 copy-start.15
  7.2 4.0 copy-start.10
  7.2 50.6 %all-gather.13.cloned.1.call-start = ((), (), s32[]{:S(2)}) async-start(), calls=%async_computation.11 | async-start | bytes 3932160 | tf_op jit(solution)/shard_map/all_gather | solution.py:393
  8.7 3.3 copy-start.9
  11.0 1.8 copy-start.14
  11.0 76.1 %all-gather.11.cloned.1.call-start = ((), (), s32[]{:S(2)}) async-start(), calls=%async_computation.9 | async-start | bytes 1548288 | tf_op jit(solution)/shard_map/all_gather | solution.py:397
  30.7 50.2 %copy-start.2 = (bf16[768,576]{1,0:T(8,128)(2,1)}, bf16[768,576]{1,0:T(8,128)(2,1)S(1)}, u32[]{:S(2)}) copy-start(bf16[768,576]{1,0:T(8,128)(2,1)S(1)} %all_gather.38.w_ref) | copy-start | bytes 2654212
  80.9 6.2 copy-start.12
  80.9 6.2 copy-start.16
  83.1 15.0 %all-to-all-start = ((bf16[4,2,256,192]{2,3,1,0:T(8,128)(2,1)}), bf16[4,2,256,192]{2,3,1,0:T(8,128)(2,1)S(1)}, u32[]{:S(2)}, u32[]{:S(2)}) async-start(bf16[4,2,256,192]{2,3,1,0:T(8,128)(2,1)} %copy.105), calls=%async_computation | async-start | bytes 1572864 | tf_op jit(solution)/shard_map/all_to_all | solution.py:396
  87.1 11.1 %copy-start.3 = (bf16[2,256,768]{2,1,0:T(8,128)(2,1)S(1)}, bf16[2,256,768]{2,1,0:T(8,128)(2,1)}, u32[]{:S(2)}) copy-start(bf16[2,256,768]{2,1,0:T(8,128)(2,1)} %param.13) | copy-start | bytes 2359300
  98.1 2.5 copy-start.6
  98.1 2.5 copy-start.11
  161.8 42.1 %all-to-all-start.2 = ((bf16[8,2,64,768]{3,2,1,0:T(8,128)(2,1)}), bf16[8,2,64,768]{3,2,1,0:T(8,128)(2,1)}, u32[]{:S(2)}, u32[]{:S(2)}) async-start(bf16[8,2,64,768]{3,2,1,0:T(8,128)(2,1)} %get-tuple-element.20), calls=%async_computation.2 | async-start | bytes 3145728 | tf_op jit(solution)/shard_map/all_to_all | solution.py:428
  166.1 37.8 %copy-start.5 = (bf16[2,256,768]{2,1,0:T(8,128)(2,1)S(1)}, bf16[2,256,768]{2,1,0:T(8,128)(2,1)}, u32[]{:S(2)}) copy-start(bf16[2,256,768]{2,1,0:T(8,128)(2,1)} %param.25) | copy-start | bytes 2359300
  266.5 42.1 %all-to-all-start.4 = ((bf16[8,2,64,768]{3,2,1,0:T(8,128)(2,1)}), bf16[8,2,64,768]{3,2,1,0:T(8,128)(2,1)}, u32[]{:S(2)}, u32[]{:S(2)}) async-start(bf16[8,2,64,768]{3,2,1,0:T(8,128)(2,1)} %expert_backward.1), calls=%async_computation.4 | async-start | bytes 3145728 | tf_op jit(solution)/shard_map/all_to_all | solution.py:428
  270.8 99.9 %reduce-scatter.9.cloned.1.call-start = ((), (), s32[]{:S(2)}) async-start(), calls=%async_computation.16 | async-start | bytes 1548288
  313.9 3.7 copy-start.7
  322.8 77.2 %reduce-scatter.7.cloned.1.call-start = ((), (), s32[]{:S(2)}) async-start(), calls=%async_computation.15 | async-start | bytes 1105920 | tf_op jit(solution)/shard_map/reduce_scatter | solution.py:477
  339.5 25.1 %copy-start.8 = (bf16[8,256,768]{2,1,0:T(8,128)(2,1)S(1)}, bf16[8,256,768]{2,1,0:T(8,128)(2,1)}, u32[]{:S(2)}) copy-start(bf16[8,256,768]{2,1,0:T(8,128)(2,1)} %all-gather.13.cloned.1.call-done) | copy-start | bytes 9437188
  370.0 83.2 %all-gather.15.cloned.1.call-start = ((), (), s32[]{:S(2)}) async-start(), calls=%async_computation.12 | async-start | bytes 4915200 | tf_op jit(solution)/shard_map/all_gather | solution.py:402
  370.6 132.0 %all-reduce.5.cloned.1.call-start = ((), (), s32[]{:S(2)}) async-start(), calls=%async_computation.10 | async-start | bytes 401408 | tf_op jit(solution)/shard_map/psum | solution.py:467
  372.5 199.2 %all-gather.17.cloned.1.call-start = ((), (), s32[]{:S(2)}) async-start(), calls=%async_computation.13 | async-start | bytes 7864320 | tf_op jit(solution)/shard_map/all_gather | solution.py:438
  373.2 270.7 %all-gather.19.cloned.1.call-start = ((), (), s32[]{:S(2)}) async-start(), calls=%async_computation.14 | async-start | bytes 7864320 | tf_op jit(solution)/shard_map/all_gather | solution.py:439
  378.3 75.0 %all-to-all-start.6 = ((bf16[4,2,256,576]{2,3,1,0:T(8,128)(2,1)}), bf16[4,2,256,576]{2,3,1,0:T(8,128)(2,1)}, u32[]{:S(2)}, u32[]{:S(2)}) async-start(bf16[4,2,256,576]{2,3,1,0:T(8,128)(2,1)} %copy.109), calls=%async_computation.6 | async-start | bytes 4718592 | tf_op jit(solution)/shard_map/all_to_all | solution.py:473
  421.2 32.0 %copy-start.4 = (bf16[2,256,768]{2,1,0:T(8,128)(2,1)S(1)}, bf16[2,256,768]{2,1,0:T(8,128)(2,1)}, u32[]{:S(2)}) copy-start(bf16[2,256,768]{2,1,0:T(8,128)(2,1)} %param.13) | copy-start | bytes 2359300
  421.2 32.0 %copy-start.13 = (f32[768]{0:T(1024)S(1)}, f32[768]{0:T(1024)}, u32[]{:S(2)}) copy-start(f32[768]{0:T(1024)} %param.14) | copy-start | bytes 9220
  643.9 29.9 %copy-start.1 = (f32[32,12]{0,1:T(8,128)S(1)}, f32[32,12]{0,1:T(8,128)}, u32[]{:S(2)}) copy-start(f32[32,12]{0,1:T(8,128)} %param.19) | copy-start | bytes 4612
Sparse Core Ops, SparseCore 0:
  11.1 46.6 all-gather.12
  60.1 23.9 all-gather.10
  322.9 31.3 reduce-scatter.8
  370.2 29.7 reduce-scatter.6
  401.7 51.5 all-gather.14
  456.6 42.1 all-reduce.4
  500.9 70.7 all-gather.16
  573.7 70.1 all-gather.18

commit v2 on v1

v2 whole, which is shorter than its diff:
```python
import functools
import math

import jax
import jax.numpy as jnp
from jax import lax
from jax.experimental import pallas as pl
from jax.experimental.pallas import tpu as pltpu
from jax.sharding import PartitionSpec as P

f32 = jnp.float32
bf16 = jnp.bfloat16
LANES = 128
MIB = 1024 * 1024
BLOCK_ROWS = 256
FORWARD_TILE = 1024
GRAD_TILE = 384
norm_eps = 1e-06
ROOT_HALF = 1.0 / math.sqrt(2.0)
DENSITY = 1.0 / math.sqrt(2.0 * math.pi)
PARAMS = pltpu.CompilerParams(vmem_limit_bytes=52 * MIB)
SMEM = pl.BlockSpec(memory_space=pltpu.SMEM)


def nn(a, b):
    return jnp.dot(a, b, preferred_element_type=f32)


def nt(a, b):
    return lax.dot_general(a, b, (((1,), (1,)), ((), ())), preferred_element_type=f32)


def tn(a, b):
    return lax.dot_general(a, b, (((0,), (0,)), ((), ())), preferred_element_type=f32)


def whole(array):
    zeros = (0,) * array.ndim
    return pl.BlockSpec(array.shape, lambda *_: zeros)


def cost(flops, *arrays):
    return pl.CostEstimate(
        flops=int(flops),
        bytes_accessed=int(sum(math.prod(a.shape) * a.dtype.itemsize for a in arrays)),
        transcendentals=0,
    )


def shape(dims, kind):
    return jax.ShapeDtypeStruct(dims, kind)


def pack_rows(values):
    half = values.shape[0] // 2
    return jnp.concatenate([values[:half], values[half:]], axis=1)


def unpack_rows(packed):
    width = packed.shape[1] // 2
    return jnp.concatenate([packed[:, :width], packed[:, width:]], axis=0)


def inverse_norm(values):
    return lax.rsqrt(jnp.mean(values * values, axis=-1, keepdims=True) + norm_eps)


def norm_backward(values, gain, upstream):
    inverse = inverse_norm(values)
    scaled = upstream * gain
    inner = jnp.mean(scaled * values, axis=-1, keepdims=True)
    result = inverse * scaled - values * (inverse * inverse * inverse * inner)
    return result, jnp.sum(upstream * values * inverse, axis=0, keepdims=True)


def gelu_and_slope(v):
    cumulative = 0.5 * (1.0 + lax.erf(v * ROOT_HALF))
    return v * cumulative, cumulative + v * (jnp.exp(-0.5 * v * v) * DENSITY)


def attend_kernel(
    place_ref, rel_ref, own_ref, near_ref, far_ref, low_ref, high_ref, w_ref, bucket_ref,
    rows_ref, qkv_ref, att_ref, prob_ref, split, outs, toeplitz,
):
    head = pl.program_id(0)
    heads, length, head_dim = outs.shape
    width = heads * head_dim
    span = 2 * length
    piece = own_ref.shape[0]

    @pl.when(head == 0)
    def _():
        for number, ref in enumerate((own_ref, near_ref, far_ref)):
            at = pl.multiple_of(place_ref[number] * piece, piece)
            rows_ref[pl.ds(at, piece), :] = ref[...]
        at = pl.multiple_of(place_ref[3] * piece, piece)
        half = piece // 2
        rows_ref[pl.ds(at, half), :] = low_ref[...]
        rows_ref[pl.ds(pl.multiple_of(at + half, half), half), :] = high_ref[...]
        qkv = nn(rows_ref[...], w_ref[...]).astype(bf16)
        qkv_ref[...] = qkv
        for part in range(3):
            for each in range(heads):
                at = part * width + each * head_dim
                split[part, each] = qkv[:, at : at + head_dim]

    bucket_row = bucket_ref[...]
    row = jnp.zeros((1, span), f32)
    for bucket in range(rel_ref.shape[0]):
        row = jnp.where(bucket_row == bucket, rel_ref[bucket, head], row)
    toeplitz[...] = pltpu.roll(
        jnp.broadcast_to(row, (LANES, span)), span - LANES + 1, 1, stride=1, stride_axis=0
    )
    keys = split[1, head]
    values = split[2, head]
    for start in range(0, length, BLOCK_ROWS):
        scores = nt(split[0, head, start : start + BLOCK_ROWS], keys)
        parts = []
        for sub in range(0, BLOCK_ROWS, LANES):
            off = length - LANES - start - sub
            parts.append(scores[sub : sub + LANES] + toeplitz[:, off : off + length])
        scores = jnp.concatenate(parts, axis=0)
        peak = jnp.max(scores, axis=-1, keepdims=True)
        grown = jnp.exp(scores - peak)
        total = jnp.sum(grown, axis=-1, keepdims=True)
        prob = (grown * (1.0 / total)).astype(bf16)
        prob_ref[0, start : start + BLOCK_ROWS, :] = prob
        outs[head, start : start + BLOCK_ROWS, :] = nn(prob, values)

    @pl.when(head == heads - 1)
    def _():
        joined = jnp.concatenate([outs[each].astype(bf16) for each in range(heads)], axis=1)
        for number in range(length // piece):
            att_ref[number] = pack_rows(joined[number * piece : (number + 1) * piece])


def attend(place, pieces, weight, rel, bucket_row, heads):
    own, near, far, low, high = pieces
    piece, model = own.shape
    length = bucket_row.shape[1] // 2
    cols = weight.shape[1]
    width = cols // 3
    head_dim = width // heads
    out_shape = [
        shape((length, model), bf16),
        shape((length, cols), bf16),
        shape((length // piece, piece // 2, 2 * width), bf16),
        shape((heads, length, length), bf16),
    ]
    return pl.pallas_call(
        attend_kernel,
        grid=(heads,),
        in_specs=[SMEM, SMEM]
        + [whole(a) for a in (own, near, far, low, high, weight, bucket_row)],
        out_specs=[whole(a) for a in out_shape[:3]]
        + [pl.BlockSpec((1, length, length), lambda h: (h, 0, 0))],
        out_shape=out_shape,
        scratch_shapes=[
            pltpu.VMEM((3, heads, length, head_dim), bf16),
            pltpu.VMEM((heads, length, head_dim), f32),
            pltpu.VMEM((LANES, 2 * length), f32),
        ],
        compiler_params=PARAMS,
        cost_estimate=cost(2 * length * model * cols + 16 * heads * length * length * head_dim, *out_shape),
        name="attend",
    )(place, rel, own, near, far, low, high, weight, bucket_row)


def attend_back_kernel(
    qkv_ref, prob_ref, grad_ref, bucket_ref, out_ref, bias_ref, split, outs, acc, score_grads
):
    head = pl.program_id(0)
    heads, length, head_dim = outs.shape[1:]
    width = heads * head_dim
    span = 2 * length
    pieces, half, _ = grad_ref.shape
    piece = 2 * half

    @pl.when(head == 0)
    def _():
        bias_ref[...] = jnp.zeros_like(bias_ref)
        for part in range(3):
            for each in range(heads):
                at = part * width + each * head_dim
                split[part, each] = qkv_ref[:, at : at + head_dim]
        for number in range(pieces):
            grad = unpack_rows(grad_ref[number])
            for each in range(heads):
                split[3, each, number * piece : (number + 1) * piece, :] = grad[
                    :, each * head_dim : (each + 1) * head_dim
                ]

    acc[...] = jnp.zeros_like(acc)
    values = split[2, head]
    for start in range(0, length, BLOCK_ROWS):
        prob_grad = nt(split[3, head, start : start + BLOCK_ROWS], values)
        prob = prob_ref[0, start : start + BLOCK_ROWS, :].astype(f32)
        weighted = prob * prob_grad
        inner = jnp.sum(weighted, axis=-1, keepdims=True)
        score_grad = weighted - prob * inner
        score_grads[start : start + BLOCK_ROWS, :] = score_grad.astype(bf16)
        for sub in range(0, BLOCK_ROWS, LANES):
            off = length - LANES - start - sub
            acc[:, off : off + length] += score_grad[sub : sub + LANES]
    outs[0, head] = nn(score_grads[...], split[1, head])
    outs[1, head] = tn(score_grads[...], split[0, head])
    outs[2, head] = tn(prob_ref[0], split[3, head])

    part = acc[...]
    rows = LANES
    while rows > 8:
        rows //= 2
        part = part[:rows] + pltpu.roll(part[rows:], span - rows, 1)
    offsets = part[0:1]
    for row in range(1, 8):
        offsets = offsets + pltpu.roll(part[row : row + 1], span - row, 1)
    offsets = pltpu.roll(offsets, LANES - 1, 1)
    hot = lax.broadcasted_iota(jnp.int32, (bias_ref.shape[0], span), 0) == bucket_ref[...]
    total = jnp.sum(jnp.where(hot, offsets, 0.0), axis=1, keepdims=True)
    lane = lax.broadcasted_iota(jnp.int32, bias_ref.shape, 1)
    bias_ref[...] = jnp.where(lane == head, total, bias_ref[...])

    @pl.when(head == heads - 1)
    def _():
        joined = jnp.concatenate(
            [outs[part, each].astype(bf16) for part in range(3) for each in range(heads)], axis=1
        )
        for number in range(pieces):
            out_ref[number] = pack_rows(joined[number * piece : (number + 1) * piece])


def attend_back(qkv, prob, grad, bucket_row, bucket_count):
    length, cols = qkv.shape
    heads = prob.shape[0]
    head_dim = cols // (3 * heads)
    pieces, half, _ = grad.shape
    out_shape = [shape((pieces, half, 2 * cols), bf16), shape((bucket_count, LANES), f32)]
    return pl.pallas_call(
        attend_back_kernel,
        grid=(heads,),
        in_specs=[
            whole(qkv),
            pl.BlockSpec((1, length, length), lambda h: (h, 0, 0)),
            whole(grad),
            whole(bucket_row),
        ],
        out_specs=[whole(a) for a in out_shape],
        out_shape=out_shape,
        scratch_shapes=[
            pltpu.VMEM((4, heads, length, head_dim), bf16),
            pltpu.VMEM((3, heads, length, head_dim), f32),
            pltpu.VMEM((LANES, 2 * length), f32),
            pltpu.VMEM((length, length), bf16),
        ],
        compiler_params=PARAMS,
        cost_estimate=cost(40 * heads * length * length * head_dim, qkv, prob, grad),
        name="attend_back",
    )(qkv, prob, grad, bucket_row)


def project_kernel(
    x_ref, dy_ref, id_ref, target_ref, gain_ref, dense_ref, *refs
):
    att_refs, (middle_ref, second_ref, flat_ref, prob_ref, sent_ref, grad_ref) = refs[:-6], refs[-6:]
    model = x_ref.shape[1]
    flats = []
    for ref in att_refs:
        flats.append(
            jnp.concatenate([unpack_rows(ref[g]) for g in range(ref.shape[0])], axis=1)
        )
    flat = jnp.concatenate(flats, axis=0)
    flat_ref[...] = flat
    middle = x_ref[...].astype(f32) + nn(flat, dense_ref[:, :model])
    middle_ref[...] = middle
    second = (middle * inverse_norm(middle) * gain_ref[...]).astype(bf16)
    second_ref[...] = second
    positions = sent_ref.shape[0]
    hot = (
        lax.broadcasted_iota(jnp.int32, (positions, x_ref.shape[0]), 0) == target_ref[...]
    ).astype(bf16)
    sent_ref[...] = nn(hot, second).astype(bf16)
    logits = nn(second, dense_ref[:, model:])
    peak = jnp.max(logits, axis=-1, keepdims=True)
    grown = jnp.exp(logits - peak)
    probs = grown / jnp.sum(grown, axis=-1, keepdims=True)
    prob_ref[...] = probs
    chosen = lax.broadcasted_iota(jnp.int32, probs.shape, 1) == id_ref[...]
    gate = jnp.sum(jnp.where(chosen, probs, 0.0), axis=-1, keepdims=True)
    out_grad = (gate * dy_ref[...].astype(f32)).astype(bf16)
    grad_ref[...] = nn(hot, out_grad).astype(bf16)


def project(x, dy, id_column, target_row, gain, dense, attended, positions):
    tokens, model = x.shape
    experts = dense.shape[1] - model
    out_shape = [
        shape((tokens, model), f32),
        shape((tokens, model), bf16),
        shape((tokens, model), bf16),
        shape((tokens, experts), f32),
        shape((positions, model), bf16),
        shape((positions, model), bf16),
    ]
    operands = (x, dy, id_column, target_row, gain, dense, *attended)
    return pl.pallas_call(
        project_kernel,
        in_specs=[whole(a) for a in operands],
        out_specs=[whole(a) for a in out_shape],
        out_shape=out_shape,
        compiler_params=PARAMS,
        cost_estimate=cost(2 * tokens * model * (model + 2 * positions), *out_shape),
        name="project",
    )(*operands)


def returned_kernel(
    back_ref, target_ref, id_ref, middle_ref, dy_ref, prob_ref, second_ref,
    out_ref, logit_ref, router_ref,
):
    tokens = middle_ref.shape[0]
    hot = (
        lax.broadcasted_iota(jnp.int32, (tokens, back_ref.shape[0]), 1) == target_ref[...]
    ).astype(bf16)
    token_out = nn(hot, back_ref[...])
    probs = prob_ref[...]
    chosen = lax.broadcasted_iota(jnp.int32, probs.shape, 1) == id_ref[...]
    gate = jnp.sum(jnp.where(chosen, probs, 0.0), axis=-1, keepdims=True)
    out_ref[...] = (middle_ref[...] + gate * token_out).astype(bf16)
    gate_grad = jnp.sum(dy_ref[...].astype(f32) * token_out, axis=-1, keepdims=True)
    picked = jnp.where(chosen, gate_grad, 0.0)
    logit_grad = probs * (picked - jnp.sum(probs * picked, axis=-1, keepdims=True))
    logit_low = logit_grad.astype(bf16)
    logit_ref[...] = logit_low
    router_ref[...] = tn(second_ref[...], logit_low).astype(bf16)


def returned(back, target_column, id_column, middle, dy, probs, second):
    tokens, model = middle.shape
    experts = probs.shape[1]
    out_shape = [
        shape((tokens, model), bf16),
        shape((tokens, experts), bf16),
        shape((model, experts), bf16),
    ]
    operands = (back, target_column, id_column, middle, dy, probs, second)
    return pl.pallas_call(
        returned_kernel,
        in_specs=[whole(a) for a in operands],
        out_specs=[whole(a) for a in out_shape],
        out_shape=out_shape,
        compiler_params=PARAMS,
        cost_estimate=cost(2 * tokens * model * back.shape[0], *out_shape, middle, back),
        name="returned",
    )(*operands)


def branch_kernel(
    back_ref, target_ref, logit_ref, dense_ref, middle_ref, gain_ref, dy_ref,
    middle_grad_ref, branch_ref, grad_ref, gain_grad_ref,
):
    tokens, model = middle_ref.shape
    hot = (
        lax.broadcasted_iota(jnp.int32, (tokens, back_ref.shape[0]), 1) == target_ref[...]
    ).astype(bf16)
    second_grad = nn(hot, back_ref[...]) + nt(logit_ref[...], dense_ref[:, model:])
    norm_grad, gain_grad = norm_backward(middle_ref[...], gain_ref[...], second_grad)
    gain_grad_ref[...] = gain_grad
    middle_grad = dy_ref[...].astype(f32) + norm_grad
    middle_grad_ref[...] = middle_grad
    branch = middle_grad.astype(bf16)
    branch_ref[...] = branch
    grad = nt(branch, dense_ref[:, :model]).astype(bf16)
    groups = grad_ref.shape[0]
    width = model // groups
    for group in range(groups):
        grad_ref[group] = pack_rows(grad[:, group * width : (group + 1) * width])


def branch_back(back, target_column, logit, dense, middle, gain, dy, number, seqs, groups):
    tokens, model = middle.shape
    piece = tokens // seqs

    def rows_of(array):
        return pl.BlockSpec((piece, array.shape[1]), lambda _: (number, 0))

    out_shape = [
        shape((piece, model), f32),
        shape((piece, model), bf16),
        shape((groups, piece // 2, 2 * model // groups), bf16),
        shape((1, model), f32),
    ]
    return pl.pallas_call(
        branch_kernel,
        grid=(1,),
        in_specs=[
            whole(back), rows_of(target_column), rows_of(logit), whole(dense), rows_of(middle),
            whole(gain), rows_of(dy),
        ],
        out_specs=[whole(a) for a in out_shape],
        out_shape=out_shape,
        compiler_params=PARAMS,
        cost_estimate=cost(2 * piece * model * (back.shape[0] + model), *out_shape, back, dense),
        name="branch_back",
    )(back, target_column, logit, dense, middle, gain, dy)


def input_kernel(grad_ref, weight_ref, x_ref, gain_ref, middle_grad_ref, *refs):
    out_ref, gain_grad_ref = refs[-2:]
    total = None
    for group in range(weight_ref.shape[0]):
        part = nt(unpack_rows(grad_ref[group]), weight_ref[group])
        total = part if total is None else total + part
    norm_grad, gain_grad = norm_backward(x_ref[0].astype(f32), gain_ref[...], total)
    out_ref[0] = middle_grad_ref[...] + norm_grad
    gain_grad_ref[...] = gain_grad


def input_back(grad, weights, x, gain, middle_grad, number, earlier):
    seqs, piece, model = x.shape
    row_spec = pl.BlockSpec((1, piece, model), lambda _: (number, 0, 0))
    out_shape = [shape(x.shape, f32), shape((1, model), f32)]
    operands = [grad, weights, x, gain, middle_grad]
    specs = [whole(grad), whole(weights), row_spec, whole(gain), whole(middle_grad)]
    aliases = {}
    if earlier is not None:
        aliases = {len(operands): 0}
        operands.append(earlier)
        specs.append(pl.BlockSpec(memory_space=pl.ANY))
    return pl.pallas_call(
        input_kernel,
        grid=(1,),
        in_specs=specs,
        out_specs=[row_spec, whole(out_shape[1])],
        out_shape=out_shape,
        input_output_aliases=aliases,
        compiler_params=PARAMS,
        cost_estimate=cost(2 * piece * math.prod(weights.shape), grad, weights, middle_grad),
        name="input_back",
    )(*operands)


def expert_kernel(x_ref, win_ref, wout_ref, y_ref, slope_ref, acc):
    tile = pl.program_id(1)
    rows = acc.shape[0]
    x = x_ref[...].reshape(rows, x_ref.shape[-1])
    pre = jnp.dot(x, win_ref[0], preferred_element_type=f32)
    hidden, slope = gelu_and_slope(pre)
    slope_ref[0] = slope.astype(bf16)
    part = jnp.dot(hidden.astype(bf16), wout_ref[0], preferred_element_type=f32)

    @pl.when(tile == 0)
    def _():
        acc[...] = part

    @pl.when(tile > 0)
    def _():
        acc[...] += part

    @pl.when(tile == pl.num_programs(1) - 1)
    def _():
        y_ref[...] = acc[...].astype(bf16).reshape(y_ref.shape)


def expert_forward(x, w_in, w_out, tile):
    sources, experts, slots, model = x.shape
    hidden = w_in.shape[2]
    rows = sources * slots
    row_spec = pl.BlockSpec((sources, 1, slots, model), lambda e, f: (0, e, 0, 0))
    return pl.pallas_call(
        expert_kernel,
        grid=(experts, hidden // tile),
        in_specs=[
            row_spec,
            pl.BlockSpec((1, model, tile), lambda e, f: (e, 0, f)),
            pl.BlockSpec((1, tile, model), lambda e, f: (e, f, 0)),
        ],
        out_specs=[row_spec, pl.BlockSpec((1, rows, tile), lambda e, f: (e, 0, f))],
        out_shape=[
            jax.ShapeDtypeStruct(x.shape, bf16),
            jax.ShapeDtypeStruct((experts, rows, hidden), bf16),
        ],
        scratch_shapes=[pltpu.VMEM((rows, model), f32)],
        compiler_params=pltpu.CompilerParams(vmem_limit_bytes=52 * MIB),
        name="expert_forward",
    )(x, w_in, w_out)


def expert_back_kernel(g_ref, win_ref, wout_ref, slope_ref, y_ref, acc):
    tile = pl.program_id(1)
    rows = acc.shape[0]
    g = g_ref[...].reshape(rows, g_ref.shape[-1])
    pre_grad = (nt(g, wout_ref[0]) * slope_ref[0].astype(f32)).astype(bf16)
    part = nt(pre_grad, win_ref[0])

    @pl.when(tile == 0)
    def _():
        acc[...] = part

    @pl.when(tile > 0)
    def _():
        acc[...] += part

    @pl.when(tile == pl.num_programs(1) - 1)
    def _():
        y_ref[...] = acc[...].astype(bf16).reshape(y_ref.shape)


def expert_backward(g, w_in, w_out, slope, tile):
    sources, experts, slots, model = g.shape
    hidden = w_in.shape[2]
    rows = sources * slots
    row_spec = pl.BlockSpec((sources, 1, slots, model), lambda e, f: (0, e, 0, 0))
    return pl.pallas_call(
        expert_back_kernel,
        grid=(experts, hidden // tile),
        in_specs=[
            row_spec,
            pl.BlockSpec((1, model, tile), lambda e, f: (e, 0, f)),
            pl.BlockSpec((1, tile, model), lambda e, f: (e, f, 0)),
            pl.BlockSpec((1, rows, tile), lambda e, f: (e, 0, f)),
        ],
        out_specs=row_spec,
        out_shape=jax.ShapeDtypeStruct(g.shape, bf16),
        scratch_shapes=[pltpu.VMEM((rows, model), f32)],
        compiler_params=pltpu.CompilerParams(vmem_limit_bytes=52 * MIB),
        name="expert_backward",
    )(g, w_in, w_out, slope)


def weight_grad_kernel(place_ref, *refs):
    pieces = (len(refs) - 4) // 2
    x_refs, g_refs = refs[:pieces], refs[pieces : 2 * pieces]
    win_ref, wout_ref = refs[2 * pieces : 2 * pieces + 2]
    gin_ref, gout_ref = refs[-2:]
    gin = gout = None
    for x_ref, g_ref in zip(x_refs, g_refs):
        rows = x_ref.shape[0] * x_ref.shape[2]
        x = x_ref[...].reshape(rows, x_ref.shape[-1])
        g = g_ref[...].reshape(rows, g_ref.shape[-1])
        hidden, slope = gelu_and_slope(nn(x, win_ref[0]))
        pre_grad = (nt(g, wout_ref[0]) * slope).astype(bf16)
        gin_part = tn(x, pre_grad)
        gout_part = tn(hidden.astype(bf16), g)
        gin = gin_part if gin is None else gin + gin_part
        gout = gout_part if gout is None else gout + gout_part
    gin_ref[0] = gin
    gout_ref[0] = gout


def weight_grads(place, xs, gs, w_in, w_out, ways):
    experts, model, hidden = w_in.shape
    cols = hidden // ways
    tile = GRAD_TILE if cols % GRAD_TILE == 0 else cols
    tiles = cols // tile

    def rows_of(array):
        sources, _, slots, _ = array.shape
        return pl.BlockSpec((sources, 1, slots, model), lambda e, t, q: (0, e, 0, 0))

    out_shape = [shape((experts, model, cols), f32), shape((experts, cols, model), f32)]
    flops = 8 * sum(math.prod(a.shape) for a in xs) * cols
    return pl.pallas_call(
        weight_grad_kernel,
        grid_spec=pltpu.PrefetchScalarGridSpec(
            num_scalar_prefetch=1,
            grid=(experts, tiles),
            in_specs=[rows_of(a) for a in (*xs, *gs)]
            + [
                pl.BlockSpec((1, model, tile), lambda e, t, q: (e, 0, q[0] * tiles + t)),
                pl.BlockSpec((1, tile, model), lambda e, t, q: (e, q[0] * tiles + t, 0)),
            ],
            out_specs=[
                pl.BlockSpec((1, model, tile), lambda e, t, q: (e, 0, t)),
                pl.BlockSpec((1, tile, model), lambda e, t, q: (e, t, 0)),
            ],
        ),
        out_shape=out_shape,
        compiler_params=PARAMS,
        cost_estimate=cost(2 * flops, *out_shape, *xs, *gs),
        name="weight_grads",
    )(place, *xs, *gs, w_in, w_out)


def partners(ways, step):
    return [(index, index ^ step) for index in range(ways)]


def swap(value, axis, step):
    return lax.ppermute(value, axis, partners(lax.axis_size(axis), step))


def gather_near(value):
    return swap(value, "seq", 1), swap(value, "seq", 2)


def gather_far(near, far):
    half = near.shape[0] // 2
    return swap(near[:half], "seq", 2), swap(far[half:], "seq", 1)


def sum_all(value):
    for axis in ("seq", "shard"):
        ways = lax.axis_size(axis)
        if ways <= 8:
            got = [swap(value, axis, step) for step in range(1, ways)]
            value = functools.reduce(jnp.add, [value] + got)
        else:
            value = lax.psum(value, axis)
    return value


def scatter_rows(value):
    ways = lax.axis_size("shard")
    rows, cols = value.shape
    parts = lax.all_to_all(value.reshape(ways, rows // ways, cols), "shard", 0, 0, tiled=True)
    return jnp.sum(parts.astype(f32), axis=0)


def body(
    block_input,
    gain_attn,
    gain_ffn,
    w_qkv,
    w_out,
    w_router,
    rel_bias,
    w_in,
    w_exp_out,
    expert_id,
    capacity_slot,
    buckets,
    output_grad,
):
    seqs, piece, model = block_input.shape
    seq_ways = lax.axis_size("seq")
    shard_ways = lax.axis_size("shard")
    bucket_count, heads_all = rel_bias.shape
    heads = heads_all // seq_ways
    width = model // seq_ways
    length = piece * seq_ways
    experts = w_router.shape[1]
    tokens = seqs * piece
    capacity = 2 * tokens // experts
    positions = experts * capacity
    slot_shape = (shard_ways, experts // shard_ways, capacity, model)
    weight_rows = w_qkv.shape[0]
    seq_index = lax.axis_index("seq").astype(jnp.int32)
    places = jnp.stack([seq_index ^ step for step in range(seq_ways)])
    gain_one_row = gain_attn.reshape(1, model)
    gain_two_row = gain_ffn.reshape(1, model)
    bucket_row = jnp.pad(
        buckets, (0, 2 * length - buckets.shape[0]), constant_values=-1
    ).reshape(1, 2 * length)
    target = jnp.where(capacity_slot < capacity, expert_id * capacity + capacity_slot, -1)
    target_row = target.reshape(1, tokens)
    target_column = target.reshape(tokens, 1)
    id_column = expert_id.reshape(tokens, 1)
    upstream = output_grad.reshape(tokens, model)

    own_columns = lax.dynamic_slice_in_dim(
        w_qkv.reshape(weight_rows, 3, model), seq_index * width, width, 2
    ).reshape(weight_rows, 3 * width)
    head_weight = lax.all_gather(own_columns, "shard", axis=0, tiled=True)
    dense = lax.all_gather(
        jnp.concatenate([w_out, w_router], axis=1), "shard", axis=0, tiled=True
    )
    inputs = block_input.astype(f32)
    normed = (inputs * inverse_norm(inputs) * gain_attn).astype(bf16)
    bias_dev = lax.dynamic_slice_in_dim(rel_bias, seq_index * heads, heads, 1)

    first_near = gather_near(normed[0])
    held = lax.optimization_barrier((normed[1], first_near))
    first_near = held[1]
    second_near = gather_near(held[0])
    first_far = gather_far(*first_near)
    second_far = gather_far(*second_near)
    sequence_pieces = (
        (normed[0], *first_near, *first_far),
        (normed[1], *second_near, *second_far),
    )
    kept, attended_tok = [], []
    for pieces in sequence_pieces:
        rows, qkv, attended, probs = attend(
            places, pieces, head_weight, bias_dev, bucket_row, heads
        )
        kept.append((rows, qkv, probs))
        attended_tok.append(lax.all_to_all(attended, "seq", 0, 0, tiled=True))

    middle, second, attended_flat, router_probs, sent, sent_grad = project(
        block_input.reshape(tokens, model),
        upstream,
        id_column,
        target_row,
        gain_two_row,
        dense,
        attended_tok,
        positions,
    )

    def exchange(rows):
        return lax.all_to_all(rows, "shard", 0, 0, tiled=True)

    held_weight, sent = lax.optimization_barrier((head_weight, sent))
    weight_groups = lax.all_gather(held_weight, "seq")
    arrived = exchange(sent.reshape(slot_shape))
    out_arrived = exchange(sent_grad.reshape(slot_shape))
    expert_out, slope = expert_forward(arrived, w_in, w_exp_out, FORWARD_TILE)
    back_out = exchange(expert_out).reshape(positions, model)
    rows_grad = expert_backward(out_arrived, w_in, w_exp_out, slope, FORWARD_TILE)
    back_grad = exchange(rows_grad).reshape(positions, model)
    arrived_near = gather_near(arrived)
    arrived_far = gather_far(*arrived_near)
    out_near = gather_near(out_arrived)
    out_far = gather_far(*out_near)

    block_output, logit_low, grad_router = returned(
        back_out, target_column, id_column, middle, upstream, router_probs, second
    )
    back_grad, arrived_near, arrived_far, weight_groups = lax.optimization_barrier(
        (back_grad, arrived_near, arrived_far, weight_groups)
    )
    middle_grads, branches, grad_heads, gain_two = [], [], [], []
    for number in range(seqs):
        middle_grad, branch, attended_grad, gain_part = branch_back(
            back_grad, target_column, logit_low, dense, middle, gain_two_row, upstream,
            number, seqs, seq_ways,
        )
        middle_grads.append(middle_grad)
        branches.append(branch)
        gain_two.append(gain_part)
        grad_heads.append(lax.all_to_all(attended_grad, "seq", 0, 0, tiled=True))
    grad_out = sum(
        tn(attended_flat[number * piece : (number + 1) * piece], branches[number])
        for number in range(seqs)
    )
    grad_dense = jnp.concatenate([grad_out.astype(bf16), grad_router], axis=1)
    grad_dense = scatter_rows(grad_dense)
    for step in (1, 2):
        grad_dense = grad_dense + swap(grad_dense, "seq", step)

    qkv_grads, bias_parts, grad_tok = [], [], []
    for number in range(seqs):
        _, qkv, probs = kept[number]
        grad = grad_heads[number]
        if number == seqs - 1:
            grad, out_near, out_far = lax.optimization_barrier((grad, out_near, out_far))
        qkv_grad, bias_part = attend_back(qkv, probs, grad, bucket_row, bucket_count)
        qkv_grads.append(qkv_grad)
        bias_parts.append(bias_part)
        grad_tok.append(lax.all_to_all(qkv_grad, "seq", 0, 0, tiled=True))
    out_arrived, _ = lax.optimization_barrier((out_arrived, qkv_grads[-1]))
    grad_in_part, grad_exp_part = weight_grads(
        places,
        (arrived, *arrived_near, *arrived_far),
        (out_arrived, *out_near, *out_far),
        w_in,
        w_exp_out,
        seq_ways,
    )
    columns = None
    for number in range(seqs):
        packed = qkv_grads[number]
        cols = packed.shape[2] // 2
        rows = kept[number][0].reshape(seq_ways, 2, piece // 2, model)
        flat = packed.reshape(seq_ways, piece // 2, 2, cols)
        part = jnp.einsum("phrd,prhe->de", rows, flat, preferred_element_type=f32)
        columns = part if columns is None else columns + part
    columns = scatter_rows(columns.astype(bf16)).astype(bf16)
    grad_qkv = lax.all_gather(columns, "seq")
    grad_qkv = (
        grad_qkv.reshape(seq_ways, weight_rows, 3, width)
        .transpose(1, 2, 0, 3)
        .reshape(weight_rows, 3 * model)
        .astype(f32)
    )
    input_grad, gain_one = None, []
    for number in range(seqs):
        input_grad, gain_part = input_back(
            grad_tok[number], weight_groups, block_input, gain_one_row, middle_grads[number],
            number, input_grad,
        )
        gain_one.append(gain_part)
    bias_grad = lax.dynamic_update_slice_in_dim(
        jnp.zeros((bucket_count, heads_all), f32),
        functools.reduce(jnp.add, bias_parts)[:, :heads],
        seq_index * heads,
        1,
    )
    early = jnp.concatenate([bias_grad.reshape(-1), sum(gain_two).reshape(-1)])
    early = sum_all(early.reshape(-1, LANES)).reshape(-1)
    gain_one = sum_all(sum(gain_one).reshape(-1, LANES)).reshape(-1)
    return (
        block_output.reshape(block_input.shape),
        input_grad,
        gain_one,
        early[bucket_count * heads_all :],
        grad_qkv,
        grad_dense[:, :model],
        grad_dense[:, model:],
        early[: bucket_count * heads_all].reshape(bucket_count, heads_all),
        grad_in_part,
        grad_exp_part,
    )


def solution(mesh):
    placed = (
        P("shard", "seq", None),
        P(),
        P(),
        P("shard", None),
        P("shard", None),
        P("shard", None),
        P(),
        P("shard", None, None),
        P("shard", None, None),
        P("shard", "seq"),
        P("shard", "seq"),
        P(),
        P("shard", "seq", None),
    )
    return jax.shard_map(
        body,
        mesh=mesh,
        in_specs=placed,
        out_specs=(
            P("shard", "seq", None),
            P("shard", "seq", None),
            P(),
            P(),
            P("shard", None),
            P("shard", None),
            P("shard", None),
            P(),
            P("shard", None, "seq"),
            P("shard", "seq", None),
        ),
        check_vma=False,
    )
```

time: 695 us -> 563 us (0.81)
  waiting for transfers between devices: 295 us -> 169 us
  blocking collectives: 173 us -> 76.9 us
  starting transfers between devices: 17.4 us -> 93.7 us
  Pallas kernels: 112 us -> 152 us
  matrix products: 29.9 us -> 10.1 us
    all_gather x4 -> x1, waiting for transfers between devices: 194 us -> 0.01 us  [body(): weight_groups = lax.all_gather(held_weight, 'seq')]
    ppermute x0 -> x38, waiting for transfers between devices: none -> 97.9 us  [swap(): return lax.ppermute(value, axis, partners(lax.axis_size(axis), step))]
    all_to_all x3 -> x1, blocking collectives: 97.3 us -> 42.1 us  [exchange(): return lax.all_to_all(rows, 'shard', 0, 0, tiled=True)]
    ppermute x0 -> x38, starting transfers between devices: none -> 47.1 us  [swap(): return lax.ppermute(value, axis, partners(lax.axis_size(axis), step))]
    pallas_call x3 -> x11, Pallas kernels: 78 us -> 118 us  [the longest x1 33 us: weight_grads(): pl.pallas_call(weight_grad_kernel, grid_spec=pltpu.PrefetchScalarGridSpec...]
    psum x1 -> x0, blocking collectives: 39.8 us -> none  [body(): lax.psum((bias_grad, grad_gain_one), ('seq', 'shard'))]
    all_to_all x4 -> x11, starting transfers between devices: 17 us -> 46.6 us  [the longest x3 11.4 us: exchange(): return lax.all_to_all(rows, 'shard', 0, 0, tiled=True)]
    dot_general x12 -> x4, matrix products: 29.9 us -> 10.1 us  [the longest x2 5.14 us: tn(): lax.dot_general(a, b, (((0,), (0,)), ((), ())), preferred_element_type=f32)]
  transfers between devices with their start and end apart: 12 -> 51, of which waited for: 8 -> 15; matrix products, arithmetic and copies ran while one was open for 6% -> 7% of each run, Pallas kernels for 7% -> 23%
where the time goes in v2:
time: 563 us; the launch traced here: 555 us
  waiting for transfers between devices  169 us (30%)
  Pallas kernels  152 us (27%)
  starting transfers between devices  93.7 us (17%)
  blocking collectives  76.9 us (14%)
  local copies, waits for them, and re-layouts  28.6 us (5%)
  between operations  15 us (3%)
  matrix products  10.1 us (2%)
  other arithmetic  9.42 us (2%)
    ppermute x38, waiting for transfers between devices, swap(): return lax.ppermute(value, axis, partners(lax.axis_size(axis), step))  97.9 us
    all_to_all x3, waiting for transfers between devices, exchange(): return lax.all_to_all(rows, 'shard', 0, 0, tiled=True)  57.2 us
    ppermute x38, starting transfers between devices, swap(): return lax.ppermute(value, axis, partners(lax.axis_size(axis), step))  47.1 us
    all_to_all x1, blocking collectives, exchange(): return lax.all_to_all(rows, 'shard', 0, 0, tiled=True)  42.1 us
    pallas_call x1, Pallas kernels, weight_grads(): pl.pallas_call(weight_grad_kernel, grid_spec=pltpu.PrefetchScalarGridSpec...  33 us
    pallas_call x2, Pallas kernels, attend(): pl.pallas_call(attend_kernel, grid=(heads,), in_specs=[SMEM, SMEM] + [who...  27.8 us
    pallas_call x2, Pallas kernels, attend_back(): pl.pallas_call(attend_back_kernel, grid=(heads,), in_specs=[whole(qkv), p...  27.4 us
    all_gather x1, blocking collectives, body(): head_weight = lax.all_gather(own_columns, 'shard', axis=0, tiled=True)  20.3 us
  transfers between devices with their start and end apart: 51, of which 15 were waited for; matrix products, arithmetic and copies ran while one was open for 7% of the time, Pallas kernels for 23%

profile of v2, /device:TPU:0, one launch (start us, length us, event | category | flops | bytes accessed | tf_op | source)
XLA Modules:
  0.0 554.6 jit_solution(6770371719685757246)
XLA Ops:
  17.5 6.8 %collective-permute-done.near_ref = bf16[256,768]{1,0:T(8,128)(2,1)S(1)} collective-permute-done((bf16[256,768]{1,0:T(8,128)(2,1)S(1)}, bf16[256,768]{1,0:T(8,128)(2,1)S(1)}, u32[]{:S(2)}, u32[]{:S(2)}) %collective-permute-start) | collective-permute-done | bytes 393248 | tf_op jit(solution)/shard_map/ppermute | solution.py:589
  27.8 20.3 %all_gather.18.w_ref = bf16[768,576]{1,0:T(8,128)(2,1)} all-gather(bf16[96,576]{1,0:T(8,128)(2,1)S(1)} %copy.96), channel_id=1, replica_groups=mesh['seq'=4,'shard'=8] {'shard'}, dimensions={0}, use_global_device_ids=true | all-gather | bytes 995328 | tf_op jit(solution)/shard_map/all_gather | solution.py:663
  56.5 13.8 %attend.2 = (bf16[1024,768]{1,0:T(8,128)(2,1)}, bf16[1024,576]{1,0:T(8,128)(2,1)}, bf16[4,128,384]{2,1,0:T(8,128)(2,1)}, bf16[3,1024,1024]{2,1,0:T(8,128)(2,1)}) custom-call(s32[4]{0:T(128)S(1)} %pad_add_fusion.place_ref, f32[32,3]{1,0:T(8,128)S(1)} %copy.119.rel_ref, bf16[256,768]{1,0:T(8,128)(2,1)S(1)} %get-tuple-element.169.own_ref, ...), custom_call_target="tpu_custom_call" | custom-call | flops 4127195136 | bytes 9437184 | tf_op jit(solution)/shard_map/attend/pallas_call | solution.py:150
  70.3 4.6 all-to-all-start
  74.9 14.0 %attend.3 = (bf16[1024,768]{1,0:T(8,128)(2,1)}, bf16[1024,576]{1,0:T(8,128)(2,1)}, bf16[4,128,384]{2,1,0:T(8,128)(2,1)}, bf16[3,1024,1024]{2,1,0:T(8,128)(2,1)}) custom-call(s32[4]{0:T(128)S(1)} %pad_add_fusion.place_ref, f32[32,3]{1,0:T(8,128)S(1)} %copy.119.rel_ref, bf16[256,768]{1,0:T(8,128)(2,1)S(1)} %get-tuple-element.67.own_ref, ...), custom_call_target="tpu_custom_call" | custom-call | flops 4127195136 | bytes 9437184 | tf_op jit(solution)/shard_map/attend/pallas_call | solution.py:150
  88.9 4.6 all-to-all-start.1
  93.8 5.6 %all-to-all-done.1.refs_1_ = bf16[4,128,384]{2,1,0:T(8,128)(2,1)S(1)} async-done(((bf16[4,128,384]{2,1,0:T(8,128)(2,1)}), bf16[4,128,384]{2,1,0:T(8,128)(2,1)S(1)}, u32[]{:S(2)}, u32[]{:S(2)}) %all-to-all-start.1) | async-done | bytes 393248 | tf_op jit(solution)/shard_map/all_to_all | solution.py:687
  99.4 6.8 %project.1 = (f32[512,768]{1,0:T(8,128)}, bf16[512,768]{1,0:T(8,128)(2,1)}, bf16[512,768]{1,0:T(8,128)(2,1)}, f32[512,16]{1,0:T(8,128)S(1)}, bf16[1024,768]{1,0:T(8,128)(2,1)}, /*index=5*/bf16[1024,768]{1,0:T(8,128)(2,1)}) custom-call(bf16[512,768]{1,0:T(8,128)(2,1)} %bitcast.61, bf16[512,768]{1,0:T(8,128)(2,1)} %bitcast.62, s32[512,1]{1,0:T(8,128)S(1)} %bitcast.69, ...), custom_call_target="tpu_custom_call" | custom-call | flops 2214592512 | bytes 6324224 | tf_op jit(solution)/shard_map/project/pallas_call | solution.py:305
  106.2 42.1 %all_to_all.60.x_ref.refs_0_ = bf16[8,2,64,768]{3,2,1,0:T(8,128)(2,1)} all-to-all(bf16[8,2,64,768]{3,2,1,0:T(8,128)(2,1)} %bitcast.84), channel_id=1, replica_groups=mesh['seq'=4,'shard'=8] {'shard'}, dimensions={0} | all-to-all | bytes 3145728 | tf_op jit(solution)/shard_map/all_to_all | solution.py:701
  151.9 17.6 %expert_forward.1 = (bf16[8,2,64,768]{3,2,1,0:T(8,128)(2,1)}, bf16[2,512,3072]{2,1,0:T(8,128)(2,1)}) custom-call(bf16[8,2,64,768]{3,2,1,0:T(8,128)(2,1)} %all_to_all.60.x_ref.refs_0_, bf16[2,768,3072]{2,1,0:T(8,128)(2,1)} %refs_10_.1, bf16[2,3072,768]{2,1,0:T(8,128)(2,1)} %refs_11_.1), custom_call_target="tpu_custom_call" | custom-call | tf_op jit(solution)/shard_map/expert_forward/pallas_call | solution.py:469
  169.5 20.2 %all-to-all-done.4.g_ref.refs_5_ = bf16[8,2,64,768]{3,2,1,0:T(8,128)(2,1)S(1)} async-done(((bf16[8,2,64,768]{3,2,1,0:T(8,128)(2,1)}), bf16[8,2,64,768]{3,2,1,0:T(8,128)(2,1)S(1)}, u32[]{:S(2)}, u32[]{:S(2)}) %all-to-all-start.4) | async-done | bytes 1572896 | tf_op jit(solution)/shard_map/all_to_all | solution.py:701
  190.8 16.6 %expert_backward.1 = bf16[8,2,64,768]{3,2,1,0:T(8,128)(2,1)} custom-call(bf16[8,2,64,768]{3,2,1,0:T(8,128)(2,1)} %copy-done.11, bf16[2,768,3072]{2,1,0:T(8,128)(2,1)} %refs_10_.1, bf16[2,3072,768]{2,1,0:T(8,128)(2,1)} %refs_11_.1, bf16[2,512,3072]{2,1,0:T(8,128)(2,1)} %get-tuple-element.79.slope_ref), custom_call_target="tpu_custom_call" | custom-call | tf_op jit(solution)/shard_map/expert_backward/pallas_call | solution.py:513
  211.8 37.0 %all-to-all-done.5 = bf16[8,2,64,768]{3,2,1,0:T(8,128)(2,1)S(1)} async-done(((bf16[8,2,64,768]{3,2,1,0:T(8,128)(2,1)}), bf16[8,2,64,768]{3,2,1,0:T(8,128)(2,1)S(1)}, u32[]{:S(2)}, u32[]{:S(2)}) %all-to-all-start.5) | async-done | bytes 1572896 | tf_op jit(solution)/shard_map/all_to_all | solution.py:701
  250.0 4.3 all-to-all-start.3
  258.4 39.9 %collective-permute-done.8.refs_1_ = bf16[8,2,64,768]{3,2,1,0:T(8,128)(2,1)S(1)} collective-permute-done((bf16[8,2,64,768]{3,2,1,0:T(8,128)(2,1)}, bf16[8,2,64,768]{3,2,1,0:T(8,128)(2,1)S(1)}, u32[]{:S(2)}, u32[]{:S(2)}) %collective-permute-start.8) | collective-permute-done | bytes 1572896 | tf_op jit(solution)/shard_map/ppermute | solution.py:589
  302.4 29.6 %collective-permute-done.12.refs_6_ = bf16[8,2,64,768]{3,2,1,0:T(8,128)(2,1)S(1)} collective-permute-done((bf16[8,2,64,768]{3,2,1,0:T(8,128)(2,1)}, bf16[8,2,64,768]{3,2,1,0:T(8,128)(2,1)S(1)}, u32[]{:S(2)}, u32[]{:S(2)}) %collective-permute-start.12) | collective-permute-done | bytes 1572896 | tf_op jit(solution)/shard_map/ppermute | solution.py:589
  336.7 12.3 %collective-permute-done.10.refs_3_ = bf16[4,2,64,768]{3,2,1,0:T(8,128)(2,1)S(1)} collective-permute-done((bf16[4,2,64,768]{3,2,1,0:T(8,128)(2,1)}, bf16[4,2,64,768]{3,2,1,0:T(8,128)(2,1)S(1)}, u32[]{:S(2)}, u32[]{:S(2)}) %collective-permute-start.10) | collective-permute-done | bytes 786464 | tf_op jit(solution)/shard_map/ppermute | solution.py:589
  349.9 4.8 returned.1
  354.7 4.5 branch_back.2
  373.2 13.7 %attend_back.2 = (bf16[4,128,1152]{2,1,0:T(8,128)(2,1)}, f32[32,128]{1,0:T(8,128)S(1)}) custom-call(bf16[1024,576]{1,0:T(8,128)(2,1)} %get-tuple-element.76.qkv_ref, bf16[3,1024,1024]{2,1,0:T(8,128)(2,1)} %get-tuple-element.77.prob_ref, bf16[4,128,384]{2,1,0:T(8,128)(2,1)S(1)} %all-to-all-done.6.grad_ref, s32[1,2048]{1,0:T(1,128)S(1)} %bitcast.75), custom_call_target="tpu_custom_call" | custom-call | flops 8053063680 | bytes 7864320 | tf_op jit(solution)/shard_map/attend_back/pallas_call | solution.py:238
  386.9 4.3 all-to-all-start.7
  394.3 13.7 %attend_back.3 = (bf16[4,128,1152]{2,1,0:T(8,128)(2,1)}, f32[32,128]{1,0:T(8,128)S(1)}) custom-call(bf16[1024,576]{1,0:T(8,128)(2,1)} %get-tuple-element.88.qkv_ref, bf16[3,1024,1024]{2,1,0:T(8,128)(2,1)} %get-tuple-element.89.prob_ref, bf16[4,128,384]{2,1,0:T(8,128)(2,1)S(1)} %all-to-all-done.8.grad_ref, s32[1,2048]{1,0:T(1,128)S(1)} %bitcast.76), custom_call_target="tpu_custom_call" | custom-call | flops 8053063680 | bytes 7864320 | tf_op jit(solution)/shard_map/attend_back/pallas_call | solution.py:238
  408.0 4.4 all-to-all-start.9
  422.3 4.9 all-to-all-done.9.grad_ref
  427.2 4.8 all-to-all-start.11
  432.0 33.0 %weight_grads.1 = (f32[2,768,768]{2,1,0:T(8,128)}, f32[2,768,768]{2,1,0:T(8,128)}) custom-call(s32[4]{0:T(128)S(1)} %pad_add_fusion.place_ref, bf16[8,2,64,768]{3,2,1,0:T(8,128)(2,1)} %all_to_all.60.x_ref.refs_0_, bf16[8,2,64,768]{3,2,1,0:T(8,128)(2,1)} %copy-done.14, bf16[8,2,64,768]{3,2,1,0:T(8,128)(2,1)} %copy-done.15, ...), custom_call_target="tpu_custom_call" | custom-call | flops 38654705664 | bytes 22020096 | tf_op jit(solution)/shard_map/weight_grads/pallas_call | solution.py:562
  476.4 5.4 all-to-all-start.10
  481.8 3.6 collective-permute-start.35
  486.2 4.9 input_back.2
  491.2 4.9 input_back.3
  505.4 5.6 %collective-permute-start.32 = (f32[9,128]{1,0:T(8,128)S(1)}, f32[9,128]{1,0:T(8,128)S(1)}, u32[]{:S(2)}, u32[]{:S(2)}) collective-permute-start(f32[9,128]{1,0:T(8,128)S(1)} %add_add_fusion.1), channel_id=1, source_target_pairs={{0,4},{1,5},{2,6},{3,7},{4,0},{5,1},{6,2},{7,3},{8,12},{9,13},{10,... | collective-permute-start | bytes 13832 | tf_op jit(solution)/shard_map/ppermute | solution.py:589
  526.5 14.4 %all-gather.1 = bf16[384,576]{1,0:T(8,128)(2,1)S(1)} all-gather(bf16[96,576]{1,0:T(8,128)(2,1)S(1)} %reduce_sum.31), channel_id=3, replica_groups=mesh['seq'=4,'shard'=8] {'seq'}, dimensions={0}, use_global_device_ids=true | all-gather | bytes 552960 | tf_op jit(solution)/shard_map/all_gather | solution.py:769
  (201 shorter events, 116.3 us)
Async XLA Ops:
  7.2 92.2 %all-gather.5.cloned.1.call-start = ((), (), s32[]{:S(2)}) async-start(), calls=%async_computation.12 | async-start | bytes 1548288 | tf_op jit(solution)/shard_map/all_gather | solution.py:664
  25.8 25.2 %collective-permute-start.4 = (bf16[256,768]{1,0:T(8,128)(2,1)S(1)}, bf16[256,768]{1,0:T(8,128)(2,1)S(1)}, u32[]{:S(2)}, u32[]{:S(2)}) collective-permute-start(bf16[256,768]{1,0:T(8,128)(2,1)S(1)} %get-tuple-element.67.own_ref), channel_id=1, source_target_pairs={{0,8},{8,0},{16,24},{24,16},{1,9},{9,1},{17,25},{25,17},{2,10},{10... | collective-permute-start | bytes 1179656 | tf_op jit(solution)/shard_map/ppermute | solution.py:589
  26.1 27.2 %collective-permute-start.5 = (bf16[256,768]{1,0:T(8,128)(2,1)S(1)}, bf16[256,768]{1,0:T(8,128)(2,1)S(1)}, u32[]{:S(2)}, u32[]{:S(2)}) collective-permute-start(bf16[256,768]{1,0:T(8,128)(2,1)S(1)} %get-tuple-element.67.own_ref), channel_id=1, source_target_pairs={{0,16},{8,24},{16,0},{24,8},{1,17},{9,25},{17,1},{25,9},{2,18},{10... | collective-permute-start | bytes 1179656 | tf_op jit(solution)/shard_map/ppermute | solution.py:589
  51.6 23.3 %collective-permute-start.6 = (bf16[128,768]{1,0:T(8,128)(2,1)}, bf16[128,768]{1,0:T(8,128)(2,1)S(1)}, u32[]{:S(2)}, u32[]{:S(2)}) collective-permute-start(bf16[128,768]{1,0:T(8,128)(2,1)} %slice.77), channel_id=1, source_target_pairs={{0,16},{8,24},{16,0},{24,8},{1,17},{9,25},{17,1},{25,9},{2,18},{10... | collective-permute-start | bytes 589832 | tf_op jit(solution)/shard_map/ppermute | solution.py:589
  54.0 20.9 %collective-permute-start.7 = (bf16[128,768]{1,0:T(8,128)(2,1)}, bf16[128,768]{1,0:T(8,128)(2,1)S(1)}, u32[]{:S(2)}, u32[]{:S(2)}) collective-permute-start(bf16[128,768]{1,0:T(8,128)(2,1)} %slice.78), channel_id=1, source_target_pairs={{0,8},{8,0},{16,24},{24,16},{1,9},{9,1},{17,25},{25,17},{2,10},{10... | collective-permute-start | bytes 589832 | tf_op jit(solution)/shard_map/ppermute | solution.py:589
  70.3 18.6 %all-to-all-start = ((bf16[4,128,384]{2,1,0:T(8,128)(2,1)}), bf16[4,128,384]{2,1,0:T(8,128)(2,1)S(1)}, u32[]{:S(2)}, u32[]{:S(2)}) async-start(bf16[4,128,384]{2,1,0:T(8,128)(2,1)} %get-tuple-element.66), calls=%async_computation | async-start | bytes 786432 | tf_op jit(solution)/shard_map/all_to_all | solution.py:687
  148.3 41.3 %all-to-all-start.4 = ((bf16[8,2,64,768]{3,2,1,0:T(8,128)(2,1)}), bf16[8,2,64,768]{3,2,1,0:T(8,128)(2,1)S(1)}, u32[]{:S(2)}, u32[]{:S(2)}) async-start(bf16[8,2,64,768]{3,2,1,0:T(8,128)(2,1)} %bitcast.83), calls=%async_computation.4 | async-start | bytes 3145728 | tf_op jit(solution)/shard_map/all_to_all | solution.py:701
  207.4 41.3 %all-to-all-start.5 = ((bf16[8,2,64,768]{3,2,1,0:T(8,128)(2,1)}), bf16[8,2,64,768]{3,2,1,0:T(8,128)(2,1)S(1)}, u32[]{:S(2)}, u32[]{:S(2)}) async-start(bf16[8,2,64,768]{3,2,1,0:T(8,128)(2,1)} %expert_backward.1), calls=%async_computation.5 | async-start | bytes 3145728 | tf_op jit(solution)/shard_map/all_to_all | solution.py:701
  211.0 138.8 %all-gather.7.cloned.1.call-start = ((), (), s32[]{:S(2)}) async-start(), calls=%async_computation.13 | async-start | bytes 4915200 | tf_op jit(solution)/shard_map/all_gather | solution.py:704
  250.0 99.9 %all-to-all-start.3 = ((bf16[8,2,64,768]{3,2,1,0:T(8,128)(2,1)}), bf16[8,2,64,768]{3,2,1,0:T(8,128)(2,1)}, u32[]{:S(2)}, u32[]{:S(2)}) async-start(bf16[8,2,64,768]{3,2,1,0:T(8,128)(2,1)} %get-tuple-element.71), calls=%async_computation.3 | async-start | bytes 3145728 | tf_op jit(solution)/shard_map/all_to_all | solution.py:701
  254.2 44.1 %collective-permute-start.8 = (bf16[8,2,64,768]{3,2,1,0:T(8,128)(2,1)}, bf16[8,2,64,768]{3,2,1,0:T(8,128)(2,1)S(1)}, u32[]{:S(2)}, u32[]{:S(2)}) collective-permute-start(bf16[8,2,64,768]{3,2,1,0:T(8,128)(2,1)} %all_to_all.60.x_ref.refs_0_), channel_id=1, source_target_pairs={{0,8},{8,0},{16,24},{24,16},{1,9},{9,1},{17,25},{25,17},{2,10},{10... | collective-permute-start | bytes 4718600 | tf_op jit(solution)/shard_map/ppermute | solution.py:589
  255.8 45.0 %collective-permute-start.9 = (bf16[8,2,64,768]{3,2,1,0:T(8,128)(2,1)}, bf16[8,2,64,768]{3,2,1,0:T(8,128)(2,1)S(1)}, u32[]{:S(2)}, u32[]{:S(2)}) collective-permute-start(bf16[8,2,64,768]{3,2,1,0:T(8,128)(2,1)} %all_to_all.60.x_ref.refs_0_), channel_id=1, source_target_pairs={{0,16},{8,24},{16,0},{24,8},{1,17},{9,25},{17,1},{25,9},{2,18},{10... | collective-permute-start | bytes 4718600 | tf_op jit(solution)/shard_map/ppermute | solution.py:589
  256.3 75.7 %collective-permute-start.12 = (bf16[8,2,64,768]{3,2,1,0:T(8,128)(2,1)}, bf16[8,2,64,768]{3,2,1,0:T(8,128)(2,1)S(1)}, u32[]{:S(2)}, u32[]{:S(2)}) collective-permute-start(bf16[8,2,64,768]{3,2,1,0:T(8,128)(2,1)} %copy-done.11), channel_id=1, source_target_pairs={{0,8},{8,0},{16,24},{24,16},{1,9},{9,1},{17,25},{25,17},{2,10},{10... | collective-permute-start | bytes 4718600 | tf_op jit(solution)/shard_map/ppermute | solution.py:589
  257.8 76.7 %collective-permute-start.13 = (bf16[8,2,64,768]{3,2,1,0:T(8,128)(2,1)}, bf16[8,2,64,768]{3,2,1,0:T(8,128)(2,1)S(1)}, u32[]{:S(2)}, u32[]{:S(2)}) collective-permute-start(bf16[8,2,64,768]{3,2,1,0:T(8,128)(2,1)} %copy-done.11), channel_id=1, source_target_pairs={{0,16},{8,24},{16,0},{24,8},{1,17},{9,25},{17,1},{25,9},{2,18},{10... | collective-permute-start | bytes 4718600 | tf_op jit(solution)/shard_map/ppermute | solution.py:589
  299.3 49.6 %collective-permute-start.10 = (bf16[4,2,64,768]{3,2,1,0:T(8,128)(2,1)}, bf16[4,2,64,768]{3,2,1,0:T(8,128)(2,1)S(1)}, u32[]{:S(2)}, u32[]{:S(2)}) collective-permute-start(bf16[4,2,64,768]{3,2,1,0:T(8,128)(2,1)} %slice.79), channel_id=1, source_target_pairs={{0,16},{8,24},{16,0},{24,8},{1,17},{9,25},{17,1},{25,9},{2,18},{10... | collective-permute-start | bytes 2359304 | tf_op jit(solution)/shard_map/ppermute | solution.py:589
  301.9 48.0 %collective-permute-start.11 = (bf16[4,2,64,768]{3,2,1,0:T(8,128)(2,1)}, bf16[4,2,64,768]{3,2,1,0:T(8,128)(2,1)}, u32[]{:S(2)}, u32[]{:S(2)}) collective-permute-start(bf16[4,2,64,768]{3,2,1,0:T(8,128)(2,1)} %slice.80), channel_id=1, source_target_pairs={{0,8},{8,0},{16,24},{24,16},{1,9},{9,1},{17,25},{25,17},{2,10},{10... | collective-permute-start | bytes 2359304 | tf_op jit(solution)/shard_map/ppermute | solution.py:589
  333.0 40.2 %collective-permute-start.14 = (bf16[4,2,64,768]{3,2,1,0:T(8,128)(2,1)}, bf16[4,2,64,768]{3,2,1,0:T(8,128)(2,1)}, u32[]{:S(2)}, u32[]{:S(2)}) collective-permute-start(bf16[4,2,64,768]{3,2,1,0:T(8,128)(2,1)} %slice.81), channel_id=1, source_target_pairs={{0,16},{8,24},{16,0},{24,8},{1,17},{9,25},{17,1},{25,9},{2,18},{10... | collective-permute-start | bytes 2359304 | tf_op jit(solution)/shard_map/ppermute | solution.py:589
  335.9 37.3 %collective-permute-start.15 = (bf16[4,2,64,768]{3,2,1,0:T(8,128)(2,1)}, bf16[4,2,64,768]{3,2,1,0:T(8,128)(2,1)}, u32[]{:S(2)}, u32[]{:S(2)}) collective-permute-start(bf16[4,2,64,768]{3,2,1,0:T(8,128)(2,1)} %slice.82), channel_id=1, source_target_pairs={{0,8},{8,0},{16,24},{24,16},{1,9},{9,1},{17,25},{25,17},{2,10},{10... | collective-permute-start | bytes 2359304 | tf_op jit(solution)/shard_map/ppermute | solution.py:589
  369.7 17.2 %all-to-all-start.8 = ((bf16[4,128,384]{2,1,0:T(8,128)(2,1)}), bf16[4,128,384]{2,1,0:T(8,128)(2,1)S(1)}, u32[]{:S(2)}, u32[]{:S(2)}) async-start(bf16[4,128,384]{2,1,0:T(8,128)(2,1)} %copy-done.5), calls=%async_computation.8 | async-start | bytes 786432 | tf_op jit(solution)/shard_map/all_to_all | solution.py:731
  386.9 21.1 %all-to-all-start.7 = ((bf16[4,128,1152]{2,1,0:T(8,128)(2,1)}), bf16[4,128,1152]{2,1,0:T(8,128)(2,1)}, u32[]{:S(2)}, u32[]{:S(2)}) async-start(bf16[4,128,1152]{2,1,0:T(8,128)(2,1)} %get-tuple-element.85), calls=%async_computation.7 | async-start | bytes 2359296 | tf_op jit(solution)/shard_map/all_to_all | solution.py:750
  408.0 19.2 %all-to-all-start.9 = ((bf16[4,128,1152]{2,1,0:T(8,128)(2,1)}), bf16[4,128,1152]{2,1,0:T(8,128)(2,1)}, u32[]{:S(2)}, u32[]{:S(2)}) async-start(bf16[4,128,1152]{2,1,0:T(8,128)(2,1)} %get-tuple-element.91), calls=%async_computation.9 | async-start | bytes 2359296 | tf_op jit(solution)/shard_map/all_to_all | solution.py:750
  418.6 63.1 %collective-permute-start.28 = (f32[9,128]{1,0:T(8,128)S(1)}, f32[9,128]{1,0:T(8,128)S(1)}, u32[]{:S(2)}, u32[]{:S(2)}) collective-permute-start(f32[9,128]{1,0:T(8,128)S(1)} %maximum_bitcast_fusion), channel_id=1, source_target_pairs={{0,24},{8,16},{16,8},{24,0},{1,25},{9,17},{17,9},{25,1},{2,26},{10... | collective-permute-start | bytes 13832 | tf_op jit(solution)/shard_map/ppermute | solution.py:589
  421.7 60.1 %collective-permute-start.27 = (f32[9,128]{1,0:T(8,128)S(1)}, f32[9,128]{1,0:T(8,128)S(1)}, u32[]{:S(2)}, u32[]{:S(2)}) collective-permute-start(f32[9,128]{1,0:T(8,128)S(1)} %maximum_bitcast_fusion), channel_id=1, source_target_pairs={{0,16},{8,24},{16,0},{24,8},{1,17},{9,25},{17,1},{25,9},{2,18},{10... | collective-permute-start | bytes 13832 | tf_op jit(solution)/shard_map/ppermute | solution.py:589
  422.2 59.5 %collective-permute-start.26 = (f32[9,128]{1,0:T(8,128)S(1)}, f32[9,128]{1,0:T(8,128)S(1)}, u32[]{:S(2)}, u32[]{:S(2)}) collective-permute-start(f32[9,128]{1,0:T(8,128)S(1)} %maximum_bitcast_fusion), channel_id=1, source_target_pairs={{0,8},{8,0},{16,24},{24,16},{1,9},{9,1},{17,25},{25,17},{2,10},{10... | collective-permute-start | bytes 13832 | tf_op jit(solution)/shard_map/ppermute | solution.py:589
  427.2 49.2 %all-to-all-start.11 = ((bf16[8,96,784]{2,1,0:T(8,128)(2,1)}), bf16[8,96,784]{2,1,0:T(8,128)(2,1)}, u32[]{:S(2)}, u32[]{:S(2)}) async-start(bf16[8,96,784]{2,1,0:T(8,128)(2,1)} %bitcast.81), calls=%async_computation.11 | async-start | bytes 2752512 | tf_op jit(solution)/shard_map/all_to_all | solution.py:615
  476.4 50.0 %all-to-all-start.10 = ((bf16[8,96,576]{2,1,0:T(8,128)(2,1)}), bf16[8,96,576]{2,1,0:T(8,128)(2,1)S(1)}, u32[]{:S(2)}, u32[]{:S(2)}) async-start(bf16[8,96,576]{2,1,0:T(8,128)(2,1)} %bitcast.27), calls=%async_computation.10 | async-start | bytes 1966080 | tf_op jit(solution)/shard_map/all_to_all | solution.py:615
  481.8 20.6 %collective-permute-start.35 = (f32[9,128]{1,0:T(8,128)S(1)}, f32[9,128]{1,0:T(8,128)S(1)}, u32[]{:S(2)}, u32[]{:S(2)}) collective-permute-start(f32[9,128]{1,0:T(8,128)S(1)} %add_add_fusion.1), channel_id=1, source_target_pairs={{0,7},{1,6},{2,5},{3,4},{4,3},{5,2},{6,1},{7,0},{8,15},{9,14},{10,... | collective-permute-start | bytes 13832 | tf_op jit(solution)/shard_map/ppermute | solution.py:589
  485.4 20.0 %collective-permute-start.34 = (f32[9,128]{1,0:T(8,128)S(1)}, f32[9,128]{1,0:T(8,128)S(1)}, u32[]{:S(2)}, u32[]{:S(2)}) collective-permute-start(f32[9,128]{1,0:T(8,128)S(1)} %add_add_fusion.1), channel_id=1, source_target_pairs={{0,6},{1,7},{2,4},{3,5},{4,2},{5,3},{6,0},{7,1},{8,14},{9,15},{10,... | collective-permute-start | bytes 13832 | tf_op jit(solution)/shard_map/ppermute | solution.py:589
  485.8 25.3 %collective-permute-start.33 = (f32[9,128]{1,0:T(8,128)S(1)}, f32[9,128]{1,0:T(8,128)S(1)}, u32[]{:S(2)}, u32[]{:S(2)}) collective-permute-start(f32[9,128]{1,0:T(8,128)S(1)} %add_add_fusion.1), channel_id=1, source_target_pairs={{0,5},{1,4},{2,7},{3,6},{4,1},{5,0},{6,3},{7,2},{8,13},{9,12},{10,... | collective-permute-start | bytes 13832 | tf_op jit(solution)/shard_map/ppermute | solution.py:589
  496.1 14.9 %collective-permute-start.18 = (f32[6,128]{1,0:T(8,128)S(1)}, f32[6,128]{1,0:T(8,128)S(1)}, u32[]{:S(2)}, u32[]{:S(2)}) collective-permute-start(f32[6,128]{1,0:T(8,128)S(1)} %bitcast.88), channel_id=1, source_target_pairs={{0,24},{8,16},{16,8},{24,0},{1,25},{9,17},{17,9},{25,1},{2,26},{10... | collective-permute-start | bytes 9224 | tf_op jit(solution)/shard_map/ppermute | solution.py:589
  497.7 14.6 %collective-permute-start.17 = (f32[6,128]{1,0:T(8,128)S(1)}, f32[6,128]{1,0:T(8,128)S(1)}, u32[]{:S(2)}, u32[]{:S(2)}) collective-permute-start(f32[6,128]{1,0:T(8,128)S(1)} %bitcast.89), channel_id=1, source_target_pairs={{0,16},{8,24},{16,0},{24,8},{1,17},{9,25},{17,1},{25,9},{2,18},{10... | collective-permute-start | bytes 9224 | tf_op jit(solution)/shard_map/ppermute | solution.py:589
  525.1 19.6 %collective-permute-start.37 = (f32[96,784]{1,0:T(8,128)}, f32[96,784]{1,0:T(8,128)}, u32[]{:S(2)}, u32[]{:S(2)}) collective-permute-start(f32[96,784]{1,0:T(8,128)} %add.134), channel_id=1, source_target_pairs={{0,16},{8,24},{16,0},{24,8},{1,17},{9,25},{17,1},{25,9},{2,18},{10... | collective-permute-start | bytes 903176 | tf_op jit(solution)/shard_map/ppermute | solution.py:589
  (43 other events, 434.3 us)
Sparse Core Ops, SparseCore 0:
  10.3 29.6 all-gather.4
  213.7 57.9 all-gather.6

commit v3 on v2

--- a/solution.py
+++ b/solution.py
@@ -78,14 +78,38 @@
     return v * cumulative, cumulative + v * (jnp.exp(-0.5 * v * v) * DENSITY)
 
 
+def bias_kernel(rel_ref, bucket_ref, out_ref):
+    span = bucket_ref.shape[1]
+    bucket_row = bucket_ref[...]
+    for head in range(out_ref.shape[0]):
+        row = jnp.zeros((1, span), f32)
+        for bucket in range(rel_ref.shape[0]):
+            row = jnp.where(bucket_row == bucket, rel_ref[bucket, head], row)
+        out_ref[head] = pltpu.roll(
+            jnp.broadcast_to(row, (LANES, span)), span - LANES + 1, 1, stride=1, stride_axis=0
+        )
+
+
+def bias_tiles(rel, bucket_row):
+    out_shape = shape((rel.shape[1], LANES, bucket_row.shape[1]), f32)
+    return pl.pallas_call(
+        bias_kernel,
+        in_specs=[SMEM, whole(bucket_row)],
+        out_specs=whole(out_shape),
+        out_shape=out_shape,
+        compiler_params=PARAMS,
+        cost_estimate=cost(0, out_shape),
+        name="bias_tiles",
+    )(rel, bucket_row)
+
+
 def attend_kernel(
-    place_ref, rel_ref, own_ref, near_ref, far_ref, low_ref, high_ref, w_ref, bucket_ref,
-    rows_ref, qkv_ref, att_ref, prob_ref, split, outs, toeplitz,
+    place_ref, own_ref, near_ref, far_ref, low_ref, high_ref, w_ref, toeplitz_ref,
+    rows_ref, qkv_ref, att_ref, prob_ref, split, outs,
 ):
     head = pl.program_id(0)
     heads, length, head_dim = outs.shape
     width = heads * head_dim
-    span = 2 * length
     piece = own_ref.shape[0]
 
     @pl.when(head == 0)
@@ -97,20 +121,13 @@
         half = piece // 2
         rows_ref[pl.ds(at, half), :] = low_ref[...]
         rows_ref[pl.ds(pl.multiple_of(at + half, half), half), :] = high_ref[...]
-        qkv = nn(rows_ref[...], w_ref[...]).astype(bf16)
+        qkv = nn(rows_ref[...], w_ref[:, : 3 * width]).astype(bf16)
         qkv_ref[...] = qkv
         for part in range(3):
             for each in range(heads):
                 at = part * width + each * head_dim
                 split[part, each] = qkv[:, at : at + head_dim]
 
-    bucket_row = bucket_ref[...]
-    row = jnp.zeros((1, span), f32)
-    for bucket in range(rel_ref.shape[0]):
-        row = jnp.where(bucket_row == bucket, rel_ref[bucket, head], row)
-    toeplitz[...] = pltpu.roll(
-        jnp.broadcast_to(row, (LANES, span)), span - LANES + 1, 1, stride=1, stride_axis=0
-    )
     keys = split[1, head]
     values = split[2, head]
     for start in range(0, length, BLOCK_ROWS):
@@ -118,7 +135,7 @@
         parts = []
         for sub in range(0, BLOCK_ROWS, LANES):
             off = length - LANES - start - sub
-            parts.append(scores[sub : sub + LANES] + toeplitz[:, off : off + length])
+            parts.append(scores[sub : sub + LANES] + toeplitz_ref[0, :, off : off + length])
         scores = jnp.concatenate(parts, axis=0)
         peak = jnp.max(scores, axis=-1, keepdims=True)
         grown = jnp.exp(scores - peak)
@@ -134,11 +151,12 @@
             att_ref[number] = pack_rows(joined[number * piece : (number + 1) * piece])
 
 
-def attend(place, pieces, weight, rel, bucket_row, heads):
+def attend(place, pieces, weight, tiles):
     own, near, far, low, high = pieces
     piece, model = own.shape
-    length = bucket_row.shape[1] // 2
-    cols = weight.shape[1]
+    heads, _, span = tiles.shape
+    length = span // 2
+    cols = 3 * (model // (length // piece))
     width = cols // 3
     head_dim = width // heads
     out_shape = [
@@ -150,20 +168,20 @@
     return pl.pallas_call(
         attend_kernel,
         grid=(heads,),
-        in_specs=[SMEM, SMEM]
-        + [whole(a) for a in (own, near, far, low, high, weight, bucket_row)],
+        in_specs=[SMEM]
+        + [whole(a) for a in (own, near, far, low, high, weight)]
+        + [pl.BlockSpec((1, LANES, span), lambda h: (h, 0, 0))],
         out_specs=[whole(a) for a in out_shape[:3]]
         + [pl.BlockSpec((1, length, length), lambda h: (h, 0, 0))],
         out_shape=out_shape,
         scratch_shapes=[
             pltpu.VMEM((3, heads, length, head_dim), bf16),
             pltpu.VMEM((heads, length, head_dim), f32),
-            pltpu.VMEM((LANES, 2 * length), f32),
         ],
         compiler_params=PARAMS,
         cost_estimate=cost(2 * length * model * cols + 16 * heads * length * length * head_dim, *out_shape),
         name="attend",
-    )(place, rel, own, near, far, low, high, weight, bucket_row)
+    )(place, own, near, far, low, high, weight, tiles)
 
 
 def attend_back_kernel(
@@ -439,6 +457,70 @@
     )(*operands)
 
 
+def column_kernel(seqs, place_ref, *refs):
+    count = len(refs) - 2 * seqs - 1
+    row_refs, grad_refs, out_refs = refs[:seqs], refs[seqs : 2 * seqs], refs[2 * seqs : -1]
+    total = refs[-1]
+    value = None
+    for row_ref, grad_ref in zip(row_refs, grad_refs):
+        grad = jnp.concatenate(
+            [unpack_rows(grad_ref[piece]) for piece in range(grad_ref.shape[0])], axis=0
+        )
+        part = tn(row_ref[...], grad)
+        value = part if value is None else value + part
+    total[...] = value.astype(bf16)
+    for number in range(count):
+        rows = out_refs[number].shape[0]
+        at = pl.multiple_of(place_ref[number] * rows, rows)
+        out_refs[number][...] = total[pl.ds(at, rows), :]
+
+
+def column_grads(places, rows, grads, chunks):
+    model = rows[0].shape[1]
+    cols = grads[0].shape[2] // 2
+    out_shape = [shape((model // chunks, cols), bf16)] * chunks
+    return pl.pallas_call(
+        functools.partial(column_kernel, len(rows)),
+        in_specs=[SMEM] + [whole(a) for a in (*rows, *grads)],
+        out_specs=[whole(a) for a in out_shape],
+        out_shape=out_shape,
+        scratch_shapes=[pltpu.VMEM((model, cols), bf16)],
+        compiler_params=PARAMS,
+        cost_estimate=cost(2 * sum(math.prod(r.shape) for r in rows) * cols, *rows, *grads),
+        name="column_grads",
+    )(places, *rows, *grads)
+
+
+def column_order_kernel(place_ref, *refs):
+    out_ref, held = refs[-2:]
+    groups = held.shape[0]
+    width = held.shape[2] // 3
+    for number in range(groups):
+        held[number] = refs[number][...].astype(f32)
+    for part in range(3):
+        joined = [
+            held[place_ref[group], :, part * width : (part + 1) * width] for group in range(groups)
+        ]
+        out_ref[:, part * groups * width : (part + 1) * groups * width] = jnp.concatenate(
+            joined, axis=1
+        )
+
+
+def column_order(places, pieces):
+    rows, cols = pieces[0].shape
+    out_shape = shape((rows, cols * len(pieces)), f32)
+    return pl.pallas_call(
+        column_order_kernel,
+        in_specs=[SMEM] + [whole(a) for a in pieces],
+        out_specs=whole(out_shape),
+        out_shape=out_shape,
+        scratch_shapes=[pltpu.VMEM((len(pieces), rows, cols), f32)],
+        compiler_params=PARAMS,
+        cost_estimate=cost(0, out_shape, *pieces),
+        name="column_order",
+    )(places, *pieces)
+
+
 def expert_kernel(x_ref, win_ref, wout_ref, y_ref, slope_ref, acc):
     tile = pl.program_id(1)
     rows = acc.shape[0]
@@ -527,8 +609,7 @@
     )(g, w_in, w_out, slope)
 
 
-def weight_grad_kernel(place_ref, *refs):
-    pieces = (len(refs) - 4) // 2
+def weight_grad_kernel(pieces, place_ref, *refs):
     x_refs, g_refs = refs[:pieces], refs[pieces : 2 * pieces]
     win_ref, wout_ref = refs[2 * pieces : 2 * pieces + 2]
     gin_ref, gout_ref = refs[-2:]
@@ -547,7 +628,7 @@
     gout_ref[0] = gout
 
 
-def weight_grads(place, xs, gs, w_in, w_out, ways):
+def weight_grads(place, xs, gs, w_in, w_out, ways, expert, earlier):
     experts, model, hidden = w_in.shape
     cols = hidden // ways
     tile = GRAD_TILE if cols % GRAD_TILE == 0 else cols
@@ -555,30 +636,37 @@
 
     def rows_of(array):
         sources, _, slots, _ = array.shape
-        return pl.BlockSpec((sources, 1, slots, model), lambda e, t, q: (0, e, 0, 0))
+        return pl.BlockSpec((sources, 1, slots, model), lambda t, q: (0, expert, 0, 0))
 
     out_shape = [shape((experts, model, cols), f32), shape((experts, cols, model), f32)]
-    flops = 8 * sum(math.prod(a.shape) for a in xs) * cols
-    return pl.pallas_call(
-        weight_grad_kernel,
+    flops = 8 * sum(math.prod(a.shape) for a in xs) * cols // experts
+    operands = [place, *xs, *gs, w_in, w_out]
+    specs = [rows_of(a) for a in (*xs, *gs)] + [
+        pl.BlockSpec((1, model, tile), lambda t, q: (expert, 0, q[0] * tiles + t)),
+        pl.BlockSpec((1, tile, model), lambda t, q: (expert, q[0] * tiles + t, 0)),
+    ]
+    aliases = {}
+    if earlier is not None:
+        aliases = {len(operands): 0, len(operands) + 1: 1}
+        operands += list(earlier)
+        specs += [pl.BlockSpec(memory_space=pl.ANY)] * 2
+    return pl.pallas_call(
+        functools.partial(weight_grad_kernel, len(xs)),
         grid_spec=pltpu.PrefetchScalarGridSpec(
             num_scalar_prefetch=1,
-            grid=(experts, tiles),
-            in_specs=[rows_of(a) for a in (*xs, *gs)]
-            + [
-                pl.BlockSpec((1, model, tile), lambda e, t, q: (e, 0, q[0] * tiles + t)),
-                pl.BlockSpec((1, tile, model), lambda e, t, q: (e, q[0] * tiles + t, 0)),
-            ],
+            grid=(tiles,),
+            in_specs=specs,
             out_specs=[
-                pl.BlockSpec((1, model, tile), lambda e, t, q: (e, 0, t)),
-                pl.BlockSpec((1, tile, model), lambda e, t, q: (e, t, 0)),
+                pl.BlockSpec((1, model, tile), lambda t, q: (expert, 0, t)),
+                pl.BlockSpec((1, tile, model), lambda t, q: (expert, t, 0)),
             ],
         ),
         out_shape=out_shape,
+        input_output_aliases=aliases,
         compiler_params=PARAMS,
         cost_estimate=cost(2 * flops, *out_shape, *xs, *gs),
         name="weight_grads",
-    )(place, *xs, *gs, w_in, w_out)
+    )(*operands)
 
 
 def partners(ways, step):
@@ -600,12 +688,10 @@
 
 def sum_all(value):
     for axis in ("seq", "shard"):
-        ways = lax.axis_size(axis)
-        if ways <= 8:
-            got = [swap(value, axis, step) for step in range(1, ways)]
-            value = functools.reduce(jnp.add, [value] + got)
-        else:
-            value = lax.psum(value, axis)
+        step = 1
+        while step < lax.axis_size(axis):
+            value = value + swap(value, axis, step)
+            step *= 2
     return value
 
 
@@ -660,13 +746,17 @@
     own_columns = lax.dynamic_slice_in_dim(
         w_qkv.reshape(weight_rows, 3, model), seq_index * width, width, 2
     ).reshape(weight_rows, 3 * width)
+    own_columns = jnp.pad(own_columns, ((0, 0), (0, max(0, model - 3 * width))))
     head_weight = lax.all_gather(own_columns, "shard", axis=0, tiled=True)
-    dense = lax.all_gather(
-        jnp.concatenate([w_out, w_router], axis=1), "shard", axis=0, tiled=True
-    )
+    dense_rows, head_weight = lax.optimization_barrier(
+        (jnp.concatenate([w_out, w_router], axis=1), head_weight)
+    )
+    dense = lax.all_gather(dense_rows, "shard", axis=0, tiled=True)
     inputs = block_input.astype(f32)
     normed = (inputs * inverse_norm(inputs) * gain_attn).astype(bf16)
-    bias_dev = lax.dynamic_slice_in_dim(rel_bias, seq_index * heads, heads, 1)
+    tiles = bias_tiles(
+        lax.dynamic_slice_in_dim(rel_bias, seq_index * heads, heads, 1), bucket_row
+    )
 
     first_near = gather_near(normed[0])
     held = lax.optimization_barrier((normed[1], first_near))
@@ -680,9 +770,7 @@
     )
     kept, attended_tok = [], []
     for pieces in sequence_pieces:
-        rows, qkv, attended, probs = attend(
-            places, pieces, head_weight, bias_dev, bucket_row, heads
-        )
+        rows, qkv, attended, probs = attend(places, pieces, head_weight, tiles)
         kept.append((rows, qkv, probs))
         attended_tok.append(lax.all_to_all(attended, "seq", 0, 0, tiled=True))
 
@@ -701,23 +789,35 @@
         return lax.all_to_all(rows, "shard", 0, 0, tiled=True)
 
     held_weight, sent = lax.optimization_barrier((head_weight, sent))
-    weight_groups = lax.all_gather(held_weight, "seq")
+    weight_groups = lax.all_gather(held_weight[:, : 3 * width], "seq")
     arrived = exchange(sent.reshape(slot_shape))
     out_arrived = exchange(sent_grad.reshape(slot_shape))
+    arrived_near = gather_near(arrived)
     expert_out, slope = expert_forward(arrived, w_in, w_exp_out, FORWARD_TILE)
+    expert_out, weight_groups = lax.optimization_barrier((expert_out, weight_groups))
     back_out = exchange(expert_out).reshape(positions, model)
     rows_grad = expert_backward(out_arrived, w_in, w_exp_out, slope, FORWARD_TILE)
+    arrived_near, rows_grad = lax.optimization_barrier((arrived_near, rows_grad))
     back_grad = exchange(rows_grad).reshape(positions, model)
-    arrived_near = gather_near(arrived)
     arrived_far = gather_far(*arrived_near)
     out_near = gather_near(out_arrived)
+    back_out, arrived_far, out_near = lax.optimization_barrier((back_out, arrived_far, out_near))
     out_far = gather_far(*out_near)
-
     block_output, logit_low, grad_router = returned(
         back_out, target_column, id_column, middle, upstream, router_probs, second
     )
-    back_grad, arrived_near, arrived_far, weight_groups = lax.optimization_barrier(
-        (back_grad, arrived_near, arrived_far, weight_groups)
+    expert_xs = (arrived, *arrived_near, *arrived_far)
+    expert_gs = (out_arrived, *out_near, *out_far)
+    expert_count = experts // shard_ways
+
+    def expert_grads(number, earlier):
+        return weight_grads(
+            places, expert_xs, expert_gs, w_in, w_exp_out, seq_ways, number, earlier
+        )
+
+    expert_part = expert_grads(0, None)
+    back_grad, expert_part, logit_low = lax.optimization_barrier(
+        (back_grad, expert_part, logit_low)
     )
     middle_grads, branches, grad_heads, gain_two = [], [], [], []
     for number in range(seqs):
@@ -734,7 +834,8 @@
         for number in range(seqs)
     )
     grad_dense = jnp.concatenate([grad_out.astype(bf16), grad_router], axis=1)
-    grad_dense = scatter_rows(grad_dense)
+    grad_dense = lax.psum_scatter(grad_dense, "shard", scatter_dimension=0, tiled=True)
+    grad_dense = grad_dense.astype(f32)
     for step in (1, 2):
         grad_dense = grad_dense + swap(grad_dense, "seq", step)
 
@@ -742,36 +843,28 @@
     for number in range(seqs):
         _, qkv, probs = kept[number]
         grad = grad_heads[number]
-        if number == seqs - 1:
-            grad, out_near, out_far = lax.optimization_barrier((grad, out_near, out_far))
         qkv_grad, bias_part = attend_back(qkv, probs, grad, bucket_row, bucket_count)
         qkv_grads.append(qkv_grad)
         bias_parts.append(bias_part)
         grad_tok.append(lax.all_to_all(qkv_grad, "seq", 0, 0, tiled=True))
-    out_arrived, _ = lax.optimization_barrier((out_arrived, qkv_grads[-1]))
-    grad_in_part, grad_exp_part = weight_grads(
-        places,
-        (arrived, *arrived_near, *arrived_far),
-        (out_arrived, *out_near, *out_far),
-        w_in,
-        w_exp_out,
-        seq_ways,
-    )
-    columns = None
-    for number in range(seqs):
-        packed = qkv_grads[number]
-        cols = packed.shape[2] // 2
-        rows = kept[number][0].reshape(seq_ways, 2, piece // 2, model)
-        flat = packed.reshape(seq_ways, piece // 2, 2, cols)
-        part = jnp.einsum("phrd,prhe->de", rows, flat, preferred_element_type=f32)
-        columns = part if columns is None else columns + part
-    columns = scatter_rows(columns.astype(bf16)).astype(bf16)
-    grad_qkv = lax.all_gather(columns, "seq")
-    grad_qkv = (
-        grad_qkv.reshape(seq_ways, weight_rows, 3, width)
-        .transpose(1, 2, 0, 3)
-        .reshape(weight_rows, 3 * model)
-        .astype(f32)
+    rows_all = [each[0] for each in kept]
+    if shard_ways <= 8 and weight_rows % 16 == 0:
+        shard_index = lax.axis_index("shard").astype(jnp.int32)
+        order = jnp.stack([shard_index ^ step for step in range(shard_ways)])
+        chunks = column_grads(order, rows_all, qkv_grads, shard_ways)
+        got = [chunks[0]] + [swap(chunks[step], "shard", step) for step in range(1, shard_ways)]
+        columns = functools.reduce(jnp.add, [each.astype(f32) for each in got])
+        last = chunks[0]
+    else:
+        (last,) = column_grads(places - places, rows_all, qkv_grads, 1)
+        columns = scatter_rows(last)
+    columns = columns.astype(bf16)
+    expert_gs = lax.optimization_barrier((expert_gs, last))[0]
+    for number in range(1, expert_count):
+        expert_part = expert_grads(number, expert_part)
+    grad_in_part, grad_exp_part = expert_part
+    grad_qkv = column_order(
+        places, [columns] + [swap(columns, "seq", step) for step in range(1, seq_ways)]
     )
     input_grad, gain_one = None, []
     for number in range(seqs):
@@ -786,18 +879,21 @@
         seq_index * heads,
         1,
     )
-    early = jnp.concatenate([bias_grad.reshape(-1), sum(gain_two).reshape(-1)])
-    early = sum_all(early.reshape(-1, LANES)).reshape(-1)
-    gain_one = sum_all(sum(gain_one).reshape(-1, LANES)).reshape(-1)
+    small = sum_all(
+        jnp.concatenate(
+            [bias_grad.reshape(-1), sum(gain_two).reshape(-1), sum(gain_one).reshape(-1)]
+        ).reshape(-1, LANES)
+    ).reshape(-1)
+    bias_size = bucket_count * heads_all
     return (
         block_output.reshape(block_input.shape),
         input_grad,
-        gain_one,
-        early[bucket_count * heads_all :],
+        small[bias_size + model :],
+        small[bias_size : bias_size + model],
         grad_qkv,
         grad_dense[:, :model],
         grad_dense[:, model:],
-        early[: bucket_count * heads_all].reshape(bucket_count, heads_all),
+        small[:bias_size].reshape(bucket_count, heads_all),
         grad_in_part,
         grad_exp_part,
     )

time: 563 us -> 494 us (0.88)
  blocking collectives: 76.9 us -> 0 us
  waiting for transfers between devices: 169 us -> 192 us
  Pallas kernels: 152 us -> 168 us
  local copies, waits for them, and re-layouts: 28.6 us -> 19.4 us
  matrix products: 10.1 us -> 2.07 us
  starting transfers between devices: 93.7 us -> 86.4 us
  other arithmetic: 9.42 us -> 2.95 us
    all_to_all x1 -> x0, blocking collectives: 42.1 us -> none  [exchange(): return lax.all_to_all(rows, 'shard', 0, 0, tiled=True)]
    all_gather x2 -> x0, blocking collectives: 34.7 us -> none  [the longest x1 20.3 us: body(): head_weight = lax.all_gather(own_columns, 'shard', axis=0, tiled=True)]
    all_gather x2 -> x3, waiting for transfers between devices: 0.01 us -> 24.1 us  [the longest x1 24.1 us: body(): head_weight = lax.all_gather(own_columns, 'shard', axis=0, tiled=True)]
    pallas_call x3 -> x7, Pallas kernels: 60.8 us -> 75.8 us  [the longest x2 37.8 us: weight_grads(): pl.pallas_call(functools.partial(weight_grad_kernel, len(xs)), grid_spec=...]
    all_to_all x2 -> x0, starting transfers between devices: 10.1 us -> none  [scatter_rows(): lax.all_to_all(value.reshape(ways, rows // ways, cols), 'shard', 0, 0, ti...]
    all_to_all x3 -> x4, starting transfers between devices: 11.4 us -> 18.2 us  [exchange(): return lax.all_to_all(rows, 'shard', 0, 0, tiled=True)]
    convert_element_type x4 -> x0, local copies, waits for them, and re-layouts: 5.85 us -> none  [the longest x3 3.55 us: body(): grad_qkv = grad_qkv.reshape(seq_ways, weight_rows, 3, width).transpose(1,...]
    ppermute x38 -> x33, starting transfers between devices: 47.1 us -> 43.1 us  [swap(): return lax.ppermute(value, axis, partners(lax.axis_size(axis), step))]
  transfers between devices with their start and end apart: 51 -> 47, of which waited for: 15 -> 22; matrix products, arithmetic and copies ran while one was open for 7% -> 4% of each run, Pallas kernels for 23% -> 32%
where the time goes in v3:
time: 494 us; the launch traced here: 485 us
  waiting for transfers between devices  192 us (39%)
  Pallas kernels  168 us (34%)
  starting transfers between devices  86.4 us (17%)
  local copies, waits for them, and re-layouts  19.4 us (4%)
  between operations  14.8 us (3%)
    ppermute x33, waiting for transfers between devices, swap(): return lax.ppermute(value, axis, partners(lax.axis_size(axis), step))  97.7 us
    all_to_all x4, waiting for transfers between devices, exchange(): return lax.all_to_all(rows, 'shard', 0, 0, tiled=True)  56.9 us
    ppermute x33, starting transfers between devices, swap(): return lax.ppermute(value, axis, partners(lax.axis_size(axis), step))  43.1 us
    pallas_call x2, Pallas kernels, weight_grads(): pl.pallas_call(functools.partial(weight_grad_kernel, len(xs)), grid_spec=...  37.8 us
    pallas_call x2, Pallas kernels, attend(): pl.pallas_call(attend_kernel, grid=(heads,), in_specs=[SMEM] + [whole(a)...  27.6 us
    pallas_call x2, Pallas kernels, attend_back(): pl.pallas_call(attend_back_kernel, grid=(heads,), in_specs=[whole(qkv), p...  27.3 us
    all_gather x1, waiting for transfers between devices, body(): head_weight = lax.all_gather(own_columns, 'shard', axis=0, tiled=True)  24.1 us
    all_to_all x4, starting transfers between devices, exchange(): return lax.all_to_all(rows, 'shard', 0, 0, tiled=True)  18.2 us
  transfers between devices with their start and end apart: 47, of which 22 were waited for; matrix products, arithmetic and copies ran while one was open for 4% of the time, Pallas kernels for 32%

profile of v3, /device:TPU:0, one launch (start us, length us, event | category | flops | bytes accessed | tf_op | source)
XLA Modules:
  0.0 485.5 jit_solution(4917549785612096744)
XLA Ops:
  11.6 24.1 %all-gather.5.cloned.1.call-done.w_ref = bf16[768,768]{1,0:T(8,128)(2,1)} async-done(((bf16[96,768]{1,0:T(8,128)(2,1)}), bf16[768,768]{1,0:T(8,128)(2,1)}) %all-gather.5.cloned.1.call-update) | async-done | bytes 1179664 | tf_op jit(solution)/shard_map/all_gather | solution.py:750
  38.8 8.3 %collective-permute-done.near_ref = bf16[256,768]{1,0:T(8,128)(2,1)S(1)} collective-permute-done((bf16[256,768]{1,0:T(8,128)(2,1)S(1)}, bf16[256,768]{1,0:T(8,128)(2,1)S(1)}, u32[]{:S(2)}, u32[]{:S(2)}) %collective-permute-start) | collective-permute-done | bytes 393248 | tf_op jit(solution)/shard_map/ppermute | solution.py:677
  65.1 13.8 %attend.2 = (bf16[1024,768]{1,0:T(8,128)(2,1)}, bf16[1024,576]{1,0:T(8,128)(2,1)}, bf16[4,128,384]{2,1,0:T(8,128)(2,1)}, bf16[3,1024,1024]{2,1,0:T(8,128)(2,1)}) custom-call(s32[4]{0:T(128)S(1)} %pad_add_fusion.place_ref, bf16[256,768]{1,0:T(8,128)(2,1)S(1)} %get-tuple-element.187.own_ref, bf16[256,768]{1,0:T(8,128)(2,1)S(1)} %collective-permute-done.near_ref, ...), custom_call_target="tpu_custom_call" | custom-call | flops 4127195136 | bytes 9437184 | tf_op jit(solution)/shard_map/attend/pallas_call | solution.py:168
  82.5 13.7 %attend.3 = (bf16[1024,768]{1,0:T(8,128)(2,1)}, bf16[1024,576]{1,0:T(8,128)(2,1)}, bf16[4,128,384]{2,1,0:T(8,128)(2,1)}, bf16[3,1024,1024]{2,1,0:T(8,128)(2,1)}) custom-call(s32[4]{0:T(128)S(1)} %pad_add_fusion.place_ref, bf16[256,768]{1,0:T(8,128)(2,1)S(1)} %get-tuple-element.88.own_ref, bf16[256,768]{1,0:T(8,128)(2,1)S(1)} %collective-permute-done.4.near_ref, ...), custom_call_target="tpu_custom_call" | custom-call | flops 4127195136 | bytes 9437184 | tf_op jit(solution)/shard_map/attend/pallas_call | solution.py:168
  96.3 4.7 all-to-all-start.1
  101.2 5.6 %all-to-all-done.1.refs_1_ = bf16[4,128,384]{2,1,0:T(8,128)(2,1)S(1)} async-done(((bf16[4,128,384]{2,1,0:T(8,128)(2,1)}), bf16[4,128,384]{2,1,0:T(8,128)(2,1)S(1)}, u32[]{:S(2)}, u32[]{:S(2)}) %all-to-all-start.1) | async-done | bytes 393248 | tf_op jit(solution)/shard_map/all_to_all | solution.py:775
  106.9 6.8 %project.1 = (f32[512,768]{1,0:T(8,128)}, bf16[512,768]{1,0:T(8,128)(2,1)}, bf16[512,768]{1,0:T(8,128)(2,1)}, f32[512,16]{1,0:T(8,128)S(1)}, bf16[1024,768]{1,0:T(8,128)(2,1)}, /*index=5*/bf16[1024,768]{1,0:T(8,128)(2,1)}) custom-call(bf16[512,768]{1,0:T(8,128)(2,1)} %bitcast.51, bf16[512,768]{1,0:T(8,128)(2,1)} %bitcast.52, s32[512,1]{1,0:T(8,128)S(1)} %bitcast.59, ...), custom_call_target="tpu_custom_call" | custom-call | flops 2214592512 | bytes 6324224 | tf_op jit(solution)/shard_map/project/pallas_call | solution.py:323
  113.7 4.4 all-to-all-start.2
  119.2 36.7 %all-to-all-done.2.x_ref.refs_0_ = bf16[8,2,64,768]{3,2,1,0:T(8,128)(2,1)} async-done(((bf16[8,2,64,768]{3,2,1,0:T(8,128)(2,1)}), bf16[8,2,64,768]{3,2,1,0:T(8,128)(2,1)}, u32[]{:S(2)}, u32[]{:S(2)}) %all-to-all-start.2) | async-done | bytes 1572896 | tf_op jit(solution)/shard_map/all_to_all | solution.py:789
  155.9 4.3 all-to-all-start.4
  160.3 17.6 %expert_forward.1 = (bf16[8,2,64,768]{3,2,1,0:T(8,128)(2,1)}, bf16[2,512,3072]{2,1,0:T(8,128)(2,1)}) custom-call(bf16[8,2,64,768]{3,2,1,0:T(8,128)(2,1)} %all-to-all-done.2.x_ref.refs_0_, bf16[2,768,3072]{2,1,0:T(8,128)(2,1)} %refs_10_.3, bf16[2,3072,768]{2,1,0:T(8,128)(2,1)} %refs_11_.3), custom_call_target="tpu_custom_call" | custom-call | tf_op jit(solution)/shard_map/expert_forward/pallas_call | solution.py:551
  177.9 20.2 %all-to-all-done.4.g_ref.refs_5_ = bf16[8,2,64,768]{3,2,1,0:T(8,128)(2,1)} async-done(((bf16[8,2,64,768]{3,2,1,0:T(8,128)(2,1)}), bf16[8,2,64,768]{3,2,1,0:T(8,128)(2,1)}, u32[]{:S(2)}, u32[]{:S(2)}) %all-to-all-start.4) | async-done | bytes 1572896 | tf_op jit(solution)/shard_map/all_to_all | solution.py:789
  198.1 4.3 all-to-all-start.3
  206.5 16.6 %expert_backward.1 = bf16[8,2,64,768]{3,2,1,0:T(8,128)(2,1)} custom-call(bf16[8,2,64,768]{3,2,1,0:T(8,128)(2,1)} %all-to-all-done.4.g_ref.refs_5_, bf16[2,768,3072]{2,1,0:T(8,128)(2,1)} %refs_10_.3, bf16[2,3072,768]{2,1,0:T(8,128)(2,1)} %refs_11_.3, bf16[2,512,3072]{2,1,0:T(8,128)(2,1)} %get-tuple-element.96.slope_ref), custom_call_target="tpu_custom_call" | custom-call | tf_op jit(solution)/shard_map/expert_backward/pallas_call | solution.py:595
  223.1 16.7 %collective-permute-done.8.refs_1_ = bf16[8,2,64,768]{3,2,1,0:T(8,128)(2,1)S(1)} collective-permute-done((bf16[8,2,64,768]{3,2,1,0:T(8,128)(2,1)}, bf16[8,2,64,768]{3,2,1,0:T(8,128)(2,1)S(1)}, u32[]{:S(2)}, u32[]{:S(2)}) %collective-permute-start.8) | collective-permute-done | bytes 1572896 | tf_op jit(solution)/shard_map/ppermute | solution.py:677
  244.5 5.2 %all-to-all-start.5 = ((bf16[8,2,64,768]{3,2,1,0:T(8,128)(2,1)}), bf16[8,2,64,768]{3,2,1,0:T(8,128)(2,1)}, u32[]{:S(2)}, u32[]{:S(2)}) async-start(bf16[8,2,64,768]{3,2,1,0:T(8,128)(2,1)} %expert_backward.1), calls=%async_computation.5 | async-start | bytes 3145728 | tf_op jit(solution)/shard_map/all_to_all | solution.py:789
  249.7 24.0 %collective-permute-done.12.refs_6_ = bf16[8,2,64,768]{3,2,1,0:T(8,128)(2,1)} collective-permute-done((bf16[8,2,64,768]{3,2,1,0:T(8,128)(2,1)}, bf16[8,2,64,768]{3,2,1,0:T(8,128)(2,1)}, u32[]{:S(2)}, u32[]{:S(2)}) %collective-permute-start.12) | collective-permute-done | bytes 1572896 | tf_op jit(solution)/shard_map/ppermute | solution.py:677
  275.2 15.8 %collective-permute-done.10.refs_3_ = bf16[4,2,64,768]{3,2,1,0:T(8,128)(2,1)S(1)} collective-permute-done((bf16[4,2,64,768]{3,2,1,0:T(8,128)(2,1)S(1)}, bf16[4,2,64,768]{3,2,1,0:T(8,128)(2,1)S(1)}, u32[]{:S(2)}, u32[]{:S(2)}) %collective-permute-start.10) | collective-permute-done | bytes 786464 | tf_op jit(solution)/shard_map/ppermute | solution.py:677
  298.4 4.8 returned.1
  303.3 9.8 %collective-permute-done.14.refs_8_ = bf16[4,2,64,768]{3,2,1,0:T(8,128)(2,1)} collective-permute-done((bf16[4,2,64,768]{3,2,1,0:T(8,128)(2,1)}, bf16[4,2,64,768]{3,2,1,0:T(8,128)(2,1)}, u32[]{:S(2)}, u32[]{:S(2)}) %collective-permute-start.14) | collective-permute-done | bytes 786464 | tf_op jit(solution)/shard_map/ppermute | solution.py:677
  316.6 18.8 %weight_grads.2 = (f32[2,768,768]{2,1,0:T(8,128)}, f32[2,768,768]{2,1,0:T(8,128)}) custom-call(s32[4]{0:T(128)S(1)} %pad_add_fusion.place_ref, bf16[8,2,64,768]{3,2,1,0:T(8,128)(2,1)} %all-to-all-done.2.x_ref.refs_0_, bf16[8,2,64,768]{3,2,1,0:T(8,128)(2,1)} %copy-done.12, bf16[8,2,64,768]{3,2,1,0:T(8,128)(2,1)} %copy-done.13, ...), custom_call_target="tpu_custom_call" | custom-call | flops 19327352832 | bytes 22020096 | tf_op jit(solution)/shard_map/weight_grads/pallas_call | solution.py:653
  335.4 4.5 branch_back.3
  343.9 4.4 branch_back.2
  354.0 13.6 %attend_back.3 = (bf16[4,128,1152]{2,1,0:T(8,128)(2,1)}, f32[32,128]{1,0:T(8,128)S(1)}) custom-call(bf16[1024,576]{1,0:T(8,128)(2,1)} %get-tuple-element.120.qkv_ref, bf16[3,1024,1024]{2,1,0:T(8,128)(2,1)} %get-tuple-element.121.prob_ref, bf16[4,128,384]{2,1,0:T(8,128)(2,1)S(1)} %all-to-all-done.8.grad_ref, s32[1,2048]{1,0:T(1,128)S(1)} %bitcast.62), custom_call_target="tpu_custom_call" | custom-call | flops 8053063680 | bytes 7864320 | tf_op jit(solution)/shard_map/attend_back/pallas_call | solution.py:256
  375.0 13.7 %attend_back.2 = (bf16[4,128,1152]{2,1,0:T(8,128)(2,1)}, f32[32,128]{1,0:T(8,128)S(1)}) custom-call(bf16[1024,576]{1,0:T(8,128)(2,1)} %get-tuple-element.104.qkv_ref, bf16[3,1024,1024]{2,1,0:T(8,128)(2,1)} %get-tuple-element.105.prob_ref, bf16[4,128,384]{2,1,0:T(8,128)(2,1)S(1)} %all-to-all-done.6.grad_ref, s32[1,2048]{1,0:T(1,128)S(1)} %bitcast.63), custom_call_target="tpu_custom_call" | custom-call | flops 8053063680 | bytes 7864320 | tf_op jit(solution)/shard_map/attend_back/pallas_call | solution.py:256
  388.6 4.7 all-to-all-start.7
  393.8 5.0 %input_back.2 = (f32[2,256,768]{2,1,0:T(8,128)}, f32[1,768]{1,0:T(1,128)S(1)}) custom-call(bf16[4,128,1152]{2,1,0:T(8,128)(2,1)} %all-to-all-done.9.grad_ref, bf16[4,768,576]{2,1,0:T(8,128)(2,1)} %bitcast.66, bf16[2,256,768]{2,1,0:T(8,128)(2,1)S(1)} %copy-done.3, f32[1,768]{1,0:T(1,128)S(1)} %reshape.108.gain_ref, ...), custom_call_target="tpu_custom_call" | custom-call | flops 905969664 | bytes 5505024 | tf_op jit(solution)/shard_map/input_back/pallas_call | solution.py:447
  398.8 7.6 %all-to-all-done.7.grad_ref = bf16[4,128,1152]{2,1,0:T(8,128)(2,1)} async-done(((bf16[4,128,1152]{2,1,0:T(8,128)(2,1)}), bf16[4,128,1152]{2,1,0:T(8,128)(2,1)}, u32[]{:S(2)}, u32[]{:S(2)}) %all-to-all-start.7) | async-done | bytes 1179680 | tf_op jit(solution)/shard_map/all_to_all | solution.py:849
  406.4 5.0 %input_back.3 = (f32[2,256,768]{2,1,0:T(8,128)}, f32[1,768]{1,0:T(1,128)S(1)}) custom-call(bf16[4,128,1152]{2,1,0:T(8,128)(2,1)} %all-to-all-done.7.grad_ref, bf16[4,768,576]{2,1,0:T(8,128)(2,1)} %bitcast.67, bf16[2,256,768]{2,1,0:T(8,128)(2,1)S(1)} %copy-done.3, f32[1,768]{1,0:T(1,128)S(1)} %reshape.108.gain_ref, ...), custom_call_target="tpu_custom_call", output_to_operand_aliasing={{0}: (5, {})} | custom-call | flops 905969664 | bytes 5505024 | tf_op jit(solution)/shard_map/input_back/pallas_call | solution.py:447
  412.9 5.3 %column_grads.1 = (bf16[96,576]{1,0:T(8,128)(2,1)S(1)}, bf16[96,576]{1,0:T(8,128)(2,1)S(1)}, bf16[96,576]{1,0:T(8,128)(2,1)S(1)}, bf16[96,576]{1,0:T(8,128)(2,1)...) custom-call(s32[8]{0:T(128)S(1)} %stack.55.place_ref, ...), custom_call_target="tpu_custom_call" | custom-call | flops 1811939328 | bytes 5505024 | tf_op jit(solution)/shard_map/column_grads/pallas_call | solution.py:482
  425.9 9.6 %collective-permute-start.23 = (bf16[96,576]{1,0:T(8,128)(2,1)S(1)}, bf16[96,576]{1,0:T(8,128)(2,1)S(1)}, u32[]{:S(2)}, u32[]{:S(2)}) collective-permute-start(bf16[96,576]{1,0:T(8,128)(2,1)S(1)} %get-tuple-element.138), channel_id=1, source_target_pairs={{0,3},{1,2},{2,1},{3,0},{4,7},{5,6},{6,5},{7,4},{8,11},{9,10},{10,... | collective-permute-start | bytes 331784 | tf_op jit(solution)/shard_map/ppermute | solution.py:677
  454.6 19.1 %weight_grads.3 = (f32[2,768,768]{2,1,0:T(8,128)}, f32[2,768,768]{2,1,0:T(8,128)}) custom-call(s32[4]{0:T(128)S(1)} %pad_add_fusion.place_ref, bf16[8,2,64,768]{3,2,1,0:T(8,128)(2,1)} %all-to-all-done.2.x_ref.refs_0_, bf16[8,2,64,768]{3,2,1,0:T(8,128)(2,1)} %copy-done.12, ...), custom_call_target="tpu_custom_call", output_to_operand_aliasing={{0}: (13, {}), {1}: (14, {})} | custom-call | flops 19327352832 | bytes 22020096 | tf_op jit(solution)/shard_map/weight_grads/pallas_call | solution.py:653
  (186 shorter events, 101.8 us)
Async XLA Ops:
  7.2 28.5 %all-gather.5.cloned.1.call-start = ((), (), s32[]{:S(2)}) async-start(), calls=%async_computation.11 | async-start | bytes 1327104 | tf_op jit(solution)/shard_map/all_gather | solution.py:750
  10.2 96.6 %all-gather.7.cloned.1.call-start = ((), (), s32[]{:S(2)}) async-start(), calls=%async_computation.12 | async-start | bytes 1548288 | tf_op jit(solution)/shard_map/all_gather | solution.py:754
  61.0 21.5 %collective-permute-start.6 = (bf16[128,768]{1,0:T(8,128)(2,1)}, bf16[128,768]{1,0:T(8,128)(2,1)S(1)}, u32[]{:S(2)}, u32[]{:S(2)}) collective-permute-start(bf16[128,768]{1,0:T(8,128)(2,1)} %slice.89), channel_id=1, source_target_pairs={{0,16},{8,24},{16,0},{24,8},{1,17},{9,25},{17,1},{25,9},{2,18},{10... | collective-permute-start | bytes 589832 | tf_op jit(solution)/shard_map/ppermute | solution.py:677
  63.2 19.3 %collective-permute-start.7 = (bf16[128,768]{1,0:T(8,128)(2,1)}, bf16[128,768]{1,0:T(8,128)(2,1)S(1)}, u32[]{:S(2)}, u32[]{:S(2)}) collective-permute-start(bf16[128,768]{1,0:T(8,128)(2,1)} %slice.90), channel_id=1, source_target_pairs={{0,8},{8,0},{16,24},{24,16},{1,9},{9,1},{17,25},{25,17},{2,10},{10... | collective-permute-start | bytes 589832 | tf_op jit(solution)/shard_map/ppermute | solution.py:677
  78.9 17.4 %all-to-all-start = ((bf16[4,128,384]{2,1,0:T(8,128)(2,1)}), bf16[4,128,384]{2,1,0:T(8,128)(2,1)S(1)}, u32[]{:S(2)}, u32[]{:S(2)}) async-start(bf16[4,128,384]{2,1,0:T(8,128)(2,1)} %get-tuple-element.87), calls=%async_computation | async-start | bytes 786432 | tf_op jit(solution)/shard_map/all_to_all | solution.py:775
  113.7 42.3 %all-to-all-start.2 = ((bf16[8,2,64,768]{3,2,1,0:T(8,128)(2,1)}), bf16[8,2,64,768]{3,2,1,0:T(8,128)(2,1)}, u32[]{:S(2)}, u32[]{:S(2)}) async-start(bf16[8,2,64,768]{3,2,1,0:T(8,128)(2,1)} %bitcast.68), calls=%async_computation.2 | async-start | bytes 3145728 | tf_op jit(solution)/shard_map/all_to_all | solution.py:789
  118.1 59.8 %all-gather.9.cloned.1.call-start = ((), (), s32[]{:S(2)}) async-start(), calls=%async_computation.13 | async-start | bytes 4915200 | tf_op jit(solution)/shard_map/all_gather | solution.py:792
  155.9 42.2 %all-to-all-start.4 = ((bf16[8,2,64,768]{3,2,1,0:T(8,128)(2,1)}), bf16[8,2,64,768]{3,2,1,0:T(8,128)(2,1)}, u32[]{:S(2)}, u32[]{:S(2)}) async-start(bf16[8,2,64,768]{3,2,1,0:T(8,128)(2,1)} %bitcast.13), calls=%async_computation.4 | async-start | bytes 3145728 | tf_op jit(solution)/shard_map/all_to_all | solution.py:789
  198.1 46.4 %all-to-all-start.3 = ((bf16[8,2,64,768]{3,2,1,0:T(8,128)(2,1)}), bf16[8,2,64,768]{3,2,1,0:T(8,128)(2,1)}, u32[]{:S(2)}, u32[]{:S(2)}) async-start(bf16[8,2,64,768]{3,2,1,0:T(8,128)(2,1)} %get-tuple-element.94), calls=%async_computation.3 | async-start | bytes 3145728 | tf_op jit(solution)/shard_map/all_to_all | solution.py:789
  202.4 37.5 %collective-permute-start.8 = (bf16[8,2,64,768]{3,2,1,0:T(8,128)(2,1)}, bf16[8,2,64,768]{3,2,1,0:T(8,128)(2,1)S(1)}, u32[]{:S(2)}, u32[]{:S(2)}) collective-permute-start(bf16[8,2,64,768]{3,2,1,0:T(8,128)(2,1)} %all-to-all-done.2.x_ref.refs_0_), channel_id=1, source_target_pairs={{0,8},{8,0},{16,24},{24,16},{1,9},{9,1},{17,25},{25,17},{2,10},{10... | collective-permute-start | bytes 4718600 | tf_op jit(solution)/shard_map/ppermute | solution.py:677
  203.9 37.5 %collective-permute-start.9 = (bf16[8,2,64,768]{3,2,1,0:T(8,128)(2,1)}, bf16[8,2,64,768]{3,2,1,0:T(8,128)(2,1)S(1)}, u32[]{:S(2)}, u32[]{:S(2)}) collective-permute-start(bf16[8,2,64,768]{3,2,1,0:T(8,128)(2,1)} %all-to-all-done.2.x_ref.refs_0_), channel_id=1, source_target_pairs={{0,16},{8,24},{16,0},{24,8},{1,17},{9,25},{17,1},{25,9},{2,18},{10... | collective-permute-start | bytes 4718600 | tf_op jit(solution)/shard_map/ppermute | solution.py:677
  204.5 69.2 %collective-permute-start.12 = (bf16[8,2,64,768]{3,2,1,0:T(8,128)(2,1)}, bf16[8,2,64,768]{3,2,1,0:T(8,128)(2,1)}, u32[]{:S(2)}, u32[]{:S(2)}) collective-permute-start(bf16[8,2,64,768]{3,2,1,0:T(8,128)(2,1)} %all-to-all-done.4.g_ref.refs_5_), channel_id=1, source_target_pairs={{0,8},{8,0},{16,24},{24,16},{1,9},{9,1},{17,25},{25,17},{2,10},{10... | collective-permute-start | bytes 4718600 | tf_op jit(solution)/shard_map/ppermute | solution.py:677
  206.0 69.2 %collective-permute-start.13 = (bf16[8,2,64,768]{3,2,1,0:T(8,128)(2,1)}, bf16[8,2,64,768]{3,2,1,0:T(8,128)(2,1)}, u32[]{:S(2)}, u32[]{:S(2)}) collective-permute-start(bf16[8,2,64,768]{3,2,1,0:T(8,128)(2,1)} %all-to-all-done.4.g_ref.refs_5_), channel_id=1, source_target_pairs={{0,16},{8,24},{16,0},{24,8},{1,17},{9,25},{17,1},{25,9},{2,18},{10... | collective-permute-start | bytes 4718600 | tf_op jit(solution)/shard_map/ppermute | solution.py:677
  241.4 49.6 %collective-permute-start.10 = (bf16[4,2,64,768]{3,2,1,0:T(8,128)(2,1)S(1)}, bf16[4,2,64,768]{3,2,1,0:T(8,128)(2,1)S(1)}, u32[]{:S(2)}, u32[]{:S(2)}) collective-permute-start(bf16[4,2,64,768]{3,2,1,0:T(8,128)(2,1)S(1)} %slice.73), channel_id=1, source_target_pairs={{0,16},{8,24},{16,0},{24,8},{1,17},{9,25},{17,1},{25,9},{2,18},{10... | collective-permute-start | bytes 2359304 | tf_op jit(solution)/shard_map/ppermute | solution.py:677
  243.6 47.4 %collective-permute-start.11 = (bf16[4,2,64,768]{3,2,1,0:T(8,128)(2,1)}, bf16[4,2,64,768]{3,2,1,0:T(8,128)(2,1)S(1)}, u32[]{:S(2)}, u32[]{:S(2)}) collective-permute-start(bf16[4,2,64,768]{3,2,1,0:T(8,128)(2,1)} %slice.74), channel_id=1, source_target_pairs={{0,8},{8,0},{16,24},{24,16},{1,9},{9,1},{17,25},{25,17},{2,10},{10... | collective-permute-start | bytes 2359304 | tf_op jit(solution)/shard_map/ppermute | solution.py:677
  244.5 90.9 %all-to-all-start.5 = ((bf16[8,2,64,768]{3,2,1,0:T(8,128)(2,1)}), bf16[8,2,64,768]{3,2,1,0:T(8,128)(2,1)}, u32[]{:S(2)}, u32[]{:S(2)}) async-start(bf16[8,2,64,768]{3,2,1,0:T(8,128)(2,1)} %expert_backward.1), calls=%async_computation.5 | async-start | bytes 3145728 | tf_op jit(solution)/shard_map/all_to_all | solution.py:789
  294.1 18.9 %collective-permute-start.14 = (bf16[4,2,64,768]{3,2,1,0:T(8,128)(2,1)}, bf16[4,2,64,768]{3,2,1,0:T(8,128)(2,1)}, u32[]{:S(2)}, u32[]{:S(2)}) collective-permute-start(bf16[4,2,64,768]{3,2,1,0:T(8,128)(2,1)} %slice.75), channel_id=1, source_target_pairs={{0,16},{8,24},{16,0},{24,8},{1,17},{9,25},{17,1},{25,9},{2,18},{10... | collective-permute-start | bytes 2359304 | tf_op jit(solution)/shard_map/ppermute | solution.py:677
  296.8 18.8 %collective-permute-start.15 = (bf16[4,2,64,768]{3,2,1,0:T(8,128)(2,1)}, bf16[4,2,64,768]{3,2,1,0:T(8,128)(2,1)}, u32[]{:S(2)}, u32[]{:S(2)}) collective-permute-start(bf16[4,2,64,768]{3,2,1,0:T(8,128)(2,1)} %slice.76), channel_id=1, source_target_pairs={{0,8},{8,0},{16,24},{24,16},{1,9},{9,1},{17,25},{25,17},{2,10},{10... | collective-permute-start | bytes 2359304 | tf_op jit(solution)/shard_map/ppermute | solution.py:677
  349.8 17.8 %all-to-all-start.6 = ((bf16[4,128,384]{2,1,0:T(8,128)(2,1)}), bf16[4,128,384]{2,1,0:T(8,128)(2,1)S(1)}, u32[]{:S(2)}, u32[]{:S(2)}) async-start(bf16[4,128,384]{2,1,0:T(8,128)(2,1)} %get-tuple-element.116), calls=%async_computation.6 | async-start | bytes 786432 | tf_op jit(solution)/shard_map/all_to_all | solution.py:831
  367.6 21.0 %all-to-all-start.9 = ((bf16[4,128,1152]{2,1,0:T(8,128)(2,1)}), bf16[4,128,1152]{2,1,0:T(8,128)(2,1)}, u32[]{:S(2)}, u32[]{:S(2)}) async-start(bf16[4,128,1152]{2,1,0:T(8,128)(2,1)} %get-tuple-element.123.refs_2_), calls=%async_computation.9 | async-start | bytes 2359296 | tf_op jit(solution)/shard_map/all_to_all | solution.py:849
  371.9 68.7 %reduce-scatter.4.cloned.1.call-start = ((), (), s32[]{:S(2)}) async-start(), calls=%async_computation.14 | async-start | bytes 1548288
  388.6 17.8 %all-to-all-start.7 = ((bf16[4,128,1152]{2,1,0:T(8,128)(2,1)}), bf16[4,128,1152]{2,1,0:T(8,128)(2,1)}, u32[]{:S(2)}, u32[]{:S(2)}) async-start(bf16[4,128,1152]{2,1,0:T(8,128)(2,1)} %get-tuple-element.117.refs_3_), calls=%async_computation.7 | async-start | bytes 2359296 | tf_op jit(solution)/shard_map/all_to_all | solution.py:849
  418.7 16.7 %collective-permute-start.26 = (bf16[96,576]{1,0:T(8,128)(2,1)S(1)}, bf16[96,576]{1,0:T(8,128)(2,1)S(1)}, u32[]{:S(2)}, u32[]{:S(2)}) collective-permute-start(bf16[96,576]{1,0:T(8,128)(2,1)S(1)} %get-tuple-element.141), channel_id=1, source_target_pairs={{0,6},{1,7},{2,4},{3,5},{4,2},{5,3},{6,0},{7,1},{8,14},{9,15},{10,... | collective-permute-start | bytes 331784 | tf_op jit(solution)/shard_map/ppermute | solution.py:677
  421.5 16.9 %collective-permute-start.17 = (f32[15,128]{1,0:T(8,128)S(1)}, f32[15,128]{1,0:T(8,128)S(1)}, u32[]{:S(2)}, u32[]{:S(2)}) collective-permute-start(f32[15,128]{1,0:T(8,128)S(1)} %fusion.9), channel_id=1, source_target_pairs={{0,16},{8,24},{16,0},{24,8},{1,17},{9,25},{17,1},{25,9},{2,18},{10... | collective-permute-start | bytes 23048 | tf_op jit(solution)/shard_map/ppermute | solution.py:677
  422.2 18.4 %collective-permute-start.25 = (bf16[96,576]{1,0:T(8,128)(2,1)S(1)}, bf16[96,576]{1,0:T(8,128)(2,1)S(1)}, u32[]{:S(2)}, u32[]{:S(2)}) collective-permute-start(bf16[96,576]{1,0:T(8,128)(2,1)S(1)} %get-tuple-element.140), channel_id=1, source_target_pairs={{0,5},{1,4},{2,7},{3,6},{4,1},{5,0},{6,3},{7,2},{8,13},{9,12},{10,... | collective-permute-start | bytes 331784 | tf_op jit(solution)/shard_map/ppermute | solution.py:677
  422.3 20.9 %collective-permute-start.24 = (bf16[96,576]{1,0:T(8,128)(2,1)S(1)}, bf16[96,576]{1,0:T(8,128)(2,1)S(1)}, u32[]{:S(2)}, u32[]{:S(2)}) collective-permute-start(bf16[96,576]{1,0:T(8,128)(2,1)S(1)} %get-tuple-element.139), channel_id=1, source_target_pairs={{0,4},{1,5},{2,6},{3,7},{4,0},{5,1},{6,2},{7,3},{8,12},{9,13},{10,... | collective-permute-start | bytes 331784 | tf_op jit(solution)/shard_map/ppermute | solution.py:677
  425.9 18.2 %collective-permute-start.23 = (bf16[96,576]{1,0:T(8,128)(2,1)S(1)}, bf16[96,576]{1,0:T(8,128)(2,1)S(1)}, u32[]{:S(2)}, u32[]{:S(2)}) collective-permute-start(bf16[96,576]{1,0:T(8,128)(2,1)S(1)} %get-tuple-element.138), channel_id=1, source_target_pairs={{0,3},{1,2},{2,1},{3,0},{4,7},{5,6},{6,5},{7,4},{8,11},{9,10},{10,... | collective-permute-start | bytes 331784 | tf_op jit(solution)/shard_map/ppermute | solution.py:677
  447.5 26.2 %collective-permute-start.28 = (bf16[96,576]{1,0:T(8,128)(2,1)S(1)}, bf16[96,576]{1,0:T(8,128)(2,1)S(1)}, u32[]{:S(2)}, u32[]{:S(2)}) collective-permute-start(bf16[96,576]{1,0:T(8,128)(2,1)S(1)} %add_convert_fusion.1.refs_0_), channel_id=1, source_target_pairs={{0,8},{8,0},{16,24},{24,16},{1,9},{9,1},{17,25},{25,17},{2,10},{10... | collective-permute-start | bytes 331784 | tf_op jit(solution)/shard_map/ppermute | solution.py:677
  448.1 25.6 %collective-permute-start.29 = (bf16[96,576]{1,0:T(8,128)(2,1)S(1)}, bf16[96,576]{1,0:T(8,128)(2,1)S(1)}, u32[]{:S(2)}, u32[]{:S(2)}) collective-permute-start(bf16[96,576]{1,0:T(8,128)(2,1)S(1)} %add_convert_fusion.1.refs_0_), channel_id=1, source_target_pairs={{0,16},{8,24},{16,0},{24,8},{1,17},{9,25},{17,1},{25,9},{2,18},{10... | collective-permute-start | bytes 331784 | tf_op jit(solution)/shard_map/ppermute | solution.py:677
  449.6 24.1 %collective-permute-start.30 = (bf16[96,576]{1,0:T(8,128)(2,1)S(1)}, bf16[96,576]{1,0:T(8,128)(2,1)S(1)}, u32[]{:S(2)}, u32[]{:S(2)}) collective-permute-start(bf16[96,576]{1,0:T(8,128)(2,1)S(1)} %add_convert_fusion.1.refs_0_), channel_id=1, source_target_pairs={{0,24},{8,16},{16,8},{24,0},{1,25},{9,17},{17,9},{25,1},{2,26},{10... | collective-permute-start | bytes 331784 | tf_op jit(solution)/shard_map/ppermute | solution.py:677
  451.0 24.4 %collective-permute-start.20 = (f32[15,128]{1,0:T(8,128)S(1)}, f32[15,128]{1,0:T(8,128)S(1)}, u32[]{:S(2)}, u32[]{:S(2)}) collective-permute-start(f32[15,128]{1,0:T(8,128)S(1)} %add.92), channel_id=1, source_target_pairs={{0,4},{1,5},{2,6},{3,7},{4,0},{5,1},{6,2},{7,3},{8,12},{9,13},{10,... | collective-permute-start | bytes 23048 | tf_op jit(solution)/shard_map/ppermute | solution.py:677
  453.9 22.9 %collective-permute-start.32 = (f32[96,784]{0,1:T(8,128)S(1)}, f32[96,784]{0,1:T(8,128)S(1)}, u32[]{:S(2)}, u32[]{:S(2)}) collective-permute-start(f32[96,784]{0,1:T(8,128)S(1)} %convert_add_fusion), channel_id=1, source_target_pairs={{0,16},{8,24},{16,0},{24,8},{1,17},{9,25},{17,1},{25,9},{2,18},{10... | collective-permute-start | bytes 903176 | tf_op jit(solution)/shard_map/ppermute | solution.py:677
  (36 other events, 404.7 us)
Sparse Core Ops, SparseCore 0:
  10.3 25.3 all-gather.4
  37.9 23.7 all-gather.6
  120.8 50.9 all-gather.8
  375.1 34.9 reduce-scatter.3
